TPU v7x, 512 devices: a whole 4x8x8 slice. The times are simulated.
512 devices in a mesh: ep: 32 (over x, y), node: 2 (over core), dp: 8 (over z).
Axes of the slice: x: 4, y: 8, z: 8, core: 2. Of those that a mesh axis runs over, the one named last changes fastest.
Arguments:
- grad_out: bfloat16 [8192, 7168], P(('ep', 'node'), 'dp'), may hold values from -6 to 6
- tokens: bfloat16 [8192, 7168], P(('ep', 'node'), 'dp'), may hold values from -0.59765625 to 0.59765625
- scores: float32 [8192, 64], P(('ep', 'node')), may hold values from 0.02 to 0.98
- expert_ids: int32 [8192, 8], P(('ep', 'node')), may hold values from 0 to 63, all different within a row; in each aligned block of 128 rows (0 to 127, 128 to 255, ...) at most 20 rows name the same one
- hidden_act: bfloat16 [64, 1280, 1024], P(('ep', 'node')), may hold values from -0.29882812 to 0.29882812
- down_weight: bfloat16 [64, 1024, 7168], P(('ep', 'node'), None, 'dp'), may hold values from -0.1875 to 0.1875
Outputs:
- weight_grad: bfloat16 [64, 1024, 7168], P(('ep', 'node'), None, 'dp')
- hidden_grad: bfloat16 [64, 1280, 1024], P(('ep', 'node'), 'dp')
- gate_grad: float32 [64, 7168], P(None, 'dp')
Inputs may be any that keep to these rules, and one draw needn't show every extreme that they name: `expert_ids`: among the routes of the 128 tokens of one source device, no expert is named more than 20 times, a bound that some block reaches.
All inputs are finite; a program needn't handle non-finite values.
Results may differ from a plain program's by a relative error of at most 0.017.
Values may be sent and summed in bfloat16 or wider, within the bound.
No kernel may reach another device: no remote copies, remote signals or barrier semaphores. Data moves between devices by JAX's collectives and lax.ppermute only.
A program may use at most 64 MiB of HBM per device.

v0:
```python
import jax
import jax.numpy as jnp
from jax import lax
from jax.sharding import PartitionSpec as P

route_scale = 2.5


def body(grad_out, tokens, scores, expert_ids, hidden_act, down_weight):
    sources = lax.axis_size(("ep", "node"))
    tok_rows = expert_ids.shape[0]
    choose_count = expert_ids.shape[1]
    expert_count = scores.shape[1]
    route_count = tok_rows * choose_count
    slot_count = hidden_act.shape[1]
    slot_most = slot_count // sources
    feature_cols = grad_out.shape[1]
    chosen = jnp.take_along_axis(scores, expert_ids, axis=1)
    total = jnp.sum(chosen, axis=1, keepdims=True)
    weights = (route_scale * chosen / total).astype(jnp.bfloat16)
    flat_ids = expert_ids.reshape(route_count)
    onehot = (flat_ids[:, None] == jnp.arange(expert_count, dtype=jnp.int32)[None, :]).astype(
        jnp.int32
    )
    before = jnp.cumsum(onehot, axis=0) - onehot
    rank = jnp.sum(before * onehot, axis=1)
    target = flat_ids * slot_most + rank
    placing = (
        target[None, :] == jnp.arange(expert_count * slot_most, dtype=jnp.int32)[:, None]
    ).astype(jnp.float32)
    place_tokens = jnp.sum(
        placing.reshape(expert_count * slot_most, tok_rows, choose_count), axis=2
    ).astype(jnp.bfloat16)
    send_rows = jnp.dot(place_tokens, grad_out, preferred_element_type=jnp.float32).astype(
        jnp.bfloat16
    )
    send_rows = send_rows.reshape(expert_count, slot_most, feature_cols)
    send_gains = jnp.dot(
        placing, weights.reshape(route_count).astype(jnp.float32), precision=lax.Precision.HIGHEST
    )
    send_gains = send_gains.astype(jnp.bfloat16).reshape(expert_count, slot_most)
    recv_rows, recv_gains = (
        lax.all_to_all(send_rows, ("ep", "node"), split_axis=0, concat_axis=0, tiled=True),
        lax.all_to_all(send_gains, ("ep", "node"), split_axis=0, concat_axis=0, tiled=True),
    )
    rows = recv_rows.reshape(slot_count, feature_cols)
    gains = recv_gains.reshape(slot_count)
    scaled = (gains.astype(jnp.float32)[:, None] * rows.astype(jnp.float32)).astype(jnp.bfloat16)
    hidden = hidden_act[0]
    down = down_weight[0]
    weight_grad = lax.dot_general(
        hidden, scaled, (((0,), (0,)), ((), ())), preferred_element_type=jnp.float32
    )
    weight_grad = weight_grad.astype(jnp.bfloat16)[None]
    hidden_grad = lax.psum_scatter(
        lax.dot_general(
            scaled, down, (((1,), (1,)), ((), ())), preferred_element_type=jnp.float32
        ).astype(jnp.bfloat16),
        "dp",
        scatter_dimension=0,
        tiled=True,
    )[None]
    outputs = jnp.dot(hidden, down, preferred_element_type=jnp.float32)
    partial_value = jnp.sum(outputs * rows.astype(jnp.float32), axis=1).reshape(sources, slot_most)
    summed = lax.psum(partial_value, "dp")
    returned = lax.all_to_all(summed, ("ep", "node"), split_axis=0, concat_axis=0, tiled=True)
    route_grad = jnp.take(returned.reshape(expert_count * slot_most), target).reshape(
        tok_rows, choose_count
    )
    mixed = jnp.sum(route_grad * chosen, axis=1, keepdims=True) / total
    score_grad = route_scale / total * (route_grad - mixed)
    logit_sel = score_grad * chosen * (1.0 - chosen)
    onehot_k = (
        expert_ids[:, :, None] == jnp.arange(expert_count, dtype=jnp.int32)[None, None, :]
    ).astype(jnp.float32)
    logit_grad = jnp.sum(logit_sel[:, :, None] * onehot_k, axis=1).astype(jnp.bfloat16)
    gate_part = lax.dot_general(
        logit_grad, tokens, (((0,), (0,)), ((), ())), preferred_element_type=jnp.float32
    )
    gate_grad = lax.psum(gate_part, ("ep", "node"))
    return (weight_grad, hidden_grad, gate_grad)


def solution(mesh):
    return jax.shard_map(
        body,
        mesh=mesh,
        in_specs=(
            P(("ep", "node"), "dp"),
            P(("ep", "node"), "dp"),
            P(("ep", "node"), None),
            P(("ep", "node"), None),
            P(("ep", "node"), None, None),
            P(("ep", "node"), None, "dp"),
        ),
        out_specs=(P(("ep", "node"), None, "dp"), P(("ep", "node"), "dp", None), P(None, "dp")),
        check_vma=False,
    )
```

profile of v0, /device:TPU:1, one launch (start us, length us, event | category | flops | bytes accessed | tf_op | source)
XLA Modules:
  0.0 400.6 jit_solution(3388126750876687958)
XLA Ops:
  9.2 18.0 %reduce-window.6 = s32[64,8,128]{2,1,0:T(8,128)S(1)} reduce-window(s32[64,8,128]{2,1,0:T(8,128)S(1)} %fusion.14, s32[]{:T(128)} %constant.24.clone.1), window={size=1x1x128 pad=0_0x0_0x127_0}, to_apply=%region_0.0 | reduce-window | flops 8323072 | bytes 524292 | tf_op jit(solution)/shard_map/reduce-window
  28.0 6.7 %convert_reduce_fusion = bf16[1280,128]{1,0:T(8,128)(2,1)S(1)} fusion(s32[128,8]{0,1:T(8,128)S(1)} %get-tuple-element.24), kind=kLoop, calls=%fused_computation.3 | loop fusion | flops 3768320 | bytes 331776 | tf_op jit(solution)/shard_map/reduce_sum | solution.py:31
  34.7 2.2 convolution_convert_fusion.1
  36.8 4.7 %reshape.158 = bf16[64,20,896]{2,1,0:T(8,128)(2,1)} reshape(bf16[1280,896]{1,0:T(8,128)(2,1)} %convolution_convert_fusion.1) | data formatting | bytes 4587520 | tf_op jit(solution)/shard_map/reshape | solution.py:37
  41.5 11.8 %all-to-all-start.1 = ((bf16[64,20,896]{2,1,0:T(8,128)(2,1)}), bf16[64,20,896]{2,1,0:T(8,128)(2,1)}, u32[]{:S(2)}, u32[]{:S(2)}) async-start(bf16[64,20,896]{2,1,0:T(8,128)(2,1)} %reshape.158), calls=%async_computation.1 | async-start | bytes 5505024 | tf_op jit(solution)/shard_map/all_to_all | solution.py:43
  53.6 64.8 %all-to-all-done.1 = bf16[64,20,896]{2,1,0:T(8,128)(2,1)} async-done(((bf16[64,20,896]{2,1,0:T(8,128)(2,1)}), bf16[64,20,896]{2,1,0:T(8,128)(2,1)}, u32[]{:S(2)}, u32[]{:S(2)}) %all-to-all-start.1) | async-done | bytes 2293792 | tf_op jit(solution)/shard_map/all_to_all | solution.py:43
  118.4 5.0 %reshape.163 = f32[1280,896]{1,0:T(8,128)} reshape(bf16[64,20,896]{2,1,0:T(8,128)(2,1)} %all-to-all-done.1) | data formatting | bytes 6881280 | tf_op jit(solution)/shard_map/convert_element_type | solution.py:48
  123.4 5.8 %copy.67 = f32[1280,896]{0,1:T(8,128)} copy(f32[1280,896]{1,0:T(8,128)} %reshape.163) | data formatting | bytes 9175040 | tf_op jit(solution)/shard_map/convert_element_type | solution.py:48
  129.2 5.5 %multiply_reduce_fusion = f32[1280]{0:T(1024)S(1)} fusion(f32[1280,896]{0,1:T(8,128)} %copy.67, bf16[1,1280,1024]{2,1,0:T(8,128)(2,1)S(1)} %copy-done, bf16[1,1024,896]{2,1,0:T(8,128)(2,1)} %param.11), kind=kOutput, calls=%fused_computation.7 | convolution fusion | flops 2351102720 | bytes 9049088 | tf_op jit(solution)/shard_map/dot_general | solution.py:63
  134.7 29.3 %psum.14 = f32[64,1,20]{2,0,1:T(8,128)} all-reduce(f32[64,1,20]{2,0,1:T(8,128)S(1)} %all_to_all.18), channel_id=1, replica_groups=mesh['ep'=32,'node'=2,'dp'=8] {'dp'}, use_global_device_ids=true, to_apply=%region_7.8 | all-reduce | flops 1280 | bytes 10240 | tf_op jit(solution)/shard_map/psum | solution.py:65
  164.0 12.9 %all-to-all-start.2 = ((f32[64,1,20]{2,1,0:T(1,128)}), f32[64,1,20]{2,1,0:T(1,128)S(1)}, u32[]{:S(2)}, u32[]{:S(2)}) async-start(f32[64,1,20]{2,1,0:T(1,128)} %bitcast.9), calls=%async_computation.3 | async-start | bytes 65536 | tf_op jit(solution)/shard_map/all_to_all | solution.py:66
  177.2 7.0 %gather_fusion.1 = f32[1024]{0:T(1024)S(1)} fusion(f32[128,64]{0,1:T(8,128)S(1)} %copy-done.1, s32[1024]{0:T(1024)S(1)} %reshape.172), kind=kCustom, calls=%fused_computation.1 | custom fusion | bytes 16384 | tf_op jit(solution)/shard_map/jit(take_along_axis)/gather | solution.py:18
  184.3 1.8 all-to-all-done.2
  187.5 6.2 %gather_fusion = f32[1024]{0:T(1024)S(1)} fusion(f32[1280]{0:T(1024)S(1)} %reshape.160, s32[1024]{0:T(1024)S(1)} %broadcast_clamp_fusion), kind=kCustom, calls=%fused_computation | custom fusion | bytes 12288 | tf_op jit(solution)/shard_map/jit(_take)/gather | solution.py:67
  194.1 1.0 fusion.9
  195.8 8.5 %all-to-all-start = ((bf16[64,1,20]{2,1,0:T(2,128)(2,1)}), bf16[64,1,20]{2,1,0:T(2,128)(2,1)S(1)}, u32[]{:S(2)}, u32[]{:S(2)}) async-start(bf16[64,1,20]{2,1,0:T(2,128)(2,1)} %all_to_all.20), calls=%async_computation | async-start | bytes 65536 | tf_op jit(solution)/shard_map/all_to_all | solution.py:44
  205.4 8.2 %all-to-all-done = bf16[64,1,20]{2,1,0:T(2,128)(2,1)S(1)} async-done(((bf16[64,1,20]{2,1,0:T(2,128)(2,1)}), bf16[64,1,20]{2,1,0:T(2,128)(2,1)S(1)}, u32[]{:S(2)}, u32[]{:S(2)}) %all-to-all-start) | async-done | bytes 2592 | tf_op jit(solution)/shard_map/all_to_all | solution.py:44
  213.6 3.9 multiply_convert_fusion
  217.5 4.7 %convert_element_type.81 = bf16[1280,896]{1,0:T(8,128)(2,1)} reshape(bf16[64,20,896]{2,1,0:T(8,128)(2,1)} %multiply_convert_fusion) | data formatting | bytes 4587520 | tf_op jit(solution)/shard_map/convert_element_type | solution.py:48
  222.2 6.6 %convolution_convert_fusion = bf16[1280,1024]{1,0:T(8,128)(2,1)} fusion(bf16[1280,896]{1,0:T(8,128)(2,1)} %convert_element_type.81, bf16[1,1024,896]{2,1,0:T(8,128)(2,1)} %param.11), kind=kOutput, calls=%fused_computation.8 | convolution fusion | flops 2350120960 | bytes 6750208 | tf_op jit(solution)/shard_map/dot_general | solution.py:56
  228.9 5.5 %convert_bitcast_fusion = bf16[1,1024,896]{1,2,0:T(8,128)(2,1)} fusion(bf16[1280,896]{1,0:T(8,128)(2,1)} %convert_element_type.81, bf16[1,1280,1024]{2,1,0:T(8,128)(2,1)S(1)} %copy-done), kind=kOutput, calls=%fused_computation.16 | convolution fusion | flops 2349727744 | bytes 6750208 | tf_op jit(solution)/shard_map/dot_general | solution.py:51
  234.4 3.8 copy.71
  238.2 153.3 %all-reduce.2.cloned.1.call-done = f32[64,896]{1,0:T(8,128)} async-done(((f32[64,896]{1,0:T(8,128)}), f32[64,896]{1,0:T(8,128)}) %all-reduce.2.cloned.1.call-update) | async-done | bytes 229392 | tf_op jit(solution)/shard_map/psum | solution.py:80
  391.6 1.6 copy.75
  (54 shorter events, 6.1 us)
Async XLA Ops:
  8.0 121.2 %copy-start = (bf16[1,1280,1024]{2,1,0:T(8,128)(2,1)S(1)}, bf16[1,1280,1024]{2,1,0:T(8,128)(2,1)}, u32[]{:S(2)}) copy-start(bf16[1,1280,1024]{2,1,0:T(8,128)(2,1)} %param.10) | copy-start | bytes 7864324
  8.0 19.9 %copy-start.4 = (s32[128,8]{0,1:T(8,128)S(1)}, s32[128,8]{0,1:T(8,128)}, u32[]{:S(2)}) copy-start(s32[128,8]{0,1:T(8,128)} %param.9) | copy-start | bytes 12292
  8.0 26.7 %copy-start.3 = (bf16[128,896]{1,0:T(8,128)(2,1)S(1)}, bf16[128,896]{1,0:T(8,128)(2,1)}, u32[]{:S(2)}) copy-start(bf16[128,896]{1,0:T(8,128)(2,1)} %param.6) | copy-start | bytes 688132
  41.5 76.9 %all-to-all-start.1 = ((bf16[64,20,896]{2,1,0:T(8,128)(2,1)}), bf16[64,20,896]{2,1,0:T(8,128)(2,1)}, u32[]{:S(2)}, u32[]{:S(2)}) async-start(bf16[64,20,896]{2,1,0:T(8,128)(2,1)} %reshape.158), calls=%async_computation.1 | async-start | bytes 5505024 | tf_op jit(solution)/shard_map/all_to_all | solution.py:43
  134.6 42.5 %copy-start.1 = (f32[128,64]{0,1:T(8,128)S(1)}, f32[128,64]{0,1:T(8,128)}, u32[]{:S(2)}) copy-start(f32[128,64]{0,1:T(8,128)} %param.8) | copy-start | bytes 98308
  164.0 22.1 %all-to-all-start.2 = ((f32[64,1,20]{2,1,0:T(1,128)}), f32[64,1,20]{2,1,0:T(1,128)S(1)}, u32[]{:S(2)}, u32[]{:S(2)}) async-start(f32[64,1,20]{2,1,0:T(1,128)} %bitcast.9), calls=%async_computation.3 | async-start | bytes 65536 | tf_op jit(solution)/shard_map/all_to_all | solution.py:66
  187.5 17.0 %copy-start.2 = (bf16[128,896]{1,0:T(8,128)(2,1)S(1)}, bf16[128,896]{1,0:T(8,128)(2,1)}, u32[]{:S(2)}) copy-start(bf16[128,896]{1,0:T(8,128)(2,1)} %param.7) | copy-start | bytes 688132
  195.8 17.7 %all-to-all-start = ((bf16[64,1,20]{2,1,0:T(2,128)(2,1)}), bf16[64,1,20]{2,1,0:T(2,128)(2,1)S(1)}, u32[]{:S(2)}, u32[]{:S(2)}) async-start(bf16[64,1,20]{2,1,0:T(2,128)(2,1)} %all_to_all.20), calls=%async_computation | async-start | bytes 65536 | tf_op jit(solution)/shard_map/all_to_all | solution.py:44
  204.4 187.2 %all-reduce.2.cloned.1.call-start = ((), (), s32[]{:S(2)}) async-start(), calls=%async_computation.5 | async-start | bytes 458752 | tf_op jit(solution)/shard_map/psum | solution.py:80
  205.3 186.2 %reduce-scatter.2.cloned.1.call-start = ((), (), s32[]{:S(2)}) async-start(), calls=%async_computation.4 | async-start | bytes 2949120 | tf_op jit(solution)/shard_map/reduce_scatter | solution.py:55
Sparse Core Ops, SparseCore 0:
  209.3 182.2 all-reduce.1
Sparse Core Ops, SparseCore 1:
  228.9 33.6 reduce-scatter.1
where the time goes:
time: 402 us; the launch traced here: 401 us
  waiting for transfers between devices  228 us (57%)
  local copies, waits for them, and re-layouts  42.8 us (11%)
  starting transfers between devices  33.3 us (8%)
  other arithmetic  29.7 us (7%)
  blocking collectives  29.3 us (7%)
  matrix products  21.6 us (5%)
  between operations  15.8 us (4%)
    psum x1, waiting for transfers between devices, body(): gate_grad = lax.psum(gate_part, ('ep', 'node'))  153 us
    all_to_all x1, waiting for transfers between devices, body(): lax.all_to_all(send_rows, ('ep', 'node'), split_axis=0, concat_axis=0, ti...  64.8 us
    psum x1, blocking collectives, body(): summed = lax.psum(partial_value, 'dp')  29.3 us
    another operation x3, other arithmetic  18.2 us
    all_to_all x1, starting transfers between devices, body(): lax.all_to_all(summed, ('ep', 'node'), split_axis=0, concat_axis=0, tiled...  12.9 us
    all_to_all x1, starting transfers between devices, body(): lax.all_to_all(send_rows, ('ep', 'node'), split_axis=0, concat_axis=0, ti...  11.8 us
    convert_element_type x2, local copies, waits for them, and re-layouts, body(): rows.astype(jnp.float32)  10.7 us
    all_to_all x1, starting transfers between devices, body(): lax.all_to_all(send_gains, ('ep', 'node'), split_axis=0, concat_axis=0, t...  8.52 us
  transfers between devices with their start and end apart: 5, of which 4 were waited for; matrix products, arithmetic and copies ran while one was open for 8% of the time, Pallas kernels for 0%

commit v1 on v0

v1 whole, which is shorter than its diff:
```python
import functools

import jax
import jax.numpy as jnp
from jax import lax
from jax.experimental import pallas as pl
from jax.experimental.pallas import tpu as pltpu
from jax.sharding import PartitionSpec as P

route_scale = 2.5
TOKS = 128
TOP = 8
EXP = 64
MOST = 20
MAIN = 16
EXTRA = MOST - MAIN
FEAT = 896
LANES = 128
COLS = FEAT // LANES
PIECE = COLS * MAIN + 32
HID = 1024
SLOTS = EXP * MOST
GROUPS = 8
BLOCK = SLOTS // GROUPS
VMEM = 48 * 1024 * 1024
bf16, f32 = jnp.bfloat16, jnp.float32


def routing(ids, scores):
    expert = lax.broadcasted_iota(jnp.int32, (EXP, TOKS), 0)
    hit = ids[0:1, :] == expert
    for k in range(1, TOP):
        hit = hit | (ids[k : k + 1, :] == expert)
    earlier = (
        lax.broadcasted_iota(jnp.int32, (TOKS, TOKS), 0) < lax.broadcasted_iota(jnp.int32, (TOKS, TOKS), 1)
    )
    ones = jnp.where(hit, 1.0, 0.0)
    rank = jnp.dot(
        ones.astype(bf16), jnp.where(earlier, 1.0, 0.0).astype(bf16), preferred_element_type=f32
    )
    rank = jnp.where(hit, rank, -1.0)
    chosen = jnp.where(hit, scores, 0.0)
    total = jnp.sum(chosen, axis=0, keepdims=True)
    weights = (route_scale * chosen / total).astype(bf16).astype(f32)
    return hit, chosen, total, weights, rank


def pack_kernel(ids_ref, scores_ref, grad_ref, send_ref, rank_ref, weight_ref):
    _, _, _, weights, rank = routing(ids_ref[...], scores_ref[...])
    rank_ref[...] = rank
    weight_ref[...] = weights
    grad = grad_ref[...]
    row = lax.broadcasted_iota(jnp.int32, (8, MAIN, TOKS), 1)
    main_rank = row.astype(f32)
    extra_rank = (MAIN + row % EXTRA).astype(f32)
    quarter = lax.broadcasted_iota(jnp.int32, (8 * MAIN, LANES), 0) % MAIN // EXTRA

    def step(i, carry):
        at = pl.ds(pl.multiple_of(i * 8, 8), 8)
        ranks = rank_ref[at, :][:, None, :]
        gains = weight_ref[at, :][:, None, :]
        place = jnp.where(ranks == main_rank, gains, 0.0).reshape(8 * MAIN, TOKS).astype(bf16)
        rows = jnp.dot(place, grad, preferred_element_type=f32)
        for j in range(COLS):
            send_ref[at, MAIN * j : MAIN * (j + 1), :] = (
                rows[:, LANES * j : LANES * (j + 1)].astype(bf16).reshape(8, MAIN, LANES)
            )
        place = jnp.where(ranks == extra_rank, gains, 0.0).reshape(8 * MAIN, TOKS).astype(bf16)
        rows = jnp.dot(place, grad, preferred_element_type=f32)
        for part in range(2):
            mixed = jnp.zeros((8 * MAIN, LANES), f32)
            for q in range(4):
                j = part * 4 + q
                if j < COLS:
                    mixed = jnp.where(quarter == q, rows[:, LANES * j : LANES * (j + 1)], mixed)
            start = COLS * MAIN + part * MAIN
            send_ref[at, start : start + MAIN, :] = mixed.astype(bf16).reshape(8, MAIN, LANES)
        return carry

    lax.fori_loop(0, EXP // 8, step, 0)


def pack(ids, scores, grad):
    return pl.pallas_call(
        pack_kernel,
        out_shape=jax.ShapeDtypeStruct((EXP, PIECE, LANES), bf16),
        scratch_shapes=[pltpu.VMEM((EXP, TOKS), f32), pltpu.VMEM((EXP, TOKS), f32)],
        compiler_params=pltpu.CompilerParams(vmem_limit_bytes=VMEM),
        cost_estimate=pl.CostEstimate(flops=500_000_000, bytes_accessed=2_700_000, transcendentals=0),
    )(ids, scores, grad)


def order_kernel(x_ref, main_ref, extra_ref):
    i = lax.broadcasted_iota(jnp.int32, (BLOCK, BLOCK), 0)
    j = lax.broadcasted_iota(jnp.int32, (BLOCK, BLOCK), 1)
    e = i - 8 * MAIN
    origin = jnp.where(i < 8 * MAIN, i // MAIN * MOST + i % MAIN, e // EXTRA * MOST + MAIN + e % EXTRA)
    move = jnp.where(origin == j, 1.0, 0.0).astype(bf16)
    y = jnp.dot(move, x_ref[...], preferred_element_type=f32).astype(bf16)
    main_ref[...] = y[: 8 * MAIN]
    extra_ref[...] = y[8 * MAIN :]


def order(hidden):
    return pl.pallas_call(
        order_kernel,
        grid=(GROUPS,),
        in_specs=[pl.BlockSpec((BLOCK, HID), lambda i: (i, 0))],
        out_specs=[
            pl.BlockSpec((8 * MAIN, HID), lambda i: (i, 0)),
            pl.BlockSpec((8 * EXTRA, HID), lambda i: (i, 0)),
        ],
        out_shape=[
            jax.ShapeDtypeStruct((EXP * MAIN, HID), bf16),
            jax.ShapeDtypeStruct((EXP * EXTRA, HID), bf16),
        ],
        cost_estimate=pl.CostEstimate(flops=500_000_000, bytes_accessed=5_300_000, transcendentals=0),
    )(hidden)


def restore_kernel(x_ref, y_ref):
    j = lax.broadcasted_iota(jnp.int32, (BLOCK, BLOCK), 0)
    i = lax.broadcasted_iota(jnp.int32, (BLOCK, BLOCK), 1)
    e = i - 8 * MAIN
    origin = jnp.where(i < 8 * MAIN, i // MAIN * MOST + i % MAIN, e // EXTRA * MOST + MAIN + e % EXTRA)
    move = jnp.where(origin == j, 1.0, 0.0).astype(bf16)
    y_ref[...] = jnp.dot(move, x_ref[...], preferred_element_type=f32).astype(bf16)


def restore(x):
    return pl.pallas_call(
        restore_kernel,
        out_shape=jax.ShapeDtypeStruct((BLOCK, HID), bf16),
        cost_estimate=pl.CostEstimate(flops=60_000_000, bytes_accessed=660_000, transcendentals=0),
    )(x)


FBLOCK = 256


def expert_kernel(recv_ref, main_ref, extra_ref, down_ref, part_ref, slot_ref, rows_ref, acc_ref):
    step = pl.program_id(0)

    @pl.when(step == 0)
    def _():
        i = lax.broadcasted_iota(jnp.int32, (LANES, LANES), 0)
        j = lax.broadcasted_iota(jnp.int32, (LANES, LANES), 1)
        q, source, r = i // 32, i % 32 // EXTRA, i % EXTRA
        move = jnp.where(source * MAIN + q * EXTRA + r == j, 1.0, 0.0).astype(bf16)
        for g in range(GROUPS):
            at = slice(8 * g, 8 * g + 8)
            for j in range(COLS):
                rows_ref[LANES * g : LANES * (g + 1), LANES * j : LANES * (j + 1)] = recv_ref[
                    at, MAIN * j : MAIN * (j + 1), :
                ].reshape(LANES, LANES)
            for part in range(2):
                start = COLS * MAIN + part * MAIN
                x = recv_ref[at, start : start + MAIN, :].reshape(LANES, LANES)
                y = jnp.dot(move, x, preferred_element_type=f32).astype(bf16)
                for q in range(4):
                    j = part * 4 + q
                    if j < COLS:
                        rows_ref[
                            EXP * MAIN + 32 * g : EXP * MAIN + 32 * (g + 1), LANES * j : LANES * (j + 1)
                        ] = y[32 * q : 32 * (q + 1)]
        acc_ref[...] = jnp.zeros_like(acc_ref)

    chunk = 256
    for c in range(SLOTS // chunk):
        at = slice(c * chunk, (c + 1) * chunk)
        part = jnp.dot(rows_ref[at, :], down_ref[...], preferred_element_type=f32)
        if c < EXP * MAIN // chunk:
            hidden = main_ref[at, :]
        else:
            hidden = extra_ref[...]
        both = part * hidden.astype(f32)
        acc_ref[at, :] += both[:, :LANES] + both[:, LANES:]
        part = part.astype(bf16)
        if c < EXP * MAIN // chunk:
            for h in range(2):
                g = 2 * c + h
                part_ref[BLOCK * g : BLOCK * g + LANES, :] = part[LANES * h : LANES * (h + 1)]
        else:
            for g in range(GROUPS):
                part_ref[BLOCK * g + LANES : BLOCK * (g + 1), :] = part[32 * g : 32 * (g + 1)]

    @pl.when(step == pl.num_programs(0) - 1)
    def _():
        slot_ref[...] = lax.dot_general(
            jnp.ones((8, LANES), f32),
            acc_ref[...],
            (((1,), (1,)), ((), ())),
            precision=lax.Precision.HIGHEST,
            preferred_element_type=f32,
        )


def expert(recv, main, extra, down_t):
    return pl.pallas_call(
        expert_kernel,
        grid=(HID // FBLOCK,),
        in_specs=[
            pl.BlockSpec((EXP, PIECE, LANES), lambda i: (0, 0, 0)),
            pl.BlockSpec((EXP * MAIN, FBLOCK), lambda i: (0, i)),
            pl.BlockSpec((EXP * EXTRA, FBLOCK), lambda i: (0, i)),
            pl.BlockSpec((FEAT, FBLOCK), lambda i: (0, i)),
        ],
        out_specs=[
            pl.BlockSpec((SLOTS, FBLOCK), lambda i: (0, i)),
            pl.BlockSpec((8, SLOTS), lambda i: (0, 0)),
            pl.BlockSpec((SLOTS, FEAT), lambda i: (0, 0)),
        ],
        out_shape=[
            jax.ShapeDtypeStruct((SLOTS, HID), bf16),
            jax.ShapeDtypeStruct((8, SLOTS), f32),
            jax.ShapeDtypeStruct((SLOTS, FEAT), bf16),
        ],
        scratch_shapes=[pltpu.VMEM((SLOTS, LANES), f32)],
        compiler_params=pltpu.CompilerParams(vmem_limit_bytes=VMEM),
        cost_estimate=pl.CostEstimate(flops=2_400_000_000, bytes_accessed=11_000_000, transcendentals=0),
    )(recv, main, extra, down_t)


def spread_kernel(slot_ref, out_ref):
    summed = jnp.sum(slot_ref[...], axis=0, keepdims=True)
    for g in range(GROUPS):
        out_ref[8 * g : 8 * g + 8, :LANES] = jnp.broadcast_to(
            summed[:, LANES * g : LANES * (g + 1)], (8, LANES)
        )
        start = EXP * MAIN + LANES * (g // 4)
        out_ref[8 * g : 8 * g + 8, LANES:] = jnp.broadcast_to(summed[:, start : start + LANES], (8, LANES))


def spread(slot):
    return pl.pallas_call(
        spread_kernel,
        out_shape=jax.ShapeDtypeStruct((EXP, 2 * LANES), f32),
        cost_estimate=pl.CostEstimate(flops=10_000, bytes_accessed=110_000, transcendentals=0),
    )(slot)


def gate_kernel(shift_ref, ids_ref, scores_ref, back_ref, tokens_ref, out_ref):
    hit, chosen, total, weights, rank = routing(ids_ref[...], scores_ref[...])
    main = pltpu.roll(back_ref[:, :LANES], shift_ref[0], 1)
    extra = pltpu.roll(back_ref[:, LANES:], shift_ref[1], 1)
    route = jnp.zeros((EXP, TOKS), f32)
    for r in range(MOST):
        value = main[:, r : r + 1] if r < MAIN else extra[:, r - MAIN : r - MAIN + 1]
        route = route + jnp.where(rank == float(r), value, 0.0)
    route = jnp.where(hit, route / jnp.where(hit, weights, 1.0), 0.0)
    mixed = jnp.sum(route * chosen, axis=0, keepdims=True) / total
    score = route_scale / total * (route - mixed)
    logit = (score * chosen * (1.0 - chosen)).astype(bf16)
    out_ref[...] = jnp.dot(logit, tokens_ref[...], preferred_element_type=f32)


def gate(shifts, ids, scores, back, tokens):
    return pl.pallas_call(
        gate_kernel,
        in_specs=[pl.BlockSpec(memory_space=pltpu.SMEM)] + [pl.BlockSpec(memory_space=pltpu.VMEM)] * 4,
        out_shape=jax.ShapeDtypeStruct((EXP, FEAT), f32),
        cost_estimate=pl.CostEstimate(flops=15_000_000, bytes_accessed=560_000, transcendentals=0),
    )(shifts, ids, scores, back, tokens)


def body(grad_out, tokens, scores, expert_ids, hidden_act, down_weight):
    both = ("ep", "node")
    exchange = functools.partial(lax.all_to_all, split_axis=0, concat_axis=0, tiled=True)
    source = lax.axis_index("ep") * lax.axis_size("node") + lax.axis_index("node")
    ids, scores = expert_ids.T, scores.T
    send = pack(ids, scores, grad_out)
    recv = exchange(send, both)
    main, extra = order(hidden_act[0])
    down_t = down_weight[0].T
    part, slot, rows = expert(recv, main, extra, down_t)
    slot = exchange(slot, "dp")
    part, slot = lax.optimization_barrier((part, slot))
    summed = lax.psum_scatter(part, "dp", scatter_dimension=0, tiled=True)
    back = exchange(spread(slot), both)
    weight_grad = lax.dot_general(
        jnp.concatenate([main, extra], axis=0),
        rows,
        (((0,), (0,)), ((), ())),
        preferred_element_type=f32,
    ).astype(bf16)[None]
    group, place = source // 8, source % 8
    shifts = jnp.stack([-MAIN * place % LANES, -(32 * (group % 4) + EXTRA * place) % LANES]).astype(jnp.int32)
    gate_part = gate(shifts, ids, scores, back, tokens)
    gate_rows = exchange(gate_part, both)
    gate_row = jnp.sum(gate_rows, axis=0, keepdims=True)
    gate_grad = exchange(jnp.broadcast_to(gate_row, (EXP, FEAT)), both)
    hidden_grad = restore(summed)[None]
    return (weight_grad, hidden_grad, gate_grad)


def solution(mesh):
    return jax.shard_map(
        body,
        mesh=mesh,
        in_specs=(
            P(("ep", "node"), "dp"),
            P(("ep", "node"), "dp"),
            P(("ep", "node"), None),
            P(("ep", "node"), None),
            P(("ep", "node"), None, None),
            P(("ep", "node"), None, "dp"),
        ),
        out_specs=(P(("ep", "node"), None, "dp"), P(("ep", "node"), "dp", None), P(None, "dp")),
        check_vma=False,
    )
```

time: 402 us -> 179 us (0.45)
  waiting for transfers between devices: 228 us -> 61.5 us
  local copies, waits for them, and re-layouts: 42.8 us -> 13.4 us
  other arithmetic: 29.7 us -> 0.83 us
  Pallas kernels: 0 us -> 24.7 us
  matrix products: 21.6 us -> 5.72 us
  starting transfers between devices: 33.3 us -> 25.5 us
    psum x1 -> x0, waiting for transfers between devices: 153 us -> none  [body(): gate_grad = lax.psum(gate_part, ('ep', 'node'))]
    all_to_all x0 -> x2, blocking collectives: none -> 31.7 us  [the longest x1 16.7 us: body(): slot = exchange(slot, 'dp')]
    psum x1 -> x0, blocking collectives: 29.3 us -> none  [body(): summed = lax.psum(partial_value, 'dp')]
    pallas_call x0 -> x6, Pallas kernels: none -> 24.7 us  [the longest x1 8.46 us: expert(): pl.pallas_call(expert_kernel, grid=(HID // FBLOCK,), in_specs=[pl.BlockSp...]
    another operation x3 -> x1, other arithmetic: 18.2 us -> 0.67 us  [body(): jnp.stack([-MAIN * place % LANES, -(32 * (group % 4) + EXTRA * place) % L...]
    dot_general x6 -> x1, matrix products: 21.6 us -> 5.72 us  [body(): lax.dot_general(jnp.concatenate([main, extra], axis=0), rows, (((0,), (0,...]
    convert_element_type x5 -> x0, local copies, waits for them, and re-layouts: 15.7 us -> none  [the longest x2 10.7 us: body(): rows.astype(jnp.float32)]
    gather x8 -> x0, local copies, waits for them, and re-layouts: 13.6 us -> none  [the longest x5 7.34 us: body(): chosen = jnp.take_along_axis(scores, expert_ids, axis=1)]
  transfers between devices with their start and end apart: 5 -> 4, of which waited for: 4 -> 3; matrix products, arithmetic and copies ran while one was open for 8% -> 8% of each run, Pallas kernels for 0% -> 6%
where the time goes in v1:
time: 179 us; the launch traced here: 178 us
  waiting for transfers between devices  61.5 us (34%)
  blocking collectives  31.7 us (18%)
  starting transfers between devices  25.5 us (14%)
  Pallas kernels  24.7 us (14%)
  between operations  14.2 us (8%)
  local copies, waits for them, and re-layouts  13.4 us (7%)
  matrix products  5.72 us (3%)
    all_to_all x1, waiting for transfers between devices, body(): recv = exchange(send, both)  47.1 us
    all_to_all x1, blocking collectives, body(): slot = exchange(slot, 'dp')  16.7 us
    all_to_all x1, blocking collectives, body(): gate_rows = exchange(gate_part, both)  15 us
    all_to_all x1, starting transfers between devices, body(): recv = exchange(send, both)  11.8 us
    unnamed x18, local copies, waits for them, and re-layouts  9.87 us
    all_to_all x1, waiting for transfers between devices, body(): back = exchange(spread(slot), both)  9.05 us
    pallas_call x1, Pallas kernels, expert(): pl.pallas_call(expert_kernel, grid=(HID // FBLOCK,), in_specs=[pl.BlockSp...  8.46 us
    all_to_all x1, starting transfers between devices, body(): back = exchange(spread(slot), both)  7.42 us
  transfers between devices with their start and end apart: 4, of which 3 were waited for; matrix products, arithmetic and copies ran while one was open for 8% of the time, Pallas kernels for 6%

profile of v1, /device:TPU:1, one launch (start us, length us, event | category | flops | bytes accessed | tf_op | source)
XLA Modules:
  0.0 177.6 jit_solution(7258704478708421494)
XLA Ops:
  7.2 0.9 copy-done
  8.1 0.8 copy-done.1
  9.5 3.8 %shard_map.86 = bf16[64,144,128]{2,1,0:T(8,128)(2,1)} custom-call(s32[8,128]{1,0:T(8,128)S(1)} %bitcast.29, f32[64,128]{1,0:T(8,128)S(1)} %bitcast.26, bf16[128,896]{1,0:T(8,128)(2,1)S(1)} %copy-done), custom_call_target="tpu_custom_call" | custom-call | flops 500000000 | bytes 2700000 | tf_op jit(solution)/shard_map/pallas_call | solution.py:84
  13.4 11.8 %all-to-all-start = ((bf16[64,144,128]{2,1,0:T(8,128)(2,1)}), bf16[64,144,128]{2,1,0:T(8,128)(2,1)}, u32[]{:S(2)}, u32[]{:S(2)}) async-start(bf16[64,144,128]{2,1,0:T(8,128)(2,1)} %shard_map.86), calls=%async_computation | async-start | bytes 4718592 | tf_op jit(solution)/shard_map/all_to_all | solution.py:272
  25.2 2.9 %copy.10 = bf16[1,1024,896]{1,2,0:T(8,128)(2,1)S(1)} copy(bf16[1,1024,896]{2,1,0:T(8,128)(2,1)} %param.11) | data formatting | bytes 3670016 | tf_op args[5]
  28.1 6.6 %shard_map.85 = (bf16[1024,1024]{1,0:T(8,128)(2,1)}, bf16[256,1024]{1,0:T(8,128)(2,1)}) custom-call(bf16[1280,1024]{1,0:T(8,128)(2,1)} %bitcast.30), custom_call_target="tpu_custom_call" | custom-call | flops 500000000 | bytes 5300000 | tf_op jit(solution)/shard_map/pallas_call | solution.py:105
  34.7 47.1 %all-to-all-done.recv_ref = bf16[64,144,128]{2,1,0:T(8,128)(2,1)} async-done(((bf16[64,144,128]{2,1,0:T(8,128)(2,1)}), bf16[64,144,128]{2,1,0:T(8,128)(2,1)}, u32[]{:S(2)}, u32[]{:S(2)}) %all-to-all-start) | async-done | bytes 2359328 | tf_op jit(solution)/shard_map/all_to_all | solution.py:272
  81.8 1.6 copy-done.3
  83.4 1.0 copy-done.5
  84.5 8.5 %shard_map.87 = (bf16[1280,1024]{1,0:T(8,128)(2,1)}, f32[8,1280]{1,0:T(8,128)S(1)}, bf16[1280,896]{1,0:T(8,128)(2,1)}) custom-call(bf16[64,144,128]{2,1,0:T(8,128)(2,1)} %all-to-all-done.recv_ref, bf16[1024,1024]{1,0:T(8,128)(2,1)S(1)} %copy-done.3, bf16[256,1024]{1,0:T(8,128)(2,1)S(1)} %copy-done.5, bf16[896,1024]{1,0:T(8,128)(2,1)S(1)} %bitcast.24), custom_call_target="tpu_custom_call" | custom-call | flops 2400000000 | bytes 11000000 | tf_op jit(solution)/shard_map/pallas_call | solution.py:199
  93.0 16.7 %all_to_all.46 = f32[8,1,1280]{2,1,0:T(1,128)S(1)} all-to-all(f32[8,1,1280]{2,1,0:T(1,128)S(1)} %copy.11), channel_id=1, replica_groups=mesh['ep'=32,'node'=2,'dp'=8] {'dp'}, dimensions={0} | all-to-all | bytes 81920 | tf_op jit(solution)/shard_map/all_to_all | solution.py:276
  110.4 1.6 shard_map.89
  111.9 1.5 copy.12
  113.5 7.4 %all-to-all-start.2 = ((f32[64,1,256]{2,1,0:T(1,128)}), f32[64,1,256]{2,1,0:T(1,128)S(1)}, u32[]{:S(2)}, u32[]{:S(2)}) async-start(f32[64,1,256]{2,1,0:T(1,128)} %copy.12), calls=%async_computation.3 | async-start | bytes 131072 | tf_op jit(solution)/shard_map/all_to_all | solution.py:279
  121.6 9.0 %all-to-all-done.2 = f32[64,1,256]{2,1,0:T(1,128)S(1)} async-done(((f32[64,1,256]{2,1,0:T(1,128)}), f32[64,1,256]{2,1,0:T(1,128)S(1)}, u32[]{:S(2)}, u32[]{:S(2)}) %all-to-all-start.2) | async-done | bytes 65568 | tf_op jit(solution)/shard_map/all_to_all | solution.py:279
  131.3 2.3 %shard_map.90 = f32[64,896]{1,0:T(8,128)} custom-call(s32[2]{0:T(128)} %pad_add_fusion.shift_ref, s32[8,128]{1,0:T(8,128)} %bitcast.28, f32[64,128]{1,0:T(8,128)} %bitcast.25, f32[64,256]{1,0:T(8,128)} %bitcast.33, bf16[128,896]{1,0:T(8,128)(2,1)} %tokens_ref.1), custom_call_target="tpu_custom_call" | custom-call | flops 15000000 | bytes 560000 | tf_op jit(solution)/shard_map/pallas_call | solution.py:258
  133.6 1.2 copy.13
  134.8 15.0 %all_to_all.47 = f32[64,1,896]{2,1,0:T(1,128)S(1)} all-to-all(f32[64,1,896]{2,1,0:T(1,128)S(1)} %copy.13), channel_id=1, replica_groups=mesh['ep'=32,'node'=2,'dp'=8] {'ep','node'}, dimensions={0} | all-to-all | bytes 458752 | tf_op jit(solution)/shard_map/all_to_all | solution.py:289
  149.9 0.8 broadcast_in_dim.14
  150.7 6.2 %all-to-all-start.4 = ((f32[64,1,896]{2,1,0:T(1,128)}), f32[64,1,896]{2,1,0:T(1,128)S(1)}, u32[]{:S(2)}, u32[]{:S(2)}) async-start(f32[64,1,896]{2,1,0:T(1,128)} %broadcast_in_dim.14), calls=%async_computation.5 | async-start | bytes 458752 | tf_op jit(solution)/shard_map/all_to_all | solution.py:291
  157.0 5.7 %convert_bitcast_fusion = bf16[1,1024,896]{2,1,0:T(8,128)(2,1)} fusion(bf16[1280,896]{1,0:T(8,128)(2,1)} %get-tuple-element.12, bf16[256,1024]{1,0:T(8,128)(2,1)S(1)} %copy-done.6, bf16[1024,1024]{1,0:T(8,128)(2,1)S(1)} %copy-done.4), kind=kOutput, calls=%fused_computation.4 | convolution fusion | flops 2354970624 | bytes 6750208 | tf_op jit(solution)/shard_map/dot_general | solution.py:280
  162.7 5.4 %all-to-all-done.4 = f32[64,1,896]{2,1,0:T(1,128)S(1)} async-done(((f32[64,1,896]{2,1,0:T(1,128)}), f32[64,1,896]{2,1,0:T(1,128)S(1)}, u32[]{:S(2)}, u32[]{:S(2)}) %all-to-all-start.4) | async-done | bytes 229408 | tf_op jit(solution)/shard_map/all_to_all | solution.py:291
  168.1 0.7 copy.20
  168.8 1.9 %shard_map.88 = bf16[160,1024]{1,0:T(8,128)(2,1)} custom-call(bf16[160,1024]{1,0:T(8,128)(2,1)} %reduce-scatter.2.cloned.1.call-done.x_ref), custom_call_target="tpu_custom_call" | custom-call | flops 60000000 | bytes 660000 | tf_op jit(solution)/shard_map/pallas_call | solution.py:131
  (18 shorter events, 2.9 us)
Async XLA Ops:
  7.2 0.9 copy-start
  8.1 0.8 copy-start.1
  8.9 0.7 copy-start.2
  13.4 68.4 %all-to-all-start = ((bf16[64,144,128]{2,1,0:T(8,128)(2,1)}), bf16[64,144,128]{2,1,0:T(8,128)(2,1)}, u32[]{:S(2)}, u32[]{:S(2)}) async-start(bf16[64,144,128]{2,1,0:T(8,128)(2,1)} %shard_map.86), calls=%async_computation | async-start | bytes 4718592 | tf_op jit(solution)/shard_map/all_to_all | solution.py:272
  25.2 143.6 %reduce-scatter.2.cloned.1.call-start = ((), (), s32[]{:S(2)}) async-start(), calls=%async_computation.6 | async-start | bytes 2949120 | tf_op jit(solution)/shard_map/reduce_scatter | solution.py:278
  81.8 1.6 copy-start.3
  83.4 1.0 copy-start.5
  110.3 46.6 %copy-start.4 = (bf16[1024,1024]{1,0:T(8,128)(2,1)S(1)}, bf16[1024,1024]{1,0:T(8,128)(2,1)}, u32[]{:S(2)}) copy-start(bf16[1024,1024]{1,0:T(8,128)(2,1)} %get-tuple-element.10.main_ref) | copy-start | bytes 6291460
  110.3 46.6 %copy-start.6 = (bf16[256,1024]{1,0:T(8,128)(2,1)S(1)}, bf16[256,1024]{1,0:T(8,128)(2,1)}, u32[]{:S(2)}) copy-start(bf16[256,1024]{1,0:T(8,128)(2,1)} %get-tuple-element.11.extra_ref) | copy-start | bytes 1572868
  113.5 17.2 %all-to-all-start.2 = ((f32[64,1,256]{2,1,0:T(1,128)}), f32[64,1,256]{2,1,0:T(1,128)S(1)}, u32[]{:S(2)}, u32[]{:S(2)}) async-start(f32[64,1,256]{2,1,0:T(1,128)} %copy.12), calls=%async_computation.3 | async-start | bytes 131072 | tf_op jit(solution)/shard_map/all_to_all | solution.py:279
  150.7 17.3 %all-to-all-start.4 = ((f32[64,1,896]{2,1,0:T(1,128)}), f32[64,1,896]{2,1,0:T(1,128)S(1)}, u32[]{:S(2)}, u32[]{:S(2)}) async-start(f32[64,1,896]{2,1,0:T(1,128)} %broadcast_in_dim.14), calls=%async_computation.5 | async-start | bytes 458752 | tf_op jit(solution)/shard_map/all_to_all | solution.py:291
Sparse Core Ops, SparseCore 0:
  110.5 36.2 reduce-scatter.1

commit v2 on v1

--- a/solution.py
+++ b/solution.py
@@ -22,7 +22,7 @@
 SLOTS = EXP * MOST
 GROUPS = 8
 BLOCK = SLOTS // GROUPS
-VMEM = 48 * 1024 * 1024
+VMEM = 60 * 1024 * 1024
 bf16, f32 = jnp.bfloat16, jnp.float32
 
 
@@ -45,10 +45,20 @@
     return hit, chosen, total, weights, rank
 
 
-def pack_kernel(ids_ref, scores_ref, grad_ref, send_ref, rank_ref, weight_ref):
+def pack_kernel(ids_any, scores_any, grad_any, send_ref, ids_ref, scores_ref, grad_ref, rank_ref, weight_ref, sems):
+    copies = [
+        pltpu.make_async_copy(ids_any, ids_ref, sems.at[0]),
+        pltpu.make_async_copy(scores_any, scores_ref, sems.at[1]),
+        pltpu.make_async_copy(grad_any, grad_ref, sems.at[2]),
+    ]
+    for copy in copies:
+        copy.start()
+    copies[0].wait()
+    copies[1].wait()
     _, _, _, weights, rank = routing(ids_ref[...], scores_ref[...])
     rank_ref[...] = rank
     weight_ref[...] = weights
+    copies[2].wait()
     grad = grad_ref[...]
     row = lax.broadcasted_iota(jnp.int32, (8, MAIN, TOKS), 1)
     main_rank = row.astype(f32)
@@ -77,14 +87,25 @@
             send_ref[at, start : start + MAIN, :] = mixed.astype(bf16).reshape(8, MAIN, LANES)
         return carry
 
-    lax.fori_loop(0, EXP // 8, step, 0)
+    lax.fori_loop(0, EXP // 8, step, 0, unroll=UNROLL)
+
+
+UNROLL = 8
 
 
 def pack(ids, scores, grad):
     return pl.pallas_call(
         pack_kernel,
+        in_specs=[pl.BlockSpec(memory_space=pl.ANY)] * 3,
         out_shape=jax.ShapeDtypeStruct((EXP, PIECE, LANES), bf16),
-        scratch_shapes=[pltpu.VMEM((EXP, TOKS), f32), pltpu.VMEM((EXP, TOKS), f32)],
+        scratch_shapes=[
+            pltpu.VMEM((TOP, TOKS), jnp.int32),
+            pltpu.VMEM((EXP, TOKS), f32),
+            pltpu.VMEM((TOKS, FEAT), bf16),
+            pltpu.VMEM((EXP, TOKS), f32),
+            pltpu.VMEM((EXP, TOKS), f32),
+            pltpu.SemaphoreType.DMA((3,)),
+        ],
         compiler_params=pltpu.CompilerParams(vmem_limit_bytes=VMEM),
         cost_estimate=pl.CostEstimate(flops=500_000_000, bytes_accessed=2_700_000, transcendentals=0),
     )(ids, scores, grad)
@@ -135,11 +156,12 @@
     )(x)
 
 
-FBLOCK = 256
-
-
-def expert_kernel(recv_ref, main_ref, extra_ref, down_ref, part_ref, slot_ref, rows_ref, acc_ref):
+FBLOCK = 512
+
+
+def expert_kernel(recv_ref, main_ref, extra_ref, down_ref, part_ref, slot_ref, rows_any, rows_ref, acc_ref, sem):
     step = pl.program_id(0)
+    keep = pltpu.make_async_copy(rows_ref, rows_any, sem)
 
     @pl.when(step == 0)
     def _():
@@ -164,21 +186,21 @@
                             EXP * MAIN + 32 * g : EXP * MAIN + 32 * (g + 1), LANES * j : LANES * (j + 1)
                         ] = y[32 * q : 32 * (q + 1)]
         acc_ref[...] = jnp.zeros_like(acc_ref)
-
-    chunk = 256
-    for c in range(SLOTS // chunk):
-        at = slice(c * chunk, (c + 1) * chunk)
+        keep.start()
+
+    for c in range(SLOTS // CHUNK):
+        at = slice(c * CHUNK, (c + 1) * CHUNK)
         part = jnp.dot(rows_ref[at, :], down_ref[...], preferred_element_type=f32)
-        if c < EXP * MAIN // chunk:
+        if c < EXP * MAIN // CHUNK:
             hidden = main_ref[at, :]
         else:
             hidden = extra_ref[...]
         both = part * hidden.astype(f32)
-        acc_ref[at, :] += both[:, :LANES] + both[:, LANES:]
+        acc_ref[at, :] += sum(both[:, LANES * q : LANES * (q + 1)] for q in range(FBLOCK // LANES))
         part = part.astype(bf16)
-        if c < EXP * MAIN // chunk:
-            for h in range(2):
-                g = 2 * c + h
+        if c < EXP * MAIN // CHUNK:
+            for h in range(CHUNK // LANES):
+                g = CHUNK // LANES * c + h
                 part_ref[BLOCK * g : BLOCK * g + LANES, :] = part[LANES * h : LANES * (h + 1)]
         else:
             for g in range(GROUPS):
@@ -186,13 +208,22 @@
 
     @pl.when(step == pl.num_programs(0) - 1)
     def _():
-        slot_ref[...] = lax.dot_general(
-            jnp.ones((8, LANES), f32),
-            acc_ref[...],
-            (((1,), (1,)), ((), ())),
-            precision=lax.Precision.HIGHEST,
-            preferred_element_type=f32,
-        )
+        ones = jnp.ones((8, LANES), bf16)
+        rest = acc_ref[...]
+        sums = jnp.zeros((8, SLOTS), f32)
+        for _ in range(3):
+            term = rest.astype(bf16)
+            rest = rest - term.astype(f32)
+            sums = sums + lax.dot_general(
+                ones, term, (((1,), (1,)), ((), ())), preferred_element_type=f32
+            )
+        for g in range(SLOTS // LANES):
+            slot_ref[:, g, :] = sums[:, LANES * g : LANES * (g + 1)]
+        keep.wait()
+
+
+CHUNK = 256
+SLOT_ROWS = 16
 
 
 def expert(recv, main, extra, down_t):
@@ -207,72 +238,106 @@
         ],
         out_specs=[
             pl.BlockSpec((SLOTS, FBLOCK), lambda i: (0, i)),
-            pl.BlockSpec((8, SLOTS), lambda i: (0, 0)),
-            pl.BlockSpec((SLOTS, FEAT), lambda i: (0, 0)),
+            pl.BlockSpec((GROUPS, SLOT_ROWS, LANES), lambda i: (0, 0, 0)),
+            pl.BlockSpec(memory_space=pl.ANY),
         ],
         out_shape=[
             jax.ShapeDtypeStruct((SLOTS, HID), bf16),
-            jax.ShapeDtypeStruct((8, SLOTS), f32),
+            jax.ShapeDtypeStruct((GROUPS, SLOT_ROWS, LANES), f32),
             jax.ShapeDtypeStruct((SLOTS, FEAT), bf16),
         ],
-        scratch_shapes=[pltpu.VMEM((SLOTS, LANES), f32)],
+        scratch_shapes=[
+            pltpu.VMEM((SLOTS, FEAT), bf16),
+            pltpu.VMEM((SLOTS, LANES), f32),
+            pltpu.SemaphoreType.DMA(()),
+        ],
         compiler_params=pltpu.CompilerParams(vmem_limit_bytes=VMEM),
         cost_estimate=pl.CostEstimate(flops=2_400_000_000, bytes_accessed=11_000_000, transcendentals=0),
     )(recv, main, extra, down_t)
 
 
 def spread_kernel(slot_ref, out_ref):
-    summed = jnp.sum(slot_ref[...], axis=0, keepdims=True)
-    for g in range(GROUPS):
-        out_ref[8 * g : 8 * g + 8, :LANES] = jnp.broadcast_to(
-            summed[:, LANES * g : LANES * (g + 1)], (8, LANES)
-        )
-        start = EXP * MAIN + LANES * (g // 4)
-        out_ref[8 * g : 8 * g + 8, LANES:] = jnp.broadcast_to(summed[:, start : start + LANES], (8, LANES))
+    summed = jnp.sum(slot_ref[...], axis=0)
+    main = summed[:GROUPS]
+    pairs = summed[GROUPS : GROUPS + 2]
+    lane = lax.broadcasted_iota(jnp.int32, (GROUPS, LANES), 1)
+    group = lax.broadcasted_iota(jnp.int32, (GROUPS, LANES), 0)
+    extra = jnp.zeros((GROUPS, LANES), f32)
+    for q in range(4):
+        moved = pltpu.roll(pairs, (MAIN - 32 * q) % LANES, 1)
+        for h in range(2):
+            extra = jnp.where(group == 4 * h + q, moved[h : h + 1], extra)
+    for place in range(8):
+        a = pltpu.roll(main, -MAIN * place % LANES, 1) if place else main
+        b = pltpu.roll(extra, -EXTRA * place % LANES, 1) if place else extra
+        value = jnp.where(lane < MAIN, a, b)
+        for g in range(GROUPS):
+            out_ref[8 * g + place : 8 * g + place + 1, :] = value[g : g + 1]
 
 
 def spread(slot):
     return pl.pallas_call(
         spread_kernel,
-        out_shape=jax.ShapeDtypeStruct((EXP, 2 * LANES), f32),
-        cost_estimate=pl.CostEstimate(flops=10_000, bytes_accessed=110_000, transcendentals=0),
+        out_shape=jax.ShapeDtypeStruct((EXP, LANES), f32),
+        cost_estimate=pl.CostEstimate(flops=10_000, bytes_accessed=100_000, transcendentals=0),
     )(slot)
 
 
-def gate_kernel(shift_ref, ids_ref, scores_ref, back_ref, tokens_ref, out_ref):
+def gate_kernel(ids_ref, scores_ref, back_ref, tokens_ref, out_ref):
     hit, chosen, total, weights, rank = routing(ids_ref[...], scores_ref[...])
-    main = pltpu.roll(back_ref[:, :LANES], shift_ref[0], 1)
-    extra = pltpu.roll(back_ref[:, LANES:], shift_ref[1], 1)
     route = jnp.zeros((EXP, TOKS), f32)
     for r in range(MOST):
-        value = main[:, r : r + 1] if r < MAIN else extra[:, r - MAIN : r - MAIN + 1]
-        route = route + jnp.where(rank == float(r), value, 0.0)
+        route = route + jnp.where(rank == float(r), back_ref[:, r : r + 1], 0.0)
     route = jnp.where(hit, route / jnp.where(hit, weights, 1.0), 0.0)
     mixed = jnp.sum(route * chosen, axis=0, keepdims=True) / total
     score = route_scale / total * (route - mixed)
     logit = (score * chosen * (1.0 - chosen)).astype(bf16)
-    out_ref[...] = jnp.dot(logit, tokens_ref[...], preferred_element_type=f32)
-
-
-def gate(shifts, ids, scores, back, tokens):
+    grad = jnp.dot(logit, tokens_ref[...], preferred_element_type=f32)
+    for j in range(COLS):
+        out_ref[:, j, :] = grad[:, LANES * j : LANES * (j + 1)]
+    out_ref[:, COLS, :] = jnp.zeros((EXP, LANES), f32)
+
+
+def gate(ids, scores, back, tokens):
     return pl.pallas_call(
         gate_kernel,
-        in_specs=[pl.BlockSpec(memory_space=pltpu.SMEM)] + [pl.BlockSpec(memory_space=pltpu.VMEM)] * 4,
+        out_shape=jax.ShapeDtypeStruct((EXP, COLS + 1, LANES), f32),
+        cost_estimate=pl.CostEstimate(flops=15_000_000, bytes_accessed=560_000, transcendentals=0),
+    )(ids, scores, back, tokens)
+
+
+def total_kernel(x_ref, out_ref):
+    out_ref[...] = jnp.broadcast_to(jnp.sum(x_ref[...], axis=0, keepdims=True), out_ref.shape)
+
+
+def total_rows(x):
+    return pl.pallas_call(
+        total_kernel,
+        out_shape=jax.ShapeDtypeStruct(x.shape, f32),
+        cost_estimate=pl.CostEstimate(flops=66_000, bytes_accessed=520_000, transcendentals=0),
+    )(x)
+
+
+def flatten_kernel(x_ref, out_ref):
+    for j in range(COLS):
+        out_ref[:, LANES * j : LANES * (j + 1)] = x_ref[:, j, :]
+
+
+def flatten(x):
+    return pl.pallas_call(
+        flatten_kernel,
         out_shape=jax.ShapeDtypeStruct((EXP, FEAT), f32),
-        cost_estimate=pl.CostEstimate(flops=15_000_000, bytes_accessed=560_000, transcendentals=0),
-    )(shifts, ids, scores, back, tokens)
+        cost_estimate=pl.CostEstimate(flops=0, bytes_accessed=490_000, transcendentals=0),
+    )(x)
 
 
 def body(grad_out, tokens, scores, expert_ids, hidden_act, down_weight):
     both = ("ep", "node")
     exchange = functools.partial(lax.all_to_all, split_axis=0, concat_axis=0, tiled=True)
-    source = lax.axis_index("ep") * lax.axis_size("node") + lax.axis_index("node")
     ids, scores = expert_ids.T, scores.T
-    send = pack(ids, scores, grad_out)
-    recv = exchange(send, both)
+    recv = exchange(pack(ids, scores, grad_out), both)
     main, extra = order(hidden_act[0])
-    down_t = down_weight[0].T
-    part, slot, rows = expert(recv, main, extra, down_t)
+    part, slot, rows = expert(recv, main, extra, down_weight[0].T)
     slot = exchange(slot, "dp")
     part, slot = lax.optimization_barrier((part, slot))
     summed = lax.psum_scatter(part, "dp", scatter_dimension=0, tiled=True)
@@ -283,12 +348,9 @@
         (((0,), (0,)), ((), ())),
         preferred_element_type=f32,
     ).astype(bf16)[None]
-    group, place = source // 8, source % 8
-    shifts = jnp.stack([-MAIN * place % LANES, -(32 * (group % 4) + EXTRA * place) % LANES]).astype(jnp.int32)
-    gate_part = gate(shifts, ids, scores, back, tokens)
-    gate_rows = exchange(gate_part, both)
-    gate_row = jnp.sum(gate_rows, axis=0, keepdims=True)
-    gate_grad = exchange(jnp.broadcast_to(gate_row, (EXP, FEAT)), both)
+    back, weight_grad = lax.optimization_barrier((back, weight_grad))
+    gate_rows = exchange(gate(ids, scores, back, tokens), both)
+    gate_grad = flatten(exchange(total_rows(gate_rows), both))
     hidden_grad = restore(summed)[None]
     return (weight_grad, hidden_grad, gate_grad)
 

time: 179 us -> 177 us (0.989)
  blocking collectives: 31.7 us -> 54.5 us
  waiting for transfers between devices: 61.5 us -> 49.7 us
  local copies, waits for them, and re-layouts: 13.4 us -> 5.84 us
  starting transfers between devices: 25.5 us -> 19.2 us
  Pallas kernels: 24.7 us -> 27.2 us
    all_to_all x1 -> x2, blocking collectives: 15 us -> 37.1 us  [the longest x1 19 us: body(): gate_rows = exchange(gate(ids, scores, back, tokens), both)]
    all_to_all x2 -> x1, starting transfers between devices: 18 us -> 11.6 us  [body(): recv = exchange(pack(ids, scores, grad_out), both)]
    all_to_all x2 -> x1, waiting for transfers between devices: 52.5 us -> 46.2 us  [body(): recv = exchange(pack(ids, scores, grad_out), both)]
    all_to_all x1, waiting for transfers between devices: 9.05 us -> 3.47 us  [body(): back = exchange(spread(slot), both)]
    unnamed x18 -> x9, local copies, waits for them, and re-layouts: 9.87 us -> 5.84 us
    pallas_call x3 -> x5, Pallas kernels: 7.69 us -> 10.9 us  [the longest x1 3.52 us: pack(): pl.pallas_call(pack_kernel, in_specs=[pl.BlockSpec(memory_space=pl.ANY)]...]
    all_to_all x3 -> x0, local copies, waits for them, and re-layouts: 2.76 us -> none  [the longest x1 1.54 us: body(): back = exchange(spread(slot), both)]
  transfers between devices with their start and end apart: 4 -> 3, of which waited for: 3 -> 2; matrix products, arithmetic and copies ran while one was open for 8% -> 5% of each run, Pallas kernels for 6% -> 8%
where the time goes in v2:
time: 177 us; the launch traced here: 176 us
  blocking collectives  54.5 us (31%)
  waiting for transfers between devices  49.7 us (28%)
  Pallas kernels  27.2 us (15%)
  starting transfers between devices  19.2 us (11%)
  between operations  14.1 us (8%)
  local copies, waits for them, and re-layouts  5.84 us (3%)
  matrix products  5.72 us (3%)
    all_to_all x1, waiting for transfers between devices, body(): recv = exchange(pack(ids, scores, grad_out), both)  46.2 us
    all_to_all x1, blocking collectives, body(): gate_rows = exchange(gate(ids, scores, back, tokens), both)  19 us
    all_to_all x1, blocking collectives, body(): gate_grad = flatten(exchange(total_rows(gate_rows), both))  18.1 us
    all_to_all x1, blocking collectives, body(): slot = exchange(slot, 'dp')  17.4 us
    all_to_all x1, starting transfers between devices, body(): recv = exchange(pack(ids, scores, grad_out), both)  11.6 us
    pallas_call x1, Pallas kernels, expert(): pl.pallas_call(expert_kernel, grid=(HID // FBLOCK,), in_specs=[pl.BlockSp...  7.71 us
    all_to_all x1, starting transfers between devices, body(): back = exchange(spread(slot), both)  7.49 us
    pallas_call x1, Pallas kernels, order(): pl.pallas_call(order_kernel, grid=(GROUPS,), in_specs=[pl.BlockSpec((BLOC...  6.63 us
  transfers between devices with their start and end apart: 3, of which 2 were waited for; matrix products, arithmetic and copies ran while one was open for 5% of the time, Pallas kernels for 8%

profile of v2, /device:TPU:1, one launch (start us, length us, event | category | flops | bytes accessed | tf_op | source)
XLA Modules:
  0.0 176.2 jit_solution(9931660226655705684)
XLA Ops:
  7.2 3.5 %shard_map.85 = bf16[64,144,128]{2,1,0:T(8,128)(2,1)} custom-call(s32[8,128]{1,0:T(8,128)} %bitcast.21, f32[64,128]{1,0:T(8,128)} %bitcast.17, bf16[128,896]{1,0:T(8,128)(2,1)} %grad_any.1), custom_call_target="tpu_custom_call" | custom-call | flops 500000000 | bytes 2700000 | tf_op jit(solution)/shard_map/pallas_call | solution.py:97
  10.7 11.6 %all-to-all-start = ((bf16[64,144,128]{2,1,0:T(8,128)(2,1)}), bf16[64,144,128]{2,1,0:T(8,128)(2,1)S(1)}, u32[]{:S(2)}, u32[]{:S(2)}) async-start(bf16[64,144,128]{2,1,0:T(8,128)(2,1)} %shard_map.85), calls=%async_computation | async-start | bytes 4718592 | tf_op jit(solution)/shard_map/all_to_all | solution.py:338
  22.3 0.0 reduce-scatter.2.cloned.1.call-start
  22.4 3.8 %copy.10 = bf16[1,1024,896]{1,2,0:T(8,128)(2,1)} copy(bf16[1,1024,896]{2,1,0:T(8,128)(2,1)} %param.11) | data formatting | bytes 3670016 | tf_op args[5]
  26.2 6.6 %shard_map.86 = (bf16[1024,1024]{1,0:T(8,128)(2,1)}, bf16[256,1024]{1,0:T(8,128)(2,1)}) custom-call(bf16[1280,1024]{1,0:T(8,128)(2,1)} %bitcast.14), custom_call_target="tpu_custom_call" | custom-call | flops 500000000 | bytes 5300000 | tf_op jit(solution)/shard_map/pallas_call | solution.py:126
  32.8 46.2 %all-to-all-done.recv_ref = bf16[64,144,128]{2,1,0:T(8,128)(2,1)S(1)} async-done(((bf16[64,144,128]{2,1,0:T(8,128)(2,1)}), bf16[64,144,128]{2,1,0:T(8,128)(2,1)S(1)}, u32[]{:S(2)}, u32[]{:S(2)}) %all-to-all-start) | async-done | bytes 2359328 | tf_op jit(solution)/shard_map/all_to_all | solution.py:338
  79.0 1.4 copy-done
  80.4 7.7 %shard_map.87 = (bf16[1280,1024]{1,0:T(8,128)(2,1)}, f32[8,16,128]{2,1,0:T(8,128)}, bf16[1280,896]{1,0:T(8,128)(2,1)}) custom-call(bf16[64,144,128]{2,1,0:T(8,128)(2,1)} %copy-done, bf16[1024,1024]{1,0:T(8,128)(2,1)} %get-tuple-element.12.main_ref, bf16[256,1024]{1,0:T(8,128)(2,1)} %get-tuple-element.13.extra_ref, bf16[896,1024]{1,0:T(8,128)(2,1)} %bitcast.15), custom_call_target="tpu_custom_call" | custom-call | flops 2400000000 | bytes 11000000 | tf_op jit(solution)/shard_map/pallas_call | solution.py:230
  88.1 0.0 copy-start.2
  88.2 0.0 copy-start.3
  88.2 17.4 %all_to_all.32.slot_ref = f32[8,16,128]{2,1,0:T(8,128)} all-to-all(f32[8,16,128]{2,1,0:T(8,128)} %get-tuple-element.15), channel_id=1, replica_groups=mesh['ep'=32,'node'=2,'dp'=8] {'dp'}, dimensions={0} | all-to-all | bytes 131072 | tf_op jit(solution)/shard_map/all_to_all | solution.py:341
  105.6 0.0 reduce-scatter.2.cloned.1.call-update
  105.6 1.6 shard_map.88
  107.2 7.5 %all-to-all-start.2 = ((f32[64,1,128]{2,1,0:T(1,128)}), f32[64,1,128]{2,1,0:T(1,128)S(1)}, u32[]{:S(2)}, u32[]{:S(2)}) async-start(f32[64,1,128]{2,1,0:T(1,128)} %bitcast.20), calls=%async_computation.2 | async-start | bytes 65536 | tf_op jit(solution)/shard_map/all_to_all | solution.py:344
  114.7 0.0 copy-done.2
  114.8 5.7 %convert_bitcast_fusion = bf16[1,1024,896]{2,1,0:T(8,128)(2,1)} fusion(bf16[1280,896]{1,0:T(8,128)(2,1)} %get-tuple-element.17, bf16[256,1024]{1,0:T(8,128)(2,1)S(1)} %copy-done.3, bf16[1024,1024]{1,0:T(8,128)(2,1)S(1)} %copy-done.2), kind=kOutput, calls=%fused_computation.4 | convolution fusion | flops 2354970624 | bytes 6750208 | tf_op jit(solution)/shard_map/dot_general | solution.py:345
  120.5 3.5 %all-to-all-done.2 = f32[64,1,128]{2,1,0:T(1,128)S(1)} async-done(((f32[64,1,128]{2,1,0:T(1,128)}), f32[64,1,128]{2,1,0:T(1,128)S(1)}, u32[]{:S(2)}, u32[]{:S(2)}) %all-to-all-start.2) | async-done | bytes 32800 | tf_op jit(solution)/shard_map/all_to_all | solution.py:344
  123.9 0.6 copy-done.1
  124.6 2.3 %shard_map.90 = f32[64,8,128]{2,1,0:T(8,128)} custom-call(s32[8,128]{1,0:T(8,128)} %bitcast.22, f32[64,128]{1,0:T(8,128)} %bitcast.18, f32[64,128]{1,0:T(8,128)} %bitcast.19, bf16[128,896]{1,0:T(8,128)(2,1)} %tokens_ref.1), custom_call_target="tpu_custom_call" | custom-call | flops 15000000 | bytes 560000 | tf_op jit(solution)/shard_map/pallas_call | solution.py:302
  126.9 19.0 %all_to_all.33.x_ref = f32[64,8,128]{2,1,0:T(8,128)} all-to-all(f32[64,8,128]{2,1,0:T(8,128)} %shard_map.90), channel_id=1, replica_groups=mesh['ep'=32,'node'=2,'dp'=8] {'ep','node'}, dimensions={0} | all-to-all | bytes 524288 | tf_op jit(solution)/shard_map/all_to_all | solution.py:352
  145.8 1.7 shard_map.91
  147.6 18.1 %all_to_all.34.x_ref = f32[64,8,128]{2,1,0:T(8,128)} all-to-all(f32[64,8,128]{2,1,0:T(8,128)} %shard_map.91), channel_id=1, replica_groups=mesh['ep'=32,'node'=2,'dp'=8] {'ep','node'}, dimensions={0} | all-to-all | bytes 524288 | tf_op jit(solution)/shard_map/all_to_all | solution.py:353
  165.7 1.8 shard_map.92
  167.5 1.9 %shard_map.89 = bf16[160,1024]{1,0:T(8,128)(2,1)} custom-call(bf16[160,1024]{1,0:T(8,128)(2,1)} %reduce-scatter.2.cloned.1.call-done.x_ref), custom_call_target="tpu_custom_call" | custom-call | flops 60000000 | bytes 660000 | tf_op jit(solution)/shard_map/pallas_call | solution.py:152
  (4 shorter events, 0.0 us)
Async XLA Ops:
  10.7 68.3 %all-to-all-start = ((bf16[64,144,128]{2,1,0:T(8,128)(2,1)}), bf16[64,144,128]{2,1,0:T(8,128)(2,1)S(1)}, u32[]{:S(2)}, u32[]{:S(2)}) async-start(bf16[64,144,128]{2,1,0:T(8,128)(2,1)} %shard_map.85), calls=%async_computation | async-start | bytes 4718592 | tf_op jit(solution)/shard_map/all_to_all | solution.py:338
  22.3 145.1 %reduce-scatter.2.cloned.1.call-start = ((), (), s32[]{:S(2)}) async-start(), calls=%async_computation.6 | async-start | bytes 2949120 | tf_op jit(solution)/shard_map/reduce_scatter | solution.py:343
  79.0 1.4 copy-start
  88.1 26.6 %copy-start.2 = (bf16[1024,1024]{1,0:T(8,128)(2,1)S(1)}, bf16[1024,1024]{1,0:T(8,128)(2,1)}, u32[]{:S(2)}) copy-start(bf16[1024,1024]{1,0:T(8,128)(2,1)} %get-tuple-element.12.main_ref) | copy-start | bytes 6291460
  88.2 26.6 %copy-start.3 = (bf16[256,1024]{1,0:T(8,128)(2,1)S(1)}, bf16[256,1024]{1,0:T(8,128)(2,1)}, u32[]{:S(2)}) copy-start(bf16[256,1024]{1,0:T(8,128)(2,1)} %get-tuple-element.13.extra_ref) | copy-start | bytes 1572868
  107.2 16.7 %all-to-all-start.2 = ((f32[64,1,128]{2,1,0:T(1,128)}), f32[64,1,128]{2,1,0:T(1,128)S(1)}, u32[]{:S(2)}, u32[]{:S(2)}) async-start(f32[64,1,128]{2,1,0:T(1,128)} %bitcast.20), calls=%async_computation.2 | async-start | bytes 65536 | tf_op jit(solution)/shard_map/all_to_all | solution.py:344
  123.9 0.6 copy-start.1
Sparse Core Ops, SparseCore 0:
  105.7 36.7 reduce-scatter.1

commit v3 on v2

--- a/solution.py
+++ b/solution.py
@@ -22,7 +22,7 @@
 SLOTS = EXP * MOST
 GROUPS = 8
 BLOCK = SLOTS // GROUPS
-VMEM = 60 * 1024 * 1024
+MIB = 1024 * 1024
 bf16, f32 = jnp.bfloat16, jnp.float32
 
 
@@ -106,7 +106,7 @@
             pltpu.VMEM((EXP, TOKS), f32),
             pltpu.SemaphoreType.DMA((3,)),
         ],
-        compiler_params=pltpu.CompilerParams(vmem_limit_bytes=VMEM),
+        compiler_params=pltpu.CompilerParams(vmem_limit_bytes=60 * MIB),
         cost_estimate=pl.CostEstimate(flops=500_000_000, bytes_accessed=2_700_000, transcendentals=0),
     )(ids, scores, grad)
 
@@ -152,6 +152,7 @@
     return pl.pallas_call(
         restore_kernel,
         out_shape=jax.ShapeDtypeStruct((BLOCK, HID), bf16),
+        compiler_params=pltpu.CompilerParams(vmem_limit_bytes=4 * MIB),
         cost_estimate=pl.CostEstimate(flops=60_000_000, bytes_accessed=660_000, transcendentals=0),
     )(x)
 
@@ -251,7 +252,7 @@
             pltpu.VMEM((SLOTS, LANES), f32),
             pltpu.SemaphoreType.DMA(()),
         ],
-        compiler_params=pltpu.CompilerParams(vmem_limit_bytes=VMEM),
+        compiler_params=pltpu.CompilerParams(vmem_limit_bytes=24 * MIB),
         cost_estimate=pl.CostEstimate(flops=2_400_000_000, bytes_accessed=11_000_000, transcendentals=0),
     )(recv, main, extra, down_t)
 
@@ -279,6 +280,7 @@
     return pl.pallas_call(
         spread_kernel,
         out_shape=jax.ShapeDtypeStruct((EXP, LANES), f32),
+        compiler_params=pltpu.CompilerParams(vmem_limit_bytes=2 * MIB),
         cost_estimate=pl.CostEstimate(flops=10_000, bytes_accessed=100_000, transcendentals=0),
     )(slot)
 
@@ -292,43 +294,16 @@
     mixed = jnp.sum(route * chosen, axis=0, keepdims=True) / total
     score = route_scale / total * (route - mixed)
     logit = (score * chosen * (1.0 - chosen)).astype(bf16)
-    grad = jnp.dot(logit, tokens_ref[...], preferred_element_type=f32)
-    for j in range(COLS):
-        out_ref[:, j, :] = grad[:, LANES * j : LANES * (j + 1)]
-    out_ref[:, COLS, :] = jnp.zeros((EXP, LANES), f32)
+    out_ref[...] = jnp.dot(logit, tokens_ref[...], preferred_element_type=f32)
 
 
 def gate(ids, scores, back, tokens):
     return pl.pallas_call(
         gate_kernel,
-        out_shape=jax.ShapeDtypeStruct((EXP, COLS + 1, LANES), f32),
+        out_shape=jax.ShapeDtypeStruct((EXP, FEAT), f32),
+        compiler_params=pltpu.CompilerParams(vmem_limit_bytes=4 * MIB),
         cost_estimate=pl.CostEstimate(flops=15_000_000, bytes_accessed=560_000, transcendentals=0),
     )(ids, scores, back, tokens)
-
-
-def total_kernel(x_ref, out_ref):
-    out_ref[...] = jnp.broadcast_to(jnp.sum(x_ref[...], axis=0, keepdims=True), out_ref.shape)
-
-
-def total_rows(x):
-    return pl.pallas_call(
-        total_kernel,
-        out_shape=jax.ShapeDtypeStruct(x.shape, f32),
-        cost_estimate=pl.CostEstimate(flops=66_000, bytes_accessed=520_000, transcendentals=0),
-    )(x)
-
-
-def flatten_kernel(x_ref, out_ref):
-    for j in range(COLS):
-        out_ref[:, LANES * j : LANES * (j + 1)] = x_ref[:, j, :]
-
-
-def flatten(x):
-    return pl.pallas_call(
-        flatten_kernel,
-        out_shape=jax.ShapeDtypeStruct((EXP, FEAT), f32),
-        cost_estimate=pl.CostEstimate(flops=0, bytes_accessed=490_000, transcendentals=0),
-    )(x)
 
 
 def body(grad_out, tokens, scores, expert_ids, hidden_act, down_weight):
@@ -339,7 +314,6 @@
     main, extra = order(hidden_act[0])
     part, slot, rows = expert(recv, main, extra, down_weight[0].T)
     slot = exchange(slot, "dp")
-    part, slot = lax.optimization_barrier((part, slot))
     summed = lax.psum_scatter(part, "dp", scatter_dimension=0, tiled=True)
     back = exchange(spread(slot), both)
     weight_grad = lax.dot_general(
@@ -350,7 +324,9 @@
     ).astype(bf16)[None]
     back, weight_grad = lax.optimization_barrier((back, weight_grad))
     gate_rows = exchange(gate(ids, scores, back, tokens), both)
-    gate_grad = flatten(exchange(total_rows(gate_rows), both))
+    gate_row = jnp.sum(gate_rows, axis=0, keepdims=True)
+    gate_row, summed = lax.optimization_barrier((gate_row, summed))
+    gate_grad = exchange(jnp.broadcast_to(gate_row, (EXP, FEAT)), both)
     hidden_grad = restore(summed)[None]
     return (weight_grad, hidden_grad, gate_grad)
 

time: 177 us -> 171 us (0.966)
  blocking collectives: 54.5 us -> 35.1 us
  waiting for transfers between devices: 49.7 us -> 58.8 us
  Pallas kernels: 27.2 us -> 18.3 us
  local copies, waits for them, and re-layouts: 5.84 us -> 12.1 us
  starting transfers between devices: 19.2 us -> 25.4 us
    all_to_all x1 -> x0, blocking collectives: 18.1 us -> none  [body(): gate_grad = flatten(exchange(total_rows(gate_rows), both))]
    all_to_all x0 -> x1, waiting for transfers between devices: none -> 9.19 us  [body(): gate_grad = exchange(jnp.broadcast_to(gate_row, (EXP, FEAT)), both)]
    all_to_all x0 -> x1, starting transfers between devices: none -> 6.2 us  [body(): gate_grad = exchange(jnp.broadcast_to(gate_row, (EXP, FEAT)), both)]
    pallas_call x3 -> x1, Pallas kernels: 5.8 us -> 0.49 us  [gate(): pl.pallas_call(gate_kernel, out_shape=jax.ShapeDtypeStruct((EXP, FEAT), f...]
    unnamed x9 -> x22, local copies, waits for them, and re-layouts: 5.84 us -> 11 us
  transfers between devices with their start and end apart: 3 -> 4, of which waited for: 2 -> 3; matrix products, arithmetic and copies ran while one was open for 5% -> 6% of each run, Pallas kernels for 8% -> 5%
where the time goes in v3:
time: 171 us; the launch traced here: 170 us
  waiting for transfers between devices  58.8 us (34%)
  blocking collectives  35.1 us (21%)
  starting transfers between devices  25.4 us (15%)
  Pallas kernels  18.3 us (11%)
  between operations  14.2 us (8%)
  local copies, waits for them, and re-layouts  12.1 us (7%)
  matrix products  5.83 us (3%)
    all_to_all x1, waiting for transfers between devices, body(): recv = exchange(pack(ids, scores, grad_out), both)  46.2 us
    all_to_all x1, blocking collectives, body(): gate_rows = exchange(gate(ids, scores, back, tokens), both)  18 us
    all_to_all x1, blocking collectives, body(): slot = exchange(slot, 'dp')  17.1 us
    all_to_all x1, starting transfers between devices, body(): recv = exchange(pack(ids, scores, grad_out), both)  11.6 us
    unnamed x22, local copies, waits for them, and re-layouts  11 us
    all_to_all x1, waiting for transfers between devices, body(): gate_grad = exchange(jnp.broadcast_to(gate_row, (EXP, FEAT)), both)  9.19 us
    all_to_all x1, starting transfers between devices, body(): back = exchange(spread(slot), both)  7.49 us
    pallas_call x1, Pallas kernels, order(): pl.pallas_call(order_kernel, grid=(GROUPS,), in_specs=[pl.BlockSpec((BLOC...  6.62 us
  transfers between devices with their start and end apart: 4, of which 3 were waited for; matrix products, arithmetic and copies ran while one was open for 6% of the time, Pallas kernels for 5%

profile of v3, /device:TPU:1, one launch (start us, length us, event | category | flops | bytes accessed | tf_op | source)
XLA Modules:
  0.0 169.8 jit_solution(12020729396675837420)
XLA Ops:
  7.2 3.5 %shard_map.85 = bf16[64,144,128]{2,1,0:T(8,128)(2,1)} custom-call(s32[8,128]{1,0:T(8,128)} %bitcast.23, f32[64,128]{1,0:T(8,128)} %bitcast.20, bf16[128,896]{1,0:T(8,128)(2,1)} %grad_any.1), custom_call_target="tpu_custom_call" | custom-call | flops 500000000 | bytes 2700000 | tf_op jit(solution)/shard_map/pallas_call | solution.py:97
  10.7 11.6 %all-to-all-start = ((bf16[64,144,128]{2,1,0:T(8,128)(2,1)}), bf16[64,144,128]{2,1,0:T(8,128)(2,1)S(1)}, u32[]{:S(2)}, u32[]{:S(2)}) async-start(bf16[64,144,128]{2,1,0:T(8,128)(2,1)} %shard_map.85), calls=%async_computation | async-start | bytes 4718592 | tf_op jit(solution)/shard_map/all_to_all | solution.py:313
  22.4 3.8 %copy.10 = bf16[1,1024,896]{1,2,0:T(8,128)(2,1)} copy(bf16[1,1024,896]{2,1,0:T(8,128)(2,1)} %param.11) | data formatting | bytes 3670016 | tf_op args[5]
  26.2 6.6 %shard_map.86 = (bf16[1024,1024]{1,0:T(8,128)(2,1)}, bf16[256,1024]{1,0:T(8,128)(2,1)}) custom-call(bf16[1280,1024]{1,0:T(8,128)(2,1)} %bitcast.25), custom_call_target="tpu_custom_call" | custom-call | flops 500000000 | bytes 5300000 | tf_op jit(solution)/shard_map/pallas_call | solution.py:126
  32.8 46.2 %all-to-all-done.recv_ref = bf16[64,144,128]{2,1,0:T(8,128)(2,1)S(1)} async-done(((bf16[64,144,128]{2,1,0:T(8,128)(2,1)}), bf16[64,144,128]{2,1,0:T(8,128)(2,1)S(1)}, u32[]{:S(2)}, u32[]{:S(2)}) %all-to-all-start) | async-done | bytes 2359328 | tf_op jit(solution)/shard_map/all_to_all | solution.py:313
  79.0 1.5 copy-done
  80.5 1.6 copy-done.5
  82.1 1.0 copy-done.7
  83.1 6.0 %shard_map.87 = (bf16[1280,1024]{1,0:T(8,128)(2,1)}, f32[8,16,128]{2,1,0:T(8,128)S(1)}, bf16[1280,896]{1,0:T(8,128)(2,1)S(1)}) custom-call(bf16[64,144,128]{2,1,0:T(8,128)(2,1)S(1)} %all-to-all-done.recv_ref, bf16[1024,1024]{1,0:T(8,128)(2,1)S(1)} %copy-done.5, bf16[256,1024]{1,0:T(8,128)(2,1)S(1)} %copy-done.7, bf16[896,1024]{1,0:T(8,128)(2,1)S(1)} %bitcast.18), custom_call_target="tpu_custom_call" | custom-call | flops 2400000000 | bytes 11000000 | tf_op jit(solution)/shard_map/pallas_call | solution.py:231
  89.1 1.4 copy-done.9
  90.5 17.1 %all_to_all.40.slot_ref = f32[8,16,128]{2,1,0:T(8,128)S(1)} all-to-all(f32[8,16,128]{2,1,0:T(8,128)S(1)} %get-tuple-element.14), channel_id=1, replica_groups=mesh['ep'=32,'node'=2,'dp'=8] {'dp'}, dimensions={0} | all-to-all | bytes 131072 | tf_op jit(solution)/shard_map/all_to_all | solution.py:316
  107.7 0.8 shard_map.88
  108.4 7.5 %all-to-all-start.2 = ((f32[64,1,128]{2,1,0:T(1,128)}), f32[64,1,128]{2,1,0:T(1,128)S(1)}, u32[]{:S(2)}, u32[]{:S(2)}) async-start(f32[64,1,128]{2,1,0:T(1,128)} %bitcast.6), calls=%async_computation.2 | async-start | bytes 65536 | tf_op jit(solution)/shard_map/all_to_all | solution.py:318
  116.0 5.8 %convert_bitcast_fusion = bf16[1,1024,896]{2,1,0:T(8,128)(2,1)} fusion(bf16[1280,896]{1,0:T(8,128)(2,1)} %copy-done.9, bf16[256,1024]{1,0:T(8,128)(2,1)S(1)} %copy-done.8, bf16[1024,1024]{1,0:T(8,128)(2,1)S(1)} %copy-done.6), kind=kOutput, calls=%fused_computation.4 | convolution fusion | flops 2354970624 | bytes 6750208 | tf_op jit(solution)/shard_map/dot_general | solution.py:319
  121.8 3.3 %all-to-all-done.2 = f32[64,1,128]{2,1,0:T(1,128)S(1)} async-done(((f32[64,1,128]{2,1,0:T(1,128)}), f32[64,1,128]{2,1,0:T(1,128)S(1)}, u32[]{:S(2)}, u32[]{:S(2)}) %all-to-all-start.2) | async-done | bytes 32800 | tf_op jit(solution)/shard_map/all_to_all | solution.py:318
  125.2 0.5 shard_map.89
  125.6 0.2 copy.12
  125.9 18.0 %all_to_all.41 = f32[64,1,896]{2,1,0:T(1,128)S(1)} all-to-all(f32[64,1,896]{2,1,0:T(1,128)S(1)} %copy.12), channel_id=1, replica_groups=mesh['ep'=32,'node'=2,'dp'=8] {'ep','node'}, dimensions={0} | all-to-all | bytes 458752 | tf_op jit(solution)/shard_map/all_to_all | solution.py:326
  144.1 0.8 broadcast_in_dim.17
  144.9 6.2 %all-to-all-start.4 = ((f32[64,1,896]{2,1,0:T(1,128)}), f32[64,1,896]{2,1,0:T(1,128)S(1)}, u32[]{:S(2)}, u32[]{:S(2)}) async-start(f32[64,1,896]{2,1,0:T(1,128)} %broadcast_in_dim.17), calls=%async_computation.5 | async-start | bytes 458752 | tf_op jit(solution)/shard_map/all_to_all | solution.py:329
  151.1 1.0 copy-done.1
  152.1 1.0 shard_map.90
  153.0 9.2 %all-to-all-done.4 = f32[64,1,896]{2,1,0:T(1,128)S(1)} async-done(((f32[64,1,896]{2,1,0:T(1,128)}), f32[64,1,896]{2,1,0:T(1,128)S(1)}, u32[]{:S(2)}, u32[]{:S(2)}) %all-to-all-start.4) | async-done | bytes 229408 | tf_op jit(solution)/shard_map/all_to_all | solution.py:329
  162.2 0.7 copy.15
  (21 shorter events, 0.3 us)
Async XLA Ops:
  10.7 68.3 %all-to-all-start = ((bf16[64,144,128]{2,1,0:T(8,128)(2,1)}), bf16[64,144,128]{2,1,0:T(8,128)(2,1)S(1)}, u32[]{:S(2)}, u32[]{:S(2)}) async-start(bf16[64,144,128]{2,1,0:T(8,128)(2,1)} %shard_map.85), calls=%async_computation | async-start | bytes 4718592 | tf_op jit(solution)/shard_map/all_to_all | solution.py:313
  22.3 121.7 %reduce-scatter.2.cloned.1.call-start = ((), (), s32[]{:S(2)}) async-start(), calls=%async_computation.6 | async-start | bytes 2949120 | tf_op jit(solution)/shard_map/reduce_scatter | solution.py:317
  79.0 1.5 copy-start
  80.5 1.6 copy-start.5
  82.1 1.0 copy-start.7
  89.1 1.4 copy-start.9
  90.5 25.4 %copy-start.6 = (bf16[1024,1024]{1,0:T(8,128)(2,1)S(1)}, bf16[1024,1024]{1,0:T(8,128)(2,1)}, u32[]{:S(2)}) copy-start(bf16[1024,1024]{1,0:T(8,128)(2,1)} %get-tuple-element.12.main_ref) | copy-start | bytes 6291460
  90.5 25.4 %copy-start.8 = (bf16[256,1024]{1,0:T(8,128)(2,1)S(1)}, bf16[256,1024]{1,0:T(8,128)(2,1)}, u32[]{:S(2)}) copy-start(bf16[256,1024]{1,0:T(8,128)(2,1)} %get-tuple-element.13.extra_ref) | copy-start | bytes 1572868
  108.4 16.7 %all-to-all-start.2 = ((f32[64,1,128]{2,1,0:T(1,128)}), f32[64,1,128]{2,1,0:T(1,128)S(1)}, u32[]{:S(2)}, u32[]{:S(2)}) async-start(f32[64,1,128]{2,1,0:T(1,128)} %bitcast.6), calls=%async_computation.2 | async-start | bytes 65536 | tf_op jit(solution)/shard_map/all_to_all | solution.py:318
  116.0 9.2 %copy-start.2 = (bf16[128,896]{1,0:T(8,128)(2,1)S(1)}, bf16[128,896]{1,0:T(8,128)(2,1)}, u32[]{:S(2)}) copy-start(bf16[128,896]{1,0:T(8,128)(2,1)} %tokens_ref.1) | copy-start | bytes 688132
  116.0 9.2 %copy-start.3 = (f32[128,64]{0,1:T(8,128)S(1)}, f32[128,64]{0,1:T(8,128)}, u32[]{:S(2)}) copy-start(f32[128,64]{0,1:T(8,128)} %param.8) | copy-start | bytes 98308
  116.0 9.2 %copy-start.4 = (s32[128,8]{0,1:T(8,128)S(1)}, s32[128,8]{0,1:T(8,128)}, u32[]{:S(2)}) copy-start(s32[128,8]{0,1:T(8,128)} %param.9) | copy-start | bytes 12292
  144.9 17.3 %all-to-all-start.4 = ((f32[64,1,896]{2,1,0:T(1,128)}), f32[64,1,896]{2,1,0:T(1,128)S(1)}, u32[]{:S(2)}, u32[]{:S(2)}) async-start(f32[64,1,896]{2,1,0:T(1,128)} %broadcast_in_dim.17), calls=%async_computation.5 | async-start | bytes 458752 | tf_op jit(solution)/shard_map/all_to_all | solution.py:329
  151.1 1.0 copy-start.1
Sparse Core Ops, SparseCore 0:
  90.7 43.3 reduce-scatter.1

commit v4 on v3

--- a/solution.py
+++ b/solution.py
@@ -111,15 +111,13 @@
     )(ids, scores, grad)
 
 
-def order_kernel(x_ref, main_ref, extra_ref):
+def order_kernel(x_ref, y_ref):
     i = lax.broadcasted_iota(jnp.int32, (BLOCK, BLOCK), 0)
     j = lax.broadcasted_iota(jnp.int32, (BLOCK, BLOCK), 1)
     e = i - 8 * MAIN
     origin = jnp.where(i < 8 * MAIN, i // MAIN * MOST + i % MAIN, e // EXTRA * MOST + MAIN + e % EXTRA)
     move = jnp.where(origin == j, 1.0, 0.0).astype(bf16)
-    y = jnp.dot(move, x_ref[...], preferred_element_type=f32).astype(bf16)
-    main_ref[...] = y[: 8 * MAIN]
-    extra_ref[...] = y[8 * MAIN :]
+    y_ref[...] = jnp.dot(move, x_ref[...], preferred_element_type=f32).astype(bf16)
 
 
 def order(hidden):
@@ -127,14 +125,8 @@
         order_kernel,
         grid=(GROUPS,),
         in_specs=[pl.BlockSpec((BLOCK, HID), lambda i: (i, 0))],
-        out_specs=[
-            pl.BlockSpec((8 * MAIN, HID), lambda i: (i, 0)),
-            pl.BlockSpec((8 * EXTRA, HID), lambda i: (i, 0)),
-        ],
-        out_shape=[
-            jax.ShapeDtypeStruct((EXP * MAIN, HID), bf16),
-            jax.ShapeDtypeStruct((EXP * EXTRA, HID), bf16),
-        ],
+        out_specs=pl.BlockSpec((BLOCK, HID), lambda i: (i, 0)),
+        out_shape=jax.ShapeDtypeStruct((SLOTS, HID), bf16),
         cost_estimate=pl.CostEstimate(flops=500_000_000, bytes_accessed=5_300_000, transcendentals=0),
     )(hidden)
 
@@ -157,117 +149,117 @@
     )(x)
 
 
-FBLOCK = 512
-
-
-def expert_kernel(recv_ref, main_ref, extra_ref, down_ref, part_ref, slot_ref, rows_any, rows_ref, acc_ref, sem):
-    step = pl.program_id(0)
-    keep = pltpu.make_async_copy(rows_ref, rows_any, sem)
-
-    @pl.when(step == 0)
-    def _():
-        i = lax.broadcasted_iota(jnp.int32, (LANES, LANES), 0)
-        j = lax.broadcasted_iota(jnp.int32, (LANES, LANES), 1)
-        q, source, r = i // 32, i % 32 // EXTRA, i % EXTRA
-        move = jnp.where(source * MAIN + q * EXTRA + r == j, 1.0, 0.0).astype(bf16)
-        for g in range(GROUPS):
-            at = slice(8 * g, 8 * g + 8)
+PARTS = 2
+CHUNK = SLOTS // PARTS
+PAIR = EXP // PARTS
+SLOT_ROWS = 16
+
+
+def expert_kernel(
+    recv_any, hidden_any, down_any, part_any, slot_ref, rows_any,
+    recv_ref, hidden_ref, down_ref, part_ref, rows_ref, in_sems, out_sems,
+):
+    come, saved, stores = [], [], []
+    for c in range(PARTS):
+        at = slice(c * PAIR, (c + 1) * PAIR)
+        come.append(pltpu.make_async_copy(recv_any.at[at], recv_ref.at[at], in_sems.at[0, c]))
+        at = slice(c * CHUNK, (c + 1) * CHUNK)
+        saved.append(pltpu.make_async_copy(hidden_any.at[at], hidden_ref.at[at], in_sems.at[1, c]))
+        stores.append(
+            [
+                pltpu.make_async_copy(rows_ref.at[at], rows_any.at[at], out_sems.at[0, c]),
+                pltpu.make_async_copy(part_ref.at[at], part_any.at[at], out_sems.at[1, c]),
+            ]
+        )
+    weights = pltpu.make_async_copy(down_any, down_ref, in_sems.at[2, 0])
+    come[0].start()
+    weights.start()
+    for c in range(PARTS):
+        if c:
+            come[c].start()
+        saved[c].start()
+
+    i = lax.broadcasted_iota(jnp.int32, (LANES, LANES), 0)
+    j = lax.broadcasted_iota(jnp.int32, (LANES, LANES), 1)
+    q, source, r = i // 32, i % 32 // EXTRA, i % EXTRA
+    move = jnp.where(source * MAIN + q * EXTRA + r == j, 1.0, 0.0).astype(bf16)
+    ones = jnp.ones((8, LANES), bf16)
+    slot_ref[...] = jnp.zeros_like(slot_ref)
+    for c in range(PARTS):
+        at = slice(c * CHUNK, (c + 1) * CHUNK)
+        come[c].wait()
+        for g in range(c * PAIR // 8, (c + 1) * PAIR // 8):
+            some = slice(8 * g, 8 * g + 8)
             for j in range(COLS):
-                rows_ref[LANES * g : LANES * (g + 1), LANES * j : LANES * (j + 1)] = recv_ref[
-                    at, MAIN * j : MAIN * (j + 1), :
+                rows_ref[BLOCK * g : BLOCK * g + LANES, LANES * j : LANES * (j + 1)] = recv_ref[
+                    some, MAIN * j : MAIN * (j + 1), :
                 ].reshape(LANES, LANES)
             for part in range(2):
                 start = COLS * MAIN + part * MAIN
-                x = recv_ref[at, start : start + MAIN, :].reshape(LANES, LANES)
+                x = recv_ref[some, start : start + MAIN, :].reshape(LANES, LANES)
                 y = jnp.dot(move, x, preferred_element_type=f32).astype(bf16)
                 for q in range(4):
                     j = part * 4 + q
                     if j < COLS:
-                        rows_ref[
-                            EXP * MAIN + 32 * g : EXP * MAIN + 32 * (g + 1), LANES * j : LANES * (j + 1)
-                        ] = y[32 * q : 32 * (q + 1)]
-        acc_ref[...] = jnp.zeros_like(acc_ref)
-        keep.start()
-
-    for c in range(SLOTS // CHUNK):
-        at = slice(c * CHUNK, (c + 1) * CHUNK)
+                        rows_ref[BLOCK * g + LANES : BLOCK * (g + 1), LANES * j : LANES * (j + 1)] = y[
+                            32 * q : 32 * (q + 1)
+                        ]
+        stores[c][0].start()
+        if c == 0:
+            weights.wait()
+        saved[c].wait()
         part = jnp.dot(rows_ref[at, :], down_ref[...], preferred_element_type=f32)
-        if c < EXP * MAIN // CHUNK:
-            hidden = main_ref[at, :]
-        else:
-            hidden = extra_ref[...]
-        both = part * hidden.astype(f32)
-        acc_ref[at, :] += sum(both[:, LANES * q : LANES * (q + 1)] for q in range(FBLOCK // LANES))
-        part = part.astype(bf16)
-        if c < EXP * MAIN // CHUNK:
-            for h in range(CHUNK // LANES):
-                g = CHUNK // LANES * c + h
-                part_ref[BLOCK * g : BLOCK * g + LANES, :] = part[LANES * h : LANES * (h + 1)]
-        else:
-            for g in range(GROUPS):
-                part_ref[BLOCK * g + LANES : BLOCK * (g + 1), :] = part[32 * g : 32 * (g + 1)]
-
-    @pl.when(step == pl.num_programs(0) - 1)
-    def _():
-        ones = jnp.ones((8, LANES), bf16)
-        rest = acc_ref[...]
-        sums = jnp.zeros((8, SLOTS), f32)
+        both = part * hidden_ref[at, :].astype(f32)
+        rest = sum(both[:, LANES * q : LANES * (q + 1)] for q in range(HID // LANES))
+        part_ref[at, :] = part.astype(bf16)
+        stores[c][1].start()
+        sums = jnp.zeros((8, CHUNK), f32)
         for _ in range(3):
             term = rest.astype(bf16)
             rest = rest - term.astype(f32)
-            sums = sums + lax.dot_general(
-                ones, term, (((1,), (1,)), ((), ())), preferred_element_type=f32
-            )
-        for g in range(SLOTS // LANES):
-            slot_ref[:, g, :] = sums[:, LANES * g : LANES * (g + 1)]
-        keep.wait()
-
-
-CHUNK = 256
-SLOT_ROWS = 16
-
-
-def expert(recv, main, extra, down_t):
+            sums = sums + lax.dot_general(ones, term, (((1,), (1,)), ((), ())), preferred_element_type=f32)
+        for h in range(CHUNK // BLOCK):
+            g = CHUNK // BLOCK * c + h
+            slot_ref[:, g, :] = sums[:, BLOCK * h : BLOCK * h + LANES]
+            slot_ref[:, GROUPS + g, : BLOCK - LANES] = sums[:, BLOCK * h + LANES : BLOCK * (h + 1)]
+    for pair in stores:
+        for store in pair:
+            store.wait()
+
+
+EXPERT_LIMIT = 52
+
+
+def expert(recv, hidden, down_t):
+    any_space = pl.BlockSpec(memory_space=pl.ANY)
     return pl.pallas_call(
         expert_kernel,
-        grid=(HID // FBLOCK,),
-        in_specs=[
-            pl.BlockSpec((EXP, PIECE, LANES), lambda i: (0, 0, 0)),
-            pl.BlockSpec((EXP * MAIN, FBLOCK), lambda i: (0, i)),
-            pl.BlockSpec((EXP * EXTRA, FBLOCK), lambda i: (0, i)),
-            pl.BlockSpec((FEAT, FBLOCK), lambda i: (0, i)),
-        ],
-        out_specs=[
-            pl.BlockSpec((SLOTS, FBLOCK), lambda i: (0, i)),
-            pl.BlockSpec((GROUPS, SLOT_ROWS, LANES), lambda i: (0, 0, 0)),
-            pl.BlockSpec(memory_space=pl.ANY),
-        ],
+        in_specs=[any_space] * 3,
+        out_specs=[any_space, pl.BlockSpec(memory_space=pltpu.VMEM), any_space],
         out_shape=[
             jax.ShapeDtypeStruct((SLOTS, HID), bf16),
             jax.ShapeDtypeStruct((GROUPS, SLOT_ROWS, LANES), f32),
             jax.ShapeDtypeStruct((SLOTS, FEAT), bf16),
         ],
         scratch_shapes=[
+            pltpu.VMEM((EXP, PIECE, LANES), bf16),
+            pltpu.VMEM((SLOTS, HID), bf16),
+            pltpu.VMEM((FEAT, HID), bf16),
+            pltpu.VMEM((SLOTS, HID), bf16),
             pltpu.VMEM((SLOTS, FEAT), bf16),
-            pltpu.VMEM((SLOTS, LANES), f32),
-            pltpu.SemaphoreType.DMA(()),
+            pltpu.SemaphoreType.DMA((3, PARTS)),
+            pltpu.SemaphoreType.DMA((2, PARTS)),
         ],
-        compiler_params=pltpu.CompilerParams(vmem_limit_bytes=24 * MIB),
+        compiler_params=pltpu.CompilerParams(vmem_limit_bytes=EXPERT_LIMIT * MIB),
         cost_estimate=pl.CostEstimate(flops=2_400_000_000, bytes_accessed=11_000_000, transcendentals=0),
-    )(recv, main, extra, down_t)
+    )(recv, hidden, down_t)
 
 
 def spread_kernel(slot_ref, out_ref):
     summed = jnp.sum(slot_ref[...], axis=0)
     main = summed[:GROUPS]
-    pairs = summed[GROUPS : GROUPS + 2]
+    extra = pltpu.roll(summed[GROUPS:], MAIN, 1)
     lane = lax.broadcasted_iota(jnp.int32, (GROUPS, LANES), 1)
-    group = lax.broadcasted_iota(jnp.int32, (GROUPS, LANES), 0)
-    extra = jnp.zeros((GROUPS, LANES), f32)
-    for q in range(4):
-        moved = pltpu.roll(pairs, (MAIN - 32 * q) % LANES, 1)
-        for h in range(2):
-            extra = jnp.where(group == 4 * h + q, moved[h : h + 1], extra)
     for place in range(8):
         a = pltpu.roll(main, -MAIN * place % LANES, 1) if place else main
         b = pltpu.roll(extra, -EXTRA * place % LANES, 1) if place else extra
@@ -311,17 +303,13 @@
     exchange = functools.partial(lax.all_to_all, split_axis=0, concat_axis=0, tiled=True)
     ids, scores = expert_ids.T, scores.T
     recv = exchange(pack(ids, scores, grad_out), both)
-    main, extra = order(hidden_act[0])
-    part, slot, rows = expert(recv, main, extra, down_weight[0].T)
+    hidden = order(hidden_act[0])
+    part, slot, rows = expert(recv, hidden, down_weight[0].T)
     slot = exchange(slot, "dp")
     summed = lax.psum_scatter(part, "dp", scatter_dimension=0, tiled=True)
     back = exchange(spread(slot), both)
-    weight_grad = lax.dot_general(
-        jnp.concatenate([main, extra], axis=0),
-        rows,
-        (((0,), (0,)), ((), ())),
-        preferred_element_type=f32,
-    ).astype(bf16)[None]
+    weight_grad = lax.dot_general(hidden, rows, (((0,), (0,)), ((), ())), preferred_element_type=f32)
+    weight_grad = weight_grad.astype(bf16)[None]
     back, weight_grad = lax.optimization_barrier((back, weight_grad))
     gate_rows = exchange(gate(ids, scores, back, tokens), both)
     gate_row = jnp.sum(gate_rows, axis=0, keepdims=True)

time: 171 us -> 166 us (0.971)
  local copies, waits for them, and re-layouts: 12.1 us -> 7.15 us
    unnamed x22 -> x15, local copies, waits for them, and re-layouts: 11 us -> 6.1 us
  transfers between devices with their start and end apart: 4 -> 4, of which waited for: 3 -> 3; matrix products, arithmetic and copies ran while one was open for 6% -> 7% of each run, Pallas kernels for 5% -> 5%
where the time goes in v4:
time: 166 us; the launch traced here: 165 us
  waiting for transfers between devices  58.4 us (35%)
  blocking collectives  34.7 us (21%)
  starting transfers between devices  25.5 us (15%)
  Pallas kernels  19.2 us (12%)
  between operations  14.2 us (9%)
  local copies, waits for them, and re-layouts  7.15 us (4%)
  matrix products  5.54 us (3%)
    all_to_all x1, waiting for transfers between devices, body(): recv = exchange(pack(ids, scores, grad_out), both)  47 us
    all_to_all x1, blocking collectives, body(): gate_rows = exchange(gate(ids, scores, back, tokens), both)  17.6 us
    all_to_all x1, blocking collectives, body(): slot = exchange(slot, 'dp')  17.1 us
    all_to_all x1, starting transfers between devices, body(): recv = exchange(pack(ids, scores, grad_out), both)  11.8 us
    all_to_all x1, waiting for transfers between devices, body(): gate_grad = exchange(jnp.broadcast_to(gate_row, (EXP, FEAT)), both)  7.69 us
    all_to_all x1, starting transfers between devices, body(): back = exchange(spread(slot), both)  7.49 us
    pallas_call x1, Pallas kernels, expert(): pl.pallas_call(expert_kernel, in_specs=[any_space] * 3, out_specs=[any_sp...  6.82 us
    pallas_call x1, Pallas kernels, order(): pl.pallas_call(order_kernel, grid=(GROUPS,), in_specs=[pl.BlockSpec((BLOC...  6.64 us
  transfers between devices with their start and end apart: 4, of which 3 were waited for; matrix products, arithmetic and copies ran while one was open for 7% of the time, Pallas kernels for 5%

profile of v4, /device:TPU:1, one launch (start us, length us, event | category | flops | bytes accessed | tf_op | source)
XLA Modules:
  0.0 164.9 jit_solution(3349783667136064111)
XLA Ops:
  7.2 3.5 %shard_map.85 = bf16[64,144,128]{2,1,0:T(8,128)(2,1)} custom-call(s32[8,128]{1,0:T(8,128)} %bitcast.26, f32[64,128]{1,0:T(8,128)} %bitcast.23, bf16[128,896]{1,0:T(8,128)(2,1)} %grad_any.1), custom_call_target="tpu_custom_call" | custom-call | flops 500000000 | bytes 2700000 | tf_op jit(solution)/shard_map/pallas_call | solution.py:97
  10.7 11.8 %all-to-all-start = ((bf16[64,144,128]{2,1,0:T(8,128)(2,1)}), bf16[64,144,128]{2,1,0:T(8,128)(2,1)}, u32[]{:S(2)}, u32[]{:S(2)}) async-start(bf16[64,144,128]{2,1,0:T(8,128)(2,1)} %shard_map.85), calls=%async_computation | async-start | bytes 4718592 | tf_op jit(solution)/shard_map/all_to_all | solution.py:305
  22.5 0.0 reduce-scatter.2.cloned.1.call-start
  22.6 2.9 %copy.11 = bf16[1,1024,896]{1,2,0:T(8,128)(2,1)S(1)} copy(bf16[1,1024,896]{2,1,0:T(8,128)(2,1)} %param.11) | data formatting | bytes 3670016 | tf_op args[5]
  25.5 6.6 %shard_map.86.hidden_any = bf16[1280,1024]{1,0:T(8,128)(2,1)} custom-call(bf16[1280,1024]{1,0:T(8,128)(2,1)} %bitcast.28), custom_call_target="tpu_custom_call" | custom-call | flops 500000000 | bytes 5300000 | tf_op jit(solution)/shard_map/pallas_call | solution.py:124
  32.1 47.0 %all-to-all-done.recv_any = bf16[64,144,128]{2,1,0:T(8,128)(2,1)} async-done(((bf16[64,144,128]{2,1,0:T(8,128)(2,1)}), bf16[64,144,128]{2,1,0:T(8,128)(2,1)}, u32[]{:S(2)}, u32[]{:S(2)}) %all-to-all-start) | async-done | bytes 2359328 | tf_op jit(solution)/shard_map/all_to_all | solution.py:305
  79.2 6.8 %shard_map.87 = (bf16[1280,1024]{1,0:T(8,128)(2,1)}, f32[8,16,128]{2,1,0:T(8,128)S(1)}, bf16[1280,896]{1,0:T(8,128)(2,1)}) custom-call(bf16[64,144,128]{2,1,0:T(8,128)(2,1)} %all-to-all-done.recv_any, bf16[1280,1024]{1,0:T(8,128)(2,1)} %shard_map.86.hidden_any, bf16[896,1024]{1,0:T(8,128)(2,1)S(1)} %bitcast.21), custom_call_target="tpu_custom_call" | custom-call | flops 2400000000 | bytes 11000000 | tf_op jit(solution)/shard_map/pallas_call | solution.py:235
  86.0 0.0 reduce-scatter.2.cloned.1.call-update
  86.0 17.1 %all_to_all.40.slot_ref = f32[8,16,128]{2,1,0:T(8,128)S(1)} all-to-all(f32[8,16,128]{2,1,0:T(8,128)S(1)} %get-tuple-element.10), channel_id=1, replica_groups=mesh['ep'=32,'node'=2,'dp'=8] {'dp'}, dimensions={0} | all-to-all | bytes 131072 | tf_op jit(solution)/shard_map/all_to_all | solution.py:308
  103.1 0.8 shard_map.88
  103.9 7.5 %all-to-all-start.2 = ((f32[64,1,128]{2,1,0:T(1,128)}), f32[64,1,128]{2,1,0:T(1,128)S(1)}, u32[]{:S(2)}, u32[]{:S(2)}) async-start(f32[64,1,128]{2,1,0:T(1,128)} %bitcast.6), calls=%async_computation.2 | async-start | bytes 65536 | tf_op jit(solution)/shard_map/all_to_all | solution.py:310
  111.4 5.5 %convert_bitcast_fusion = bf16[1,1024,896]{1,2,0:T(8,128)(2,1)} fusion(bf16[1280,896]{1,0:T(8,128)(2,1)} %get-tuple-element.11, bf16[1280,1024]{1,0:T(8,128)(2,1)S(1)} %copy-done.4), kind=kOutput, calls=%fused_computation | convolution fusion | flops 2349727744 | bytes 6750208 | tf_op jit(solution)/shard_map/dot_general | solution.py:311
  116.9 3.6 %all-to-all-done.2 = f32[64,1,128]{2,1,0:T(1,128)S(1)} async-done(((f32[64,1,128]{2,1,0:T(1,128)}), f32[64,1,128]{2,1,0:T(1,128)S(1)}, u32[]{:S(2)}, u32[]{:S(2)}) %all-to-all-start.2) | async-done | bytes 32800 | tf_op jit(solution)/shard_map/all_to_all | solution.py:310
  120.6 0.5 shard_map.89
  121.1 0.2 copy.13
  121.3 17.6 %all_to_all.41 = f32[64,1,896]{2,1,0:T(1,128)S(1)} all-to-all(f32[64,1,896]{2,1,0:T(1,128)S(1)} %copy.13), channel_id=1, replica_groups=mesh['ep'=32,'node'=2,'dp'=8] {'ep','node'}, dimensions={0} | all-to-all | bytes 458752 | tf_op jit(solution)/shard_map/all_to_all | solution.py:314
  139.0 0.2 reduce_sum.9
  139.1 0.0 reduce-scatter.2.cloned.1.call-done.x_ref
  139.2 0.8 broadcast_in_dim.17
  140.0 6.2 %all-to-all-start.4 = ((f32[64,1,896]{2,1,0:T(1,128)}), f32[64,1,896]{2,1,0:T(1,128)S(1)}, u32[]{:S(2)}, u32[]{:S(2)}) async-start(f32[64,1,896]{2,1,0:T(1,128)} %broadcast_in_dim.17), calls=%async_computation.5 | async-start | bytes 458752 | tf_op jit(solution)/shard_map/all_to_all | solution.py:317
  146.2 2.5 %copy.14 = bf16[1,1024,896]{2,1,0:T(8,128)(2,1)} copy(bf16[1,1024,896]{1,2,0:T(8,128)(2,1)S(1)} %copy-done.5) | data formatting | bytes 3670016
  148.7 1.0 shard_map.90
  149.7 7.7 %all-to-all-done.4 = f32[64,1,896]{2,1,0:T(1,128)S(1)} async-done(((f32[64,1,896]{2,1,0:T(1,128)}), f32[64,1,896]{2,1,0:T(1,128)S(1)}, u32[]{:S(2)}, u32[]{:S(2)}) %all-to-all-start.4) | async-done | bytes 229408 | tf_op jit(solution)/shard_map/all_to_all | solution.py:317
  157.3 0.7 copy.17
  (14 shorter events, 0.1 us)
Async XLA Ops:
  10.7 68.4 %all-to-all-start = ((bf16[64,144,128]{2,1,0:T(8,128)(2,1)}), bf16[64,144,128]{2,1,0:T(8,128)(2,1)}, u32[]{:S(2)}, u32[]{:S(2)}) async-start(bf16[64,144,128]{2,1,0:T(8,128)(2,1)} %shard_map.85), calls=%async_computation | async-start | bytes 4718592 | tf_op jit(solution)/shard_map/all_to_all | solution.py:305
  22.5 116.6 %reduce-scatter.2.cloned.1.call-start = ((), (), s32[]{:S(2)}) async-start(), calls=%async_computation.6 | async-start | bytes 2949120 | tf_op jit(solution)/shard_map/reduce_scatter | solution.py:309
  86.0 25.4 %copy-start.4 = (bf16[1280,1024]{1,0:T(8,128)(2,1)S(1)}, bf16[1280,1024]{1,0:T(8,128)(2,1)}, u32[]{:S(2)}) copy-start(bf16[1280,1024]{1,0:T(8,128)(2,1)} %shard_map.86.hidden_any) | copy-start | bytes 7864324
  103.9 16.7 %all-to-all-start.2 = ((f32[64,1,128]{2,1,0:T(1,128)}), f32[64,1,128]{2,1,0:T(1,128)S(1)}, u32[]{:S(2)}, u32[]{:S(2)}) async-start(f32[64,1,128]{2,1,0:T(1,128)} %bitcast.6), calls=%async_computation.2 | async-start | bytes 65536 | tf_op jit(solution)/shard_map/all_to_all | solution.py:310
  111.4 9.2 %copy-start.1 = (bf16[128,896]{1,0:T(8,128)(2,1)S(1)}, bf16[128,896]{1,0:T(8,128)(2,1)}, u32[]{:S(2)}) copy-start(bf16[128,896]{1,0:T(8,128)(2,1)} %tokens_ref.1) | copy-start | bytes 688132
  111.4 9.2 %copy-start.2 = (f32[128,64]{0,1:T(8,128)S(1)}, f32[128,64]{0,1:T(8,128)}, u32[]{:S(2)}) copy-start(f32[128,64]{0,1:T(8,128)} %param.8) | copy-start | bytes 98308
  111.4 9.2 %copy-start.3 = (s32[128,8]{0,1:T(8,128)S(1)}, s32[128,8]{0,1:T(8,128)}, u32[]{:S(2)}) copy-start(s32[128,8]{0,1:T(8,128)} %param.9) | copy-start | bytes 12292
  116.9 29.3 %copy-start.5 = (bf16[1,1024,896]{1,2,0:T(8,128)(2,1)S(1)}, bf16[1,1024,896]{1,2,0:T(8,128)(2,1)}, u32[]{:S(2)}) copy-start(bf16[1,1024,896]{1,2,0:T(8,128)(2,1)} %convert_bitcast_fusion) | copy-start | bytes 5505028
  139.2 9.5 %copy-start = (bf16[160,1024]{1,0:T(8,128)(2,1)S(1)}, bf16[160,1024]{1,0:T(8,128)(2,1)}, u32[]{:S(2)}) copy-start(bf16[160,1024]{1,0:T(8,128)(2,1)} %reduce-scatter.2.cloned.1.call-done.x_ref) | copy-start | bytes 983044
  140.0 17.3 %all-to-all-start.4 = ((f32[64,1,896]{2,1,0:T(1,128)}), f32[64,1,896]{2,1,0:T(1,128)S(1)}, u32[]{:S(2)}, u32[]{:S(2)}) async-start(f32[64,1,896]{2,1,0:T(1,128)} %broadcast_in_dim.17), calls=%async_computation.5 | async-start | bytes 458752 | tf_op jit(solution)/shard_map/all_to_all | solution.py:317
Sparse Core Ops, SparseCore 0:
  86.1 43.3 reduce-scatter.1

commit v5 on v4

--- a/solution.py
+++ b/solution.py
@@ -22,6 +22,7 @@
 SLOTS = EXP * MOST
 GROUPS = 8
 BLOCK = SLOTS // GROUPS
+ROW = 4
 MIB = 1024 * 1024
 bf16, f32 = jnp.bfloat16, jnp.float32
 
@@ -45,7 +46,9 @@
     return hit, chosen, total, weights, rank
 
 
-def pack_kernel(ids_any, scores_any, grad_any, send_ref, ids_ref, scores_ref, grad_ref, rank_ref, weight_ref, sems):
+def pack_kernel(
+    ids_any, scores_any, grad_any, send_any, ids_ref, scores_ref, grad_ref, rank_ref, weight_ref, send_ref, sems, out_sems
+):
     copies = [
         pltpu.make_async_copy(ids_any, ids_ref, sems.at[0]),
         pltpu.make_async_copy(scores_any, scores_ref, sems.at[1]),
@@ -65,8 +68,9 @@
     extra_rank = (MAIN + row % EXTRA).astype(f32)
     quarter = lax.broadcasted_iota(jnp.int32, (8 * MAIN, LANES), 0) % MAIN // EXTRA
 
-    def step(i, carry):
-        at = pl.ds(pl.multiple_of(i * 8, 8), 8)
+    outs = []
+    for i in range(EXP // 8):
+        at = slice(8 * i, 8 * i + 8)
         ranks = rank_ref[at, :][:, None, :]
         gains = weight_ref[at, :][:, None, :]
         place = jnp.where(ranks == main_rank, gains, 0.0).reshape(8 * MAIN, TOKS).astype(bf16)
@@ -85,18 +89,17 @@
                     mixed = jnp.where(quarter == q, rows[:, LANES * j : LANES * (j + 1)], mixed)
             start = COLS * MAIN + part * MAIN
             send_ref[at, start : start + MAIN, :] = mixed.astype(bf16).reshape(8, MAIN, LANES)
-        return carry
-
-    lax.fori_loop(0, EXP // 8, step, 0, unroll=UNROLL)
-
-
-UNROLL = 8
+        outs.append(pltpu.make_async_copy(send_ref.at[at], send_any.at[at], out_sems.at[i]))
+        outs[i].start()
+    for out in outs:
+        out.wait()
 
 
 def pack(ids, scores, grad):
     return pl.pallas_call(
         pack_kernel,
         in_specs=[pl.BlockSpec(memory_space=pl.ANY)] * 3,
+        out_specs=pl.BlockSpec(memory_space=pl.ANY),
         out_shape=jax.ShapeDtypeStruct((EXP, PIECE, LANES), bf16),
         scratch_shapes=[
             pltpu.VMEM((TOP, TOKS), jnp.int32),
@@ -104,7 +107,9 @@
             pltpu.VMEM((TOKS, FEAT), bf16),
             pltpu.VMEM((EXP, TOKS), f32),
             pltpu.VMEM((EXP, TOKS), f32),
+            pltpu.VMEM((EXP, PIECE, LANES), bf16),
             pltpu.SemaphoreType.DMA((3,)),
+            pltpu.SemaphoreType.DMA((EXP // 8,)),
         ],
         compiler_params=pltpu.CompilerParams(vmem_limit_bytes=60 * MIB),
         cost_estimate=pl.CostEstimate(flops=500_000_000, bytes_accessed=2_700_000, transcendentals=0),
@@ -260,12 +265,20 @@
     main = summed[:GROUPS]
     extra = pltpu.roll(summed[GROUPS:], MAIN, 1)
     lane = lax.broadcasted_iota(jnp.int32, (GROUPS, LANES), 1)
+    span = lane[:1] // 32
     for place in range(8):
         a = pltpu.roll(main, -MAIN * place % LANES, 1) if place else main
         b = pltpu.roll(extra, -EXTRA * place % LANES, 1) if place else extra
         value = jnp.where(lane < MAIN, a, b)
-        for g in range(GROUPS):
-            out_ref[8 * g + place : 8 * g + place + 1, :] = value[g : g + 1]
+        moved = [pltpu.roll(value, 32 * k, 1) if k else value for k in range(ROW)]
+        for x in range(ROW):
+            for high in range(2):
+                line = jnp.zeros((1, LANES), f32)
+                for k in range(ROW):
+                    g = (x - k) % ROW * 2 + high
+                    line = jnp.where(span == k, moved[k][g : g + 1], line)
+                at = EXP // ROW * x + 8 * high + place
+                out_ref[at : at + 1, :] = line
 
 
 def spread(slot):
@@ -277,33 +290,51 @@
     )(slot)
 
 
-def gate_kernel(ids_ref, scores_ref, back_ref, tokens_ref, out_ref):
-    hit, chosen, total, weights, rank = routing(ids_ref[...], scores_ref[...])
-    route = jnp.zeros((EXP, TOKS), f32)
-    for r in range(MOST):
-        route = route + jnp.where(rank == float(r), back_ref[:, r : r + 1], 0.0)
-    route = jnp.where(hit, route / jnp.where(hit, weights, 1.0), 0.0)
-    mixed = jnp.sum(route * chosen, axis=0, keepdims=True) / total
-    score = route_scale / total * (route - mixed)
-    logit = (score * chosen * (1.0 - chosen)).astype(bf16)
-    out_ref[...] = jnp.dot(logit, tokens_ref[...], preferred_element_type=f32)
-
-
-def gate(ids, scores, back, tokens):
+def gate_kernel(x_ref, table_ref, tables_ref, back_ref, tokens_ref, others_ref, out_ref, logit_ref):
+    for k in range(ROW):
+        table = tables_ref[k - 1] if k else table_ref[...]
+        hit, chosen, total, weights, rank = routing(table[EXP:].astype(jnp.int32), table[:EXP])
+        route = jnp.zeros((EXP, TOKS), f32)
+        for r in range(MOST):
+            at = 32 * k + r
+            route = route + jnp.where(rank == float(r), back_ref[:, at : at + 1], 0.0)
+        route = jnp.where(hit, route / jnp.where(hit, weights, 1.0), 0.0)
+        mixed = jnp.sum(route * chosen, axis=0, keepdims=True) / total
+        score = route_scale / total * (route - mixed)
+        logit_ref[:, TOKS * k : TOKS * (k + 1)] = (score * chosen * (1.0 - chosen)).astype(bf16)
+    own = pl.ds(pl.multiple_of(x_ref[0] * (EXP // ROW), EXP // ROW), EXP // ROW)
+    grad = jnp.zeros((EXP // ROW, FEAT), f32)
+    for k in range(ROW):
+        tokens = others_ref[k - 1] if k else tokens_ref[...]
+        grad = grad + jnp.dot(logit_ref[own, TOKS * k : TOKS * (k + 1)], tokens, preferred_element_type=f32)
+    out_ref[...] = grad
+
+
+def gate(x, table, tables, back, tokens, others):
     return pl.pallas_call(
         gate_kernel,
-        out_shape=jax.ShapeDtypeStruct((EXP, FEAT), f32),
-        compiler_params=pltpu.CompilerParams(vmem_limit_bytes=4 * MIB),
-        cost_estimate=pl.CostEstimate(flops=15_000_000, bytes_accessed=560_000, transcendentals=0),
-    )(ids, scores, back, tokens)
+        in_specs=[pl.BlockSpec(memory_space=pltpu.SMEM)] + [pl.BlockSpec(memory_space=pltpu.VMEM)] * 5,
+        out_shape=jax.ShapeDtypeStruct((EXP // ROW, FEAT), f32),
+        scratch_shapes=[pltpu.VMEM((EXP, ROW * TOKS), bf16)],
+        compiler_params=pltpu.CompilerParams(vmem_limit_bytes=6 * MIB),
+        cost_estimate=pl.CostEstimate(flops=30_000_000, bytes_accessed=1_200_000, transcendentals=0),
+    )(x, table, tables, back, tokens, others)
 
 
 def body(grad_out, tokens, scores, expert_ids, hidden_act, down_weight):
-    both = ("ep", "node")
+    both = ("x", "y", "node")
     exchange = functools.partial(lax.all_to_all, split_axis=0, concat_axis=0, tiled=True)
+
+    def gather(v):
+        return jnp.stack([lax.ppermute(v, "x", [(i, (i + k) % ROW) for i in range(ROW)]) for k in range(1, ROW)])
+
     ids, scores = expert_ids.T, scores.T
     recv = exchange(pack(ids, scores, grad_out), both)
     hidden = order(hidden_act[0])
+    table = jnp.concatenate([scores, ids.astype(f32)], axis=0)
+    hidden, far_tokens, far_table = lax.optimization_barrier((hidden, tokens, table))
+    others, tables = gather(far_tokens), gather(far_table)
+    recv, others, tables = lax.optimization_barrier((recv, others, tables))
     part, slot, rows = expert(recv, hidden, down_weight[0].T)
     slot = exchange(slot, "dp")
     summed = lax.psum_scatter(part, "dp", scatter_dimension=0, tiled=True)
@@ -311,7 +342,8 @@
     weight_grad = lax.dot_general(hidden, rows, (((0,), (0,)), ((), ())), preferred_element_type=f32)
     weight_grad = weight_grad.astype(bf16)[None]
     back, weight_grad = lax.optimization_barrier((back, weight_grad))
-    gate_rows = exchange(gate(ids, scores, back, tokens), both)
+    x = lax.axis_index("x").astype(jnp.int32).reshape(1)
+    gate_rows = exchange(gate(x, table, tables, back, tokens, others), ("y", "node"))
     gate_row = jnp.sum(gate_rows, axis=0, keepdims=True)
     gate_row, summed = lax.optimization_barrier((gate_row, summed))
     gate_grad = exchange(jnp.broadcast_to(gate_row, (EXP, FEAT)), both)
@@ -320,17 +352,12 @@
 
 
 def solution(mesh):
+    devices = mesh.devices.reshape(ROW, -1, *mesh.devices.shape[1:])
+    both = ("x", "y", "node")
     return jax.shard_map(
         body,
-        mesh=mesh,
-        in_specs=(
-            P(("ep", "node"), "dp"),
-            P(("ep", "node"), "dp"),
-            P(("ep", "node"), None),
-            P(("ep", "node"), None),
-            P(("ep", "node"), None, None),
-            P(("ep", "node"), None, "dp"),
-        ),
-        out_specs=(P(("ep", "node"), None, "dp"), P(("ep", "node"), "dp", None), P(None, "dp")),
+        mesh=jax.sharding.Mesh(devices, (*both, "dp")),
+        in_specs=(P(both, "dp"), P(both, "dp"), P(both, None), P(both, None), P(both, None, None), P(both, None, "dp")),
+        out_specs=(P(both, None, "dp"), P(both, "dp", None), P(None, "dp")),
         check_vma=False,
     )

time: 166 us -> 164 us (0.988)
  starting transfers between devices: 25.5 us -> 57.4 us
  blocking collectives: 34.7 us -> 11.4 us
  waiting for transfers between devices: 58.4 us -> 47 us
    all_to_all x1, waiting for transfers between devices: 47 us -> 15.8 us  [body(): recv = exchange(pack(ids, scores, grad_out), both)]
    all_to_all x2 -> x1, blocking collectives: 34.7 us -> 11.4 us  [body(): exchange(gate(x, table, tables, back, tokens, others), ('y', 'node'))]
    ppermute x0 -> x6, starting transfers between devices: none -> 17.8 us  [gather(): lax.ppermute(v, 'x', [(i, (i + k) % ROW) for i in range(ROW)])]
    ppermute x0 -> x6, waiting for transfers between devices: none -> 11.6 us  [gather(): lax.ppermute(v, 'x', [(i, (i + k) % ROW) for i in range(ROW)])]
    all_to_all x0 -> x1, starting transfers between devices: none -> 10.1 us  [body(): slot = exchange(slot, 'dp')]
    all_to_all x0 -> x1, waiting for transfers between devices: none -> 7.15 us  [body(): slot = exchange(slot, 'dp')]
    all_to_all x1, starting transfers between devices: 6.2 us -> 10.1 us  [body(): gate_grad = exchange(jnp.broadcast_to(gate_row, (EXP, FEAT)), both)]
    unnamed x15 -> x14, local copies, waits for them, and re-layouts: 6.1 us -> 5.27 us
  transfers between devices with their start and end apart: 4 -> 11, of which waited for: 3 -> 6; matrix products, arithmetic and copies ran while one was open for 7% -> 6% of each run, Pallas kernels for 5% -> 6%
where the time goes in v5:
time: 164 us; the launch traced here: 163 us
  starting transfers between devices  57.4 us (35%)
  waiting for transfers between devices  47 us (29%)
  Pallas kernels  19.9 us (12%)
  between operations  14.3 us (9%)
  blocking collectives  11.4 us (7%)
  local copies, waits for them, and re-layouts  6.15 us (4%)
  matrix products  5.94 us (4%)
    ppermute x6, starting transfers between devices, gather(): lax.ppermute(v, 'x', [(i, (i + k) % ROW) for i in range(ROW)])  17.8 us
    all_to_all x1, waiting for transfers between devices, body(): recv = exchange(pack(ids, scores, grad_out), both)  15.8 us
    all_to_all x1, starting transfers between devices, body(): recv = exchange(pack(ids, scores, grad_out), both)  11.8 us
    ppermute x6, waiting for transfers between devices, gather(): lax.ppermute(v, 'x', [(i, (i + k) % ROW) for i in range(ROW)])  11.6 us
    all_to_all x1, blocking collectives, body(): exchange(gate(x, table, tables, back, tokens, others), ('y', 'node'))  11.4 us
    all_to_all x1, starting transfers between devices, body(): slot = exchange(slot, 'dp')  10.1 us
    all_to_all x1, starting transfers between devices, body(): gate_grad = exchange(jnp.broadcast_to(gate_row, (EXP, FEAT)), both)  10.1 us
    all_to_all x1, waiting for transfers between devices, body(): gate_grad = exchange(jnp.broadcast_to(gate_row, (EXP, FEAT)), both)  9.19 us
  transfers between devices with their start and end apart: 11, of which 6 were waited for; matrix products, arithmetic and copies ran while one was open for 6% of the time, Pallas kernels for 6%

profile of v5, /device:TPU:1, one launch (start us, length us, event | category | flops | bytes accessed | tf_op | source)
XLA Modules:
  0.0 163.1 jit_solution(13219752840418862604)
XLA Ops:
  7.2 2.9 %shard_map.85 = bf16[64,144,128]{2,1,0:T(8,128)(2,1)} custom-call(s32[8,128]{1,0:T(8,128)} %bitcast.41, f32[64,128]{1,0:T(8,128)} %bitcast.36, bf16[128,896]{1,0:T(8,128)(2,1)} %grad_any.1), custom_call_target="tpu_custom_call" | custom-call | flops 500000000 | bytes 2700000 | tf_op jit(solution)/shard_map/pallas_call | solution.py:99
  10.1 11.8 %all-to-all-start = ((bf16[64,144,128]{2,1,0:T(8,128)(2,1)}), bf16[64,144,128]{2,1,0:T(8,128)(2,1)}, u32[]{:S(2)}, u32[]{:S(2)}) async-start(bf16[64,144,128]{2,1,0:T(8,128)(2,1)} %shard_map.85), calls=%async_computation | async-start | bytes 4718592 | tf_op jit(solution)/shard_map/all_to_all | solution.py:332
  22.0 6.7 %shard_map.86.hidden_any = bf16[1280,1024]{1,0:T(8,128)(2,1)} custom-call(bf16[1280,1024]{1,0:T(8,128)(2,1)} %bitcast.30), custom_call_target="tpu_custom_call" | custom-call | flops 500000000 | bytes 5300000 | tf_op jit(solution)/shard_map/pallas_call | solution.py:129
  28.7 3.4 %collective-permute-start = (bf16[128,896]{1,0:T(8,128)(2,1)S(1)}, bf16[128,896]{1,0:T(8,128)(2,1)S(1)}, u32[]{:S(2)}, u32[]{:S(2)}) collective-permute-start(bf16[128,896]{1,0:T(8,128)(2,1)S(1)} %copy-done.1), channel_id=1, source_target_pairs={{0,128},{128,256},{256,384},{384,0},{1,129},{129,257},{257,385},{3... | collective-permute-start | bytes 688136 | tf_op jit(solution)/shard_map/ppermute | solution.py:329
  32.1 4.5 %collective-permute-start.1 = (bf16[128,896]{1,0:T(8,128)(2,1)S(1)}, bf16[128,896]{1,0:T(8,128)(2,1)S(1)}, u32[]{:S(2)}, u32[]{:S(2)}) collective-permute-start(bf16[128,896]{1,0:T(8,128)(2,1)S(1)} %copy-done.1), channel_id=1, source_target_pairs={{0,256},{128,384},{256,0},{384,128},{1,257},{129,385},{257,1},{385... | collective-permute-start | bytes 688136 | tf_op jit(solution)/shard_map/ppermute | solution.py:329
  36.6 3.0 %collective-permute-start.2 = (bf16[128,896]{1,0:T(8,128)(2,1)S(1)}, bf16[128,896]{1,0:T(8,128)(2,1)S(1)}, u32[]{:S(2)}, u32[]{:S(2)}) collective-permute-start(bf16[128,896]{1,0:T(8,128)(2,1)S(1)} %copy-done.1), channel_id=1, source_target_pairs={{0,384},{128,0},{256,128},{384,256},{1,385},{129,1},{257,129},{385... | collective-permute-start | bytes 688136 | tf_op jit(solution)/shard_map/ppermute | solution.py:329
  39.6 2.3 %collective-permute-start.3 = (f32[72,128]{1,0:T(8,128)S(1)}, f32[72,128]{1,0:T(8,128)S(1)}, u32[]{:S(2)}, u32[]{:S(2)}) collective-permute-start(f32[72,128]{1,0:T(8,128)S(1)} %pad_maximum_fusion.2.table_ref), channel_id=1, source_target_pairs={{0,128},{128,256},{256,384},{384,0},{1,129},{129,257},{257,385},{3... | collective-permute-start | bytes 110600 | tf_op jit(solution)/shard_map/ppermute | solution.py:329
  41.9 2.7 %collective-permute-start.4 = (f32[72,128]{1,0:T(8,128)S(1)}, f32[72,128]{1,0:T(8,128)S(1)}, u32[]{:S(2)}, u32[]{:S(2)}) collective-permute-start(f32[72,128]{1,0:T(8,128)S(1)} %pad_maximum_fusion.2.table_ref), channel_id=1, source_target_pairs={{0,256},{128,384},{256,0},{384,128},{1,257},{129,385},{257,1},{385... | collective-permute-start | bytes 110600 | tf_op jit(solution)/shard_map/ppermute | solution.py:329
  44.6 10.0 %collective-permute-done.3 = f32[72,128]{1,0:T(8,128)S(1)} collective-permute-done((f32[72,128]{1,0:T(8,128)S(1)}, f32[72,128]{1,0:T(8,128)S(1)}, u32[]{:S(2)}, u32[]{:S(2)}) %collective-permute-start.3) | collective-permute-done | bytes 36896 | tf_op jit(solution)/shard_map/ppermute | solution.py:329
  54.6 1.9 %collective-permute-start.5 = (f32[72,128]{1,0:T(8,128)S(1)}, f32[72,128]{1,0:T(8,128)S(1)}, u32[]{:S(2)}, u32[]{:S(2)}) collective-permute-start(f32[72,128]{1,0:T(8,128)S(1)} %pad_maximum_fusion.2.table_ref), channel_id=1, source_target_pairs={{0,384},{128,0},{256,128},{384,256},{1,385},{129,1},{257,129},{385... | collective-permute-start | bytes 110600 | tf_op jit(solution)/shard_map/ppermute | solution.py:329
  56.5 2.9 %copy.10 = bf16[1,1024,896]{1,2,0:T(8,128)(2,1)S(1)} copy(bf16[1,1024,896]{2,1,0:T(8,128)(2,1)} %param.11) | data formatting | bytes 3670016 | tf_op args[5]
  59.4 1.6 collective-permute-done.5
  61.7 1.0 pad_maximum_fusion.others_ref
  62.8 15.8 %all-to-all-done.recv_any = bf16[64,144,128]{2,1,0:T(8,128)(2,1)} async-done(((bf16[64,144,128]{2,1,0:T(8,128)(2,1)}), bf16[64,144,128]{2,1,0:T(8,128)(2,1)}, u32[]{:S(2)}, u32[]{:S(2)}) %all-to-all-start) | async-done | bytes 2359328 | tf_op jit(solution)/shard_map/all_to_all | solution.py:332
  78.5 7.3 %shard_map.87 = (bf16[1280,1024]{1,0:T(8,128)(2,1)}, f32[8,16,128]{2,1,0:T(8,128)}, bf16[1280,896]{1,0:T(8,128)(2,1)}) custom-call(bf16[64,144,128]{2,1,0:T(8,128)(2,1)} %all-to-all-done.recv_any, bf16[1280,1024]{1,0:T(8,128)(2,1)} %shard_map.86.hidden_any, bf16[896,1024]{1,0:T(8,128)(2,1)S(1)} %bitcast.27), custom_call_target="tpu_custom_call" | custom-call | flops 2400000000 | bytes 11000000 | tf_op jit(solution)/shard_map/pallas_call | solution.py:240
  85.8 10.1 %all-to-all-start.1 = ((f32[8,16,128]{2,1,0:T(8,128)}), f32[8,16,128]{2,1,0:T(8,128)S(1)}, u32[]{:S(2)}, u32[]{:S(2)}) async-start(f32[8,16,128]{2,1,0:T(8,128)} %get-tuple-element.20), calls=%async_computation.1 | async-start | bytes 131072 | tf_op jit(solution)/shard_map/all_to_all | solution.py:339
  96.0 7.2 %all-to-all-done.1.slot_ref = f32[8,16,128]{2,1,0:T(8,128)S(1)} async-done(((f32[8,16,128]{2,1,0:T(8,128)}), f32[8,16,128]{2,1,0:T(8,128)S(1)}, u32[]{:S(2)}, u32[]{:S(2)}) %all-to-all-start.1) | async-done | bytes 65568 | tf_op jit(solution)/shard_map/all_to_all | solution.py:339
  104.0 7.5 %all-to-all-start.2 = ((f32[64,1,128]{2,1,0:T(1,128)}), f32[64,1,128]{2,1,0:T(1,128)S(1)}, u32[]{:S(2)}, u32[]{:S(2)}) async-start(f32[64,1,128]{2,1,0:T(1,128)} %bitcast.12), calls=%async_computation.2 | async-start | bytes 65536 | tf_op jit(solution)/shard_map/all_to_all | solution.py:341
  111.5 5.9 %convert_bitcast_fusion = bf16[1,1024,896]{2,1,0:T(8,128)(2,1)} fusion(bf16[1280,1024]{1,0:T(8,128)(2,1)} %shard_map.86.hidden_any, bf16[1280,896]{1,0:T(8,128)(2,1)S(1)} %copy-done.5), kind=kOutput, calls=%fused_computation | convolution fusion | flops 2349727744 | bytes 6750208 | tf_op jit(solution)/shard_map/dot_general | solution.py:342
  117.4 3.3 %all-to-all-done.2 = f32[64,1,128]{2,1,0:T(1,128)S(1)} async-done(((f32[64,1,128]{2,1,0:T(1,128)}), f32[64,1,128]{2,1,0:T(1,128)S(1)}, u32[]{:S(2)}, u32[]{:S(2)}) %all-to-all-start.2) | async-done | bytes 32800 | tf_op jit(solution)/shard_map/all_to_all | solution.py:341
  120.7 1.2 shard_map.89
  122.0 11.4 %all_to_all.40 = f32[16,1,896]{2,1,0:T(1,128)S(1)} all-to-all(f32[16,1,896]{2,1,0:T(1,128)S(1)} %copy.12), channel_id=1, replica_groups=mesh['x'=4,'y'=8,'node'=2,'dp'=8] {'y','node'}, dimensions={0} | all-to-all | bytes 114688 | tf_op jit(solution)/shard_map/all_to_all | solution.py:346
  134.3 10.1 %all-to-all-start.4 = ((f32[64,1,896]{2,1,0:T(1,128)}), f32[64,1,896]{2,1,0:T(1,128)S(1)}, u32[]{:S(2)}, u32[]{:S(2)}) async-start(f32[64,1,896]{2,1,0:T(1,128)} %broadcast_in_dim.17), calls=%async_computation.5 | async-start | bytes 458752 | tf_op jit(solution)/shard_map/all_to_all | solution.py:349
  146.4 9.2 %all-to-all-done.4 = f32[64,1,896]{2,1,0:T(1,128)S(1)} async-done(((f32[64,1,896]{2,1,0:T(1,128)}), f32[64,1,896]{2,1,0:T(1,128)S(1)}, u32[]{:S(2)}, u32[]{:S(2)}) %all-to-all-start.4) | async-done | bytes 229408 | tf_op jit(solution)/shard_map/all_to_all | solution.py:349
  (30 shorter events, 5.2 us)
Async XLA Ops:
  10.1 68.4 %all-to-all-start = ((bf16[64,144,128]{2,1,0:T(8,128)(2,1)}), bf16[64,144,128]{2,1,0:T(8,128)(2,1)}, u32[]{:S(2)}, u32[]{:S(2)}) async-start(bf16[64,144,128]{2,1,0:T(8,128)(2,1)} %shard_map.85), calls=%async_computation | async-start | bytes 4718592 | tf_op jit(solution)/shard_map/all_to_all | solution.py:332
  21.9 111.6 %reduce-scatter.2.cloned.1.call-start = ((), (), s32[]{:S(2)}) async-start(), calls=%async_computation.6 | async-start | bytes 2949120 | tf_op jit(solution)/shard_map/reduce_scatter | solution.py:340
  21.9 6.7 %copy-start.4 = (s32[128,8]{0,1:T(8,128)S(1)}, s32[128,8]{0,1:T(8,128)}, u32[]{:S(2)}) copy-start(s32[128,8]{0,1:T(8,128)} %param.9) | copy-start | bytes 12292
  22.0 6.7 %copy-start.3 = (f32[128,64]{0,1:T(8,128)S(1)}, f32[128,64]{0,1:T(8,128)}, u32[]{:S(2)}) copy-start(f32[128,64]{0,1:T(8,128)} %param.8) | copy-start | bytes 98308
  22.0 6.7 %copy-start.1 = (bf16[128,896]{1,0:T(8,128)(2,1)S(1)}, bf16[128,896]{1,0:T(8,128)(2,1)}, u32[]{:S(2)}) copy-start(bf16[128,896]{1,0:T(8,128)(2,1)} %tokens_ref.1) | copy-start | bytes 688132
  28.7 32.3 %collective-permute-start = (bf16[128,896]{1,0:T(8,128)(2,1)S(1)}, bf16[128,896]{1,0:T(8,128)(2,1)S(1)}, u32[]{:S(2)}, u32[]{:S(2)}) collective-permute-start(bf16[128,896]{1,0:T(8,128)(2,1)S(1)} %copy-done.1), channel_id=1, source_target_pairs={{0,128},{128,256},{256,384},{384,0},{1,129},{129,257},{257,385},{3... | collective-permute-start | bytes 688136 | tf_op jit(solution)/shard_map/ppermute | solution.py:329
  32.1 28.9 %collective-permute-start.1 = (bf16[128,896]{1,0:T(8,128)(2,1)S(1)}, bf16[128,896]{1,0:T(8,128)(2,1)S(1)}, u32[]{:S(2)}, u32[]{:S(2)}) collective-permute-start(bf16[128,896]{1,0:T(8,128)(2,1)S(1)} %copy-done.1), channel_id=1, source_target_pairs={{0,256},{128,384},{256,0},{384,128},{1,257},{129,385},{257,1},{385... | collective-permute-start | bytes 688136 | tf_op jit(solution)/shard_map/ppermute | solution.py:329
  36.6 24.4 %collective-permute-start.2 = (bf16[128,896]{1,0:T(8,128)(2,1)S(1)}, bf16[128,896]{1,0:T(8,128)(2,1)S(1)}, u32[]{:S(2)}, u32[]{:S(2)}) collective-permute-start(bf16[128,896]{1,0:T(8,128)(2,1)S(1)} %copy-done.1), channel_id=1, source_target_pairs={{0,384},{128,0},{256,128},{384,256},{1,385},{129,1},{257,129},{385... | collective-permute-start | bytes 688136 | tf_op jit(solution)/shard_map/ppermute | solution.py:329
  39.6 15.0 %collective-permute-start.3 = (f32[72,128]{1,0:T(8,128)S(1)}, f32[72,128]{1,0:T(8,128)S(1)}, u32[]{:S(2)}, u32[]{:S(2)}) collective-permute-start(f32[72,128]{1,0:T(8,128)S(1)} %pad_maximum_fusion.2.table_ref), channel_id=1, source_target_pairs={{0,128},{128,256},{256,384},{384,0},{1,129},{129,257},{257,385},{3... | collective-permute-start | bytes 110600 | tf_op jit(solution)/shard_map/ppermute | solution.py:329
  41.9 17.5 %collective-permute-start.4 = (f32[72,128]{1,0:T(8,128)S(1)}, f32[72,128]{1,0:T(8,128)S(1)}, u32[]{:S(2)}, u32[]{:S(2)}) collective-permute-start(f32[72,128]{1,0:T(8,128)S(1)} %pad_maximum_fusion.2.table_ref), channel_id=1, source_target_pairs={{0,256},{128,384},{256,0},{384,128},{1,257},{129,385},{257,1},{385... | collective-permute-start | bytes 110600 | tf_op jit(solution)/shard_map/ppermute | solution.py:329
  54.6 6.4 %collective-permute-start.5 = (f32[72,128]{1,0:T(8,128)S(1)}, f32[72,128]{1,0:T(8,128)S(1)}, u32[]{:S(2)}, u32[]{:S(2)}) collective-permute-start(f32[72,128]{1,0:T(8,128)S(1)} %pad_maximum_fusion.2.table_ref), channel_id=1, source_target_pairs={{0,384},{128,0},{256,128},{384,256},{1,385},{129,1},{257,129},{385... | collective-permute-start | bytes 110600 | tf_op jit(solution)/shard_map/ppermute | solution.py:329
  61.0 0.7 copy-start.2
  85.8 25.7 %copy-start.5 = (bf16[1280,896]{1,0:T(8,128)(2,1)S(1)}, bf16[1280,896]{1,0:T(8,128)(2,1)}, u32[]{:S(2)}) copy-start(bf16[1280,896]{1,0:T(8,128)(2,1)} %get-tuple-element.21) | copy-start | bytes 6881284
  85.8 17.3 %all-to-all-start.1 = ((f32[8,16,128]{2,1,0:T(8,128)}), f32[8,16,128]{2,1,0:T(8,128)S(1)}, u32[]{:S(2)}, u32[]{:S(2)}) async-start(f32[8,16,128]{2,1,0:T(8,128)} %get-tuple-element.20), calls=%async_computation.1 | async-start | bytes 131072 | tf_op jit(solution)/shard_map/all_to_all | solution.py:339
  104.0 16.7 %all-to-all-start.2 = ((f32[64,1,128]{2,1,0:T(1,128)}), f32[64,1,128]{2,1,0:T(1,128)S(1)}, u32[]{:S(2)}, u32[]{:S(2)}) async-start(f32[64,1,128]{2,1,0:T(1,128)} %bitcast.12), calls=%async_computation.2 | async-start | bytes 65536 | tf_op jit(solution)/shard_map/all_to_all | solution.py:341
  134.3 21.3 %all-to-all-start.4 = ((f32[64,1,896]{2,1,0:T(1,128)}), f32[64,1,896]{2,1,0:T(1,128)S(1)}, u32[]{:S(2)}, u32[]{:S(2)}) async-start(f32[64,1,896]{2,1,0:T(1,128)} %broadcast_in_dim.17), calls=%async_computation.5 | async-start | bytes 458752 | tf_op jit(solution)/shard_map/all_to_all | solution.py:349
  144.4 1.0 copy-start
Sparse Core Ops, SparseCore 0:
  85.9 43.6 reduce-scatter.1

commit v6 on v5

--- a/solution.py
+++ b/solution.py
@@ -116,12 +116,15 @@
     )(ids, scores, grad)
 
 
+def source_order(i):
+    e = i - 8 * MAIN
+    return jnp.where(i < 8 * MAIN, i // MAIN * MOST + i % MAIN, e // EXTRA * MOST + MAIN + e % EXTRA)
+
+
 def order_kernel(x_ref, y_ref):
     i = lax.broadcasted_iota(jnp.int32, (BLOCK, BLOCK), 0)
     j = lax.broadcasted_iota(jnp.int32, (BLOCK, BLOCK), 1)
-    e = i - 8 * MAIN
-    origin = jnp.where(i < 8 * MAIN, i // MAIN * MOST + i % MAIN, e // EXTRA * MOST + MAIN + e % EXTRA)
-    move = jnp.where(origin == j, 1.0, 0.0).astype(bf16)
+    move = jnp.where(source_order(i) == j, 1.0, 0.0).astype(bf16)
     y_ref[...] = jnp.dot(move, x_ref[...], preferred_element_type=f32).astype(bf16)
 
 
@@ -136,24 +139,6 @@
     )(hidden)
 
 
-def restore_kernel(x_ref, y_ref):
-    j = lax.broadcasted_iota(jnp.int32, (BLOCK, BLOCK), 0)
-    i = lax.broadcasted_iota(jnp.int32, (BLOCK, BLOCK), 1)
-    e = i - 8 * MAIN
-    origin = jnp.where(i < 8 * MAIN, i // MAIN * MOST + i % MAIN, e // EXTRA * MOST + MAIN + e % EXTRA)
-    move = jnp.where(origin == j, 1.0, 0.0).astype(bf16)
-    y_ref[...] = jnp.dot(move, x_ref[...], preferred_element_type=f32).astype(bf16)
-
-
-def restore(x):
-    return pl.pallas_call(
-        restore_kernel,
-        out_shape=jax.ShapeDtypeStruct((BLOCK, HID), bf16),
-        compiler_params=pltpu.CompilerParams(vmem_limit_bytes=4 * MIB),
-        cost_estimate=pl.CostEstimate(flops=60_000_000, bytes_accessed=660_000, transcendentals=0),
-    )(x)
-
-
 PARTS = 2
 CHUNK = SLOTS // PARTS
 PAIR = EXP // PARTS
@@ -161,8 +146,8 @@
 
 
 def expert_kernel(
-    recv_any, hidden_any, down_any, part_any, slot_ref, rows_any,
-    recv_ref, hidden_ref, down_ref, part_ref, rows_ref, in_sems, out_sems,
+    recv_any, hidden_any, down_ref, part_any, slot_ref, rows_any,
+    recv_ref, hidden_ref, part_ref, rows_ref, in_sems, out_sems,
 ):
     come, saved, stores = [], [], []
     for c in range(PARTS):
@@ -176,22 +161,19 @@
                 pltpu.make_async_copy(part_ref.at[at], part_any.at[at], out_sems.at[1, c]),
             ]
         )
-    weights = pltpu.make_async_copy(down_any, down_ref, in_sems.at[2, 0])
-    come[0].start()
-    weights.start()
     for c in range(PARTS):
-        if c:
-            come[c].start()
+        come[c].start()
         saved[c].start()
 
     i = lax.broadcasted_iota(jnp.int32, (LANES, LANES), 0)
     j = lax.broadcasted_iota(jnp.int32, (LANES, LANES), 1)
     q, source, r = i // 32, i % 32 // EXTRA, i % EXTRA
     move = jnp.where(source * MAIN + q * EXTRA + r == j, 1.0, 0.0).astype(bf16)
+    j = lax.broadcasted_iota(jnp.int32, (BLOCK, BLOCK), 0)
+    back = jnp.where(source_order(lax.broadcasted_iota(jnp.int32, (BLOCK, BLOCK), 1)) == j, 1.0, 0.0).astype(bf16)
     ones = jnp.ones((8, LANES), bf16)
     slot_ref[...] = jnp.zeros_like(slot_ref)
     for c in range(PARTS):
-        at = slice(c * CHUNK, (c + 1) * CHUNK)
         come[c].wait()
         for g in range(c * PAIR // 8, (c + 1) * PAIR // 8):
             some = slice(8 * g, 8 * g + 8)
@@ -210,13 +192,15 @@
                             32 * q : 32 * (q + 1)
                         ]
         stores[c][0].start()
-        if c == 0:
-            weights.wait()
         saved[c].wait()
-        part = jnp.dot(rows_ref[at, :], down_ref[...], preferred_element_type=f32)
-        both = part * hidden_ref[at, :].astype(f32)
-        rest = sum(both[:, LANES * q : LANES * (q + 1)] for q in range(HID // LANES))
-        part_ref[at, :] = part.astype(bf16)
+        terms = []
+        for g in range(CHUNK // BLOCK * c, CHUNK // BLOCK * (c + 1)):
+            line = slice(BLOCK * g, BLOCK * (g + 1))
+            part = jnp.dot(rows_ref[line, :], down_ref[...], preferred_element_type=f32)
+            both = part * hidden_ref[line, :].astype(f32)
+            terms.append(sum(both[:, LANES * q : LANES * (q + 1)] for q in range(HID // LANES)))
+            part_ref[line, :] = jnp.dot(back, part.astype(bf16), preferred_element_type=f32).astype(bf16)
+        rest = jnp.concatenate(terms, axis=0)
         stores[c][1].start()
         sums = jnp.zeros((8, CHUNK), f32)
         for _ in range(3):
@@ -239,7 +223,7 @@
     any_space = pl.BlockSpec(memory_space=pl.ANY)
     return pl.pallas_call(
         expert_kernel,
-        in_specs=[any_space] * 3,
+        in_specs=[any_space, any_space, pl.BlockSpec(memory_space=pltpu.VMEM)],
         out_specs=[any_space, pl.BlockSpec(memory_space=pltpu.VMEM), any_space],
         out_shape=[
             jax.ShapeDtypeStruct((SLOTS, HID), bf16),
@@ -249,10 +233,9 @@
         scratch_shapes=[
             pltpu.VMEM((EXP, PIECE, LANES), bf16),
             pltpu.VMEM((SLOTS, HID), bf16),
-            pltpu.VMEM((FEAT, HID), bf16),
             pltpu.VMEM((SLOTS, HID), bf16),
             pltpu.VMEM((SLOTS, FEAT), bf16),
-            pltpu.SemaphoreType.DMA((3, PARTS)),
+            pltpu.SemaphoreType.DMA((2, PARTS)),
             pltpu.SemaphoreType.DMA((2, PARTS)),
         ],
         compiler_params=pltpu.CompilerParams(vmem_limit_bytes=EXPERT_LIMIT * MIB),
@@ -345,10 +328,8 @@
     x = lax.axis_index("x").astype(jnp.int32).reshape(1)
     gate_rows = exchange(gate(x, table, tables, back, tokens, others), ("y", "node"))
     gate_row = jnp.sum(gate_rows, axis=0, keepdims=True)
-    gate_row, summed = lax.optimization_barrier((gate_row, summed))
     gate_grad = exchange(jnp.broadcast_to(gate_row, (EXP, FEAT)), both)
-    hidden_grad = restore(summed)[None]
-    return (weight_grad, hidden_grad, gate_grad)
+    return (weight_grad, summed[None], gate_grad)
 
 
 def solution(mesh):

time: 164 us -> 160 us (0.976)
  blocking collectives: 11.4 us -> 28 us
  starting transfers between devices: 57.4 us -> 47.3 us
  waiting for transfers between devices: 47 us -> 37.7 us
  local copies, waits for them, and re-layouts: 6.15 us -> 4.49 us
    all_to_all x0 -> x1, blocking collectives: none -> 16.6 us  [body(): gate_grad = exchange(jnp.broadcast_to(gate_row, (EXP, FEAT)), both)]
    all_to_all x1 -> x0, starting transfers between devices: 10.1 us -> none  [body(): gate_grad = exchange(jnp.broadcast_to(gate_row, (EXP, FEAT)), both)]
    all_to_all x1 -> x0, waiting for transfers between devices: 9.19 us -> none  [body(): gate_grad = exchange(jnp.broadcast_to(gate_row, (EXP, FEAT)), both)]
    unnamed x14 -> x12, local copies, waits for them, and re-layouts: 5.27 us -> 4.3 us
    pallas_call x2 -> x1, Pallas kernels: 8.22 us -> 8.6 us  [expert(): pl.pallas_call(expert_kernel, in_specs=[any_space, any_space, pl.BlockSpe...]
  transfers between devices with their start and end apart: 11 -> 10, of which waited for: 6 -> 5; matrix products, arithmetic and copies ran while one was open for 6% -> 7% of each run, Pallas kernels for 6% -> 5%
where the time goes in v6:
time: 160 us; the launch traced here: 159 us
  starting transfers between devices  47.3 us (30%)
  waiting for transfers between devices  37.7 us (24%)
  blocking collectives  28 us (18%)
  Pallas kernels  20.3 us (13%)
  between operations  14.2 us (9%)
  matrix products  5.94 us (4%)
  local copies, waits for them, and re-layouts  4.49 us (3%)
    ppermute x6, starting transfers between devices, gather(): lax.ppermute(v, 'x', [(i, (i + k) % ROW) for i in range(ROW)])  17.8 us
    all_to_all x1, blocking collectives, body(): gate_grad = exchange(jnp.broadcast_to(gate_row, (EXP, FEAT)), both)  16.6 us
    all_to_all x1, waiting for transfers between devices, body(): recv = exchange(pack(ids, scores, grad_out), both)  15.8 us
    all_to_all x1, starting transfers between devices, body(): recv = exchange(pack(ids, scores, grad_out), both)  11.8 us
    ppermute x6, waiting for transfers between devices, gather(): lax.ppermute(v, 'x', [(i, (i + k) % ROW) for i in range(ROW)])  11.5 us
    all_to_all x1, blocking collectives, body(): exchange(gate(x, table, tables, back, tokens, others), ('y', 'node'))  11.4 us
    all_to_all x1, starting transfers between devices, body(): slot = exchange(slot, 'dp')  10.1 us
    pallas_call x1, Pallas kernels, expert(): pl.pallas_call(expert_kernel, in_specs=[any_space, any_space, pl.BlockSpe...  8.6 us
  transfers between devices with their start and end apart: 10, of which 5 were waited for; matrix products, arithmetic and copies ran while one was open for 7% of the time, Pallas kernels for 5%

profile of v6, /device:TPU:1, one launch (start us, length us, event | category | flops | bytes accessed | tf_op | source)
XLA Modules:
  0.0 159.1 jit_solution(1377050966918180729)
XLA Ops:
  7.2 2.9 %shard_map.85 = bf16[64,144,128]{2,1,0:T(8,128)(2,1)} custom-call(s32[8,128]{1,0:T(8,128)} %bitcast.40, f32[64,128]{1,0:T(8,128)} %bitcast.35, bf16[128,896]{1,0:T(8,128)(2,1)} %grad_any.1), custom_call_target="tpu_custom_call" | custom-call | flops 500000000 | bytes 2700000 | tf_op jit(solution)/shard_map/pallas_call | solution.py:99
  10.1 11.8 %all-to-all-start = ((bf16[64,144,128]{2,1,0:T(8,128)(2,1)}), bf16[64,144,128]{2,1,0:T(8,128)(2,1)}, u32[]{:S(2)}, u32[]{:S(2)}) async-start(bf16[64,144,128]{2,1,0:T(8,128)(2,1)} %shard_map.85), calls=%async_computation | async-start | bytes 4718592 | tf_op jit(solution)/shard_map/all_to_all | solution.py:315
  22.0 6.7 %shard_map.86.hidden_any = bf16[1280,1024]{1,0:T(8,128)(2,1)} custom-call(bf16[1280,1024]{1,0:T(8,128)(2,1)} %bitcast.30), custom_call_target="tpu_custom_call" | custom-call | flops 500000000 | bytes 5300000 | tf_op jit(solution)/shard_map/pallas_call | solution.py:132
  28.7 3.4 %collective-permute-start = (bf16[128,896]{1,0:T(8,128)(2,1)S(1)}, bf16[128,896]{1,0:T(8,128)(2,1)S(1)}, u32[]{:S(2)}, u32[]{:S(2)}) collective-permute-start(bf16[128,896]{1,0:T(8,128)(2,1)S(1)} %copy-done), channel_id=1, source_target_pairs={{0,128},{128,256},{256,384},{384,0},{1,129},{129,257},{257,385},{3... | collective-permute-start | bytes 688136 | tf_op jit(solution)/shard_map/ppermute | solution.py:312
  32.1 4.5 %collective-permute-start.1 = (bf16[128,896]{1,0:T(8,128)(2,1)S(1)}, bf16[128,896]{1,0:T(8,128)(2,1)S(1)}, u32[]{:S(2)}, u32[]{:S(2)}) collective-permute-start(bf16[128,896]{1,0:T(8,128)(2,1)S(1)} %copy-done), channel_id=1, source_target_pairs={{0,256},{128,384},{256,0},{384,128},{1,257},{129,385},{257,1},{385... | collective-permute-start | bytes 688136 | tf_op jit(solution)/shard_map/ppermute | solution.py:312
  36.6 3.0 %collective-permute-start.2 = (bf16[128,896]{1,0:T(8,128)(2,1)S(1)}, bf16[128,896]{1,0:T(8,128)(2,1)S(1)}, u32[]{:S(2)}, u32[]{:S(2)}) collective-permute-start(bf16[128,896]{1,0:T(8,128)(2,1)S(1)} %copy-done), channel_id=1, source_target_pairs={{0,384},{128,0},{256,128},{384,256},{1,385},{129,1},{257,129},{385... | collective-permute-start | bytes 688136 | tf_op jit(solution)/shard_map/ppermute | solution.py:312
  39.6 2.3 %collective-permute-start.3 = (f32[72,128]{1,0:T(8,128)S(1)}, f32[72,128]{1,0:T(8,128)S(1)}, u32[]{:S(2)}, u32[]{:S(2)}) collective-permute-start(f32[72,128]{1,0:T(8,128)S(1)} %pad_maximum_fusion.2.table_ref), channel_id=1, source_target_pairs={{0,128},{128,256},{256,384},{384,0},{1,129},{129,257},{257,385},{3... | collective-permute-start | bytes 110600 | tf_op jit(solution)/shard_map/ppermute | solution.py:312
  41.9 2.7 %collective-permute-start.4 = (f32[72,128]{1,0:T(8,128)S(1)}, f32[72,128]{1,0:T(8,128)S(1)}, u32[]{:S(2)}, u32[]{:S(2)}) collective-permute-start(f32[72,128]{1,0:T(8,128)S(1)} %pad_maximum_fusion.2.table_ref), channel_id=1, source_target_pairs={{0,256},{128,384},{256,0},{384,128},{1,257},{129,385},{257,1},{385... | collective-permute-start | bytes 110600 | tf_op jit(solution)/shard_map/ppermute | solution.py:312
  44.6 10.0 %collective-permute-done.3 = f32[72,128]{1,0:T(8,128)S(1)} collective-permute-done((f32[72,128]{1,0:T(8,128)S(1)}, f32[72,128]{1,0:T(8,128)S(1)}, u32[]{:S(2)}, u32[]{:S(2)}) %collective-permute-start.3) | collective-permute-done | bytes 36896 | tf_op jit(solution)/shard_map/ppermute | solution.py:312
  54.6 1.9 %collective-permute-start.5 = (f32[72,128]{1,0:T(8,128)S(1)}, f32[72,128]{1,0:T(8,128)S(1)}, u32[]{:S(2)}, u32[]{:S(2)}) collective-permute-start(f32[72,128]{1,0:T(8,128)S(1)} %pad_maximum_fusion.2.table_ref), channel_id=1, source_target_pairs={{0,384},{128,0},{256,128},{384,256},{1,385},{129,1},{257,129},{385... | collective-permute-start | bytes 110600 | tf_op jit(solution)/shard_map/ppermute | solution.py:312
  56.5 2.9 %copy.10 = bf16[1,1024,896]{1,2,0:T(8,128)(2,1)S(1)} copy(bf16[1,1024,896]{2,1,0:T(8,128)(2,1)} %param.11) | data formatting | bytes 3670016 | tf_op args[5]
  59.4 1.6 collective-permute-done.5
  61.7 1.0 pad_maximum_fusion.others_ref
  62.8 15.8 %all-to-all-done.recv_any = bf16[64,144,128]{2,1,0:T(8,128)(2,1)} async-done(((bf16[64,144,128]{2,1,0:T(8,128)(2,1)}), bf16[64,144,128]{2,1,0:T(8,128)(2,1)}, u32[]{:S(2)}, u32[]{:S(2)}) %all-to-all-start) | async-done | bytes 2359328 | tf_op jit(solution)/shard_map/all_to_all | solution.py:315
  78.5 8.6 %shard_map.87 = (bf16[1280,1024]{1,0:T(8,128)(2,1)}, f32[8,16,128]{2,1,0:T(8,128)}, bf16[1280,896]{1,0:T(8,128)(2,1)}) custom-call(bf16[64,144,128]{2,1,0:T(8,128)(2,1)} %all-to-all-done.recv_any, bf16[1280,1024]{1,0:T(8,128)(2,1)} %shard_map.86.hidden_any, bf16[896,1024]{1,0:T(8,128)(2,1)S(1)} %bitcast.27), custom_call_target="tpu_custom_call" | custom-call | flops 2400000000 | bytes 11000000 | tf_op jit(solution)/shard_map/pallas_call | solution.py:224
  87.2 10.1 %all-to-all-start.1 = ((f32[8,16,128]{2,1,0:T(8,128)}), f32[8,16,128]{2,1,0:T(8,128)S(1)}, u32[]{:S(2)}, u32[]{:S(2)}) async-start(f32[8,16,128]{2,1,0:T(8,128)} %get-tuple-element.18), calls=%async_computation.1 | async-start | bytes 131072 | tf_op jit(solution)/shard_map/all_to_all | solution.py:322
  97.3 7.2 %all-to-all-done.1.slot_ref = f32[8,16,128]{2,1,0:T(8,128)S(1)} async-done(((f32[8,16,128]{2,1,0:T(8,128)}), f32[8,16,128]{2,1,0:T(8,128)S(1)}, u32[]{:S(2)}, u32[]{:S(2)}) %all-to-all-start.1) | async-done | bytes 65568 | tf_op jit(solution)/shard_map/all_to_all | solution.py:322
  104.5 0.9 shard_map.88
  105.3 7.5 %all-to-all-start.2 = ((f32[64,1,128]{2,1,0:T(1,128)}), f32[64,1,128]{2,1,0:T(1,128)S(1)}, u32[]{:S(2)}, u32[]{:S(2)}) async-start(f32[64,1,128]{2,1,0:T(1,128)} %bitcast.12), calls=%async_computation.2 | async-start | bytes 65536 | tf_op jit(solution)/shard_map/all_to_all | solution.py:324
  112.8 5.9 %convert_bitcast_fusion = bf16[1,1024,896]{2,1,0:T(8,128)(2,1)} fusion(bf16[1280,1024]{1,0:T(8,128)(2,1)} %shard_map.86.hidden_any, bf16[1280,896]{1,0:T(8,128)(2,1)S(1)} %copy-done.4), kind=kOutput, calls=%fused_computation | convolution fusion | flops 2349727744 | bytes 6750208 | tf_op jit(solution)/shard_map/dot_general | solution.py:325
  118.8 3.3 %all-to-all-done.2 = f32[64,1,128]{2,1,0:T(1,128)S(1)} async-done(((f32[64,1,128]{2,1,0:T(1,128)}), f32[64,1,128]{2,1,0:T(1,128)S(1)}, u32[]{:S(2)}, u32[]{:S(2)}) %all-to-all-start.2) | async-done | bytes 32800 | tf_op jit(solution)/shard_map/all_to_all | solution.py:324
  122.0 1.2 shard_map.89
  123.3 11.4 %all_to_all.40 = f32[16,1,896]{2,1,0:T(1,128)S(1)} all-to-all(f32[16,1,896]{2,1,0:T(1,128)S(1)} %copy.12), channel_id=1, replica_groups=mesh['x'=4,'y'=8,'node'=2,'dp'=8] {'y','node'}, dimensions={0} | all-to-all | bytes 114688 | tf_op jit(solution)/shard_map/all_to_all | solution.py:329
  134.9 16.6 %all_to_all.41 = f32[64,1,896]{2,1,0:T(1,128)S(1)} all-to-all(f32[64,1,896]{2,1,0:T(1,128)S(1)} %broadcast_in_dim.14), channel_id=1, replica_groups=mesh['x'=4,'y'=8,'node'=2,'dp'=8] {'x','y','node'}, dimensions={0} | all-to-all | bytes 458752 | tf_op jit(solution)/shard_map/all_to_all | solution.py:331
  (24 shorter events, 1.7 us)
Async XLA Ops:
  10.1 68.4 %all-to-all-start = ((bf16[64,144,128]{2,1,0:T(8,128)(2,1)}), bf16[64,144,128]{2,1,0:T(8,128)(2,1)}, u32[]{:S(2)}, u32[]{:S(2)}) async-start(bf16[64,144,128]{2,1,0:T(8,128)(2,1)} %shard_map.85), calls=%async_computation | async-start | bytes 4718592 | tf_op jit(solution)/shard_map/all_to_all | solution.py:315
  21.9 130.3 %reduce-scatter.2.cloned.1.call-start = ((), (), s32[]{:S(2)}) async-start(), calls=%async_computation.6 | async-start | bytes 2949120 | tf_op jit(solution)/shard_map/reduce_scatter | solution.py:323
  21.9 6.7 %copy-start.3 = (s32[128,8]{0,1:T(8,128)S(1)}, s32[128,8]{0,1:T(8,128)}, u32[]{:S(2)}) copy-start(s32[128,8]{0,1:T(8,128)} %param.9) | copy-start | bytes 12292
  21.9 6.7 %copy-start.2 = (f32[128,64]{0,1:T(8,128)S(1)}, f32[128,64]{0,1:T(8,128)}, u32[]{:S(2)}) copy-start(f32[128,64]{0,1:T(8,128)} %param.8) | copy-start | bytes 98308
  22.0 6.7 %copy-start = (bf16[128,896]{1,0:T(8,128)(2,1)S(1)}, bf16[128,896]{1,0:T(8,128)(2,1)}, u32[]{:S(2)}) copy-start(bf16[128,896]{1,0:T(8,128)(2,1)} %tokens_ref.1) | copy-start | bytes 688132
  28.7 32.3 %collective-permute-start = (bf16[128,896]{1,0:T(8,128)(2,1)S(1)}, bf16[128,896]{1,0:T(8,128)(2,1)S(1)}, u32[]{:S(2)}, u32[]{:S(2)}) collective-permute-start(bf16[128,896]{1,0:T(8,128)(2,1)S(1)} %copy-done), channel_id=1, source_target_pairs={{0,128},{128,256},{256,384},{384,0},{1,129},{129,257},{257,385},{3... | collective-permute-start | bytes 688136 | tf_op jit(solution)/shard_map/ppermute | solution.py:312
  32.1 28.9 %collective-permute-start.1 = (bf16[128,896]{1,0:T(8,128)(2,1)S(1)}, bf16[128,896]{1,0:T(8,128)(2,1)S(1)}, u32[]{:S(2)}, u32[]{:S(2)}) collective-permute-start(bf16[128,896]{1,0:T(8,128)(2,1)S(1)} %copy-done), channel_id=1, source_target_pairs={{0,256},{128,384},{256,0},{384,128},{1,257},{129,385},{257,1},{385... | collective-permute-start | bytes 688136 | tf_op jit(solution)/shard_map/ppermute | solution.py:312
  36.6 24.4 %collective-permute-start.2 = (bf16[128,896]{1,0:T(8,128)(2,1)S(1)}, bf16[128,896]{1,0:T(8,128)(2,1)S(1)}, u32[]{:S(2)}, u32[]{:S(2)}) collective-permute-start(bf16[128,896]{1,0:T(8,128)(2,1)S(1)} %copy-done), channel_id=1, source_target_pairs={{0,384},{128,0},{256,128},{384,256},{1,385},{129,1},{257,129},{385... | collective-permute-start | bytes 688136 | tf_op jit(solution)/shard_map/ppermute | solution.py:312
  39.6 15.0 %collective-permute-start.3 = (f32[72,128]{1,0:T(8,128)S(1)}, f32[72,128]{1,0:T(8,128)S(1)}, u32[]{:S(2)}, u32[]{:S(2)}) collective-permute-start(f32[72,128]{1,0:T(8,128)S(1)} %pad_maximum_fusion.2.table_ref), channel_id=1, source_target_pairs={{0,128},{128,256},{256,384},{384,0},{1,129},{129,257},{257,385},{3... | collective-permute-start | bytes 110600 | tf_op jit(solution)/shard_map/ppermute | solution.py:312
  41.9 17.5 %collective-permute-start.4 = (f32[72,128]{1,0:T(8,128)S(1)}, f32[72,128]{1,0:T(8,128)S(1)}, u32[]{:S(2)}, u32[]{:S(2)}) collective-permute-start(f32[72,128]{1,0:T(8,128)S(1)} %pad_maximum_fusion.2.table_ref), channel_id=1, source_target_pairs={{0,256},{128,384},{256,0},{384,128},{1,257},{129,385},{257,1},{385... | collective-permute-start | bytes 110600 | tf_op jit(solution)/shard_map/ppermute | solution.py:312
  54.6 6.4 %collective-permute-start.5 = (f32[72,128]{1,0:T(8,128)S(1)}, f32[72,128]{1,0:T(8,128)S(1)}, u32[]{:S(2)}, u32[]{:S(2)}) collective-permute-start(f32[72,128]{1,0:T(8,128)S(1)} %pad_maximum_fusion.2.table_ref), channel_id=1, source_target_pairs={{0,384},{128,0},{256,128},{384,256},{1,385},{129,1},{257,129},{385... | collective-permute-start | bytes 110600 | tf_op jit(solution)/shard_map/ppermute | solution.py:312
  61.0 0.7 copy-start.1
  87.1 25.7 %copy-start.4 = (bf16[1280,896]{1,0:T(8,128)(2,1)S(1)}, bf16[1280,896]{1,0:T(8,128)(2,1)}, u32[]{:S(2)}) copy-start(bf16[1280,896]{1,0:T(8,128)(2,1)} %get-tuple-element.19) | copy-start | bytes 6881284
  87.2 17.3 %all-to-all-start.1 = ((f32[8,16,128]{2,1,0:T(8,128)}), f32[8,16,128]{2,1,0:T(8,128)S(1)}, u32[]{:S(2)}, u32[]{:S(2)}) async-start(f32[8,16,128]{2,1,0:T(8,128)} %get-tuple-element.18), calls=%async_computation.1 | async-start | bytes 131072 | tf_op jit(solution)/shard_map/all_to_all | solution.py:322
  105.3 16.7 %all-to-all-start.2 = ((f32[64,1,128]{2,1,0:T(1,128)}), f32[64,1,128]{2,1,0:T(1,128)S(1)}, u32[]{:S(2)}, u32[]{:S(2)}) async-start(f32[64,1,128]{2,1,0:T(1,128)} %bitcast.12), calls=%async_computation.2 | async-start | bytes 65536 | tf_op jit(solution)/shard_map/all_to_all | solution.py:324
Sparse Core Ops, SparseCore 0:
  87.3 43.4 reduce-scatter.1

commit v7 on v6

--- a/solution.py
+++ b/solution.py
@@ -169,11 +169,10 @@
     j = lax.broadcasted_iota(jnp.int32, (LANES, LANES), 1)
     q, source, r = i // 32, i % 32 // EXTRA, i % EXTRA
     move = jnp.where(source * MAIN + q * EXTRA + r == j, 1.0, 0.0).astype(bf16)
-    j = lax.broadcasted_iota(jnp.int32, (BLOCK, BLOCK), 0)
-    back = jnp.where(source_order(lax.broadcasted_iota(jnp.int32, (BLOCK, BLOCK), 1)) == j, 1.0, 0.0).astype(bf16)
     ones = jnp.ones((8, LANES), bf16)
     slot_ref[...] = jnp.zeros_like(slot_ref)
     for c in range(PARTS):
+        at = slice(c * CHUNK, (c + 1) * CHUNK)
         come[c].wait()
         for g in range(c * PAIR // 8, (c + 1) * PAIR // 8):
             some = slice(8 * g, 8 * g + 8)
@@ -194,12 +193,21 @@
         stores[c][0].start()
         saved[c].wait()
         terms = []
+        whole = jnp.dot(rows_ref[at, :], down_ref[...], preferred_element_type=f32)
         for g in range(CHUNK // BLOCK * c, CHUNK // BLOCK * (c + 1)):
             line = slice(BLOCK * g, BLOCK * (g + 1))
-            part = jnp.dot(rows_ref[line, :], down_ref[...], preferred_element_type=f32)
+            part = whole[BLOCK * g - c * CHUNK : BLOCK * (g + 1) - c * CHUNK]
             both = part * hidden_ref[line, :].astype(f32)
             terms.append(sum(both[:, LANES * q : LANES * (q + 1)] for q in range(HID // LANES)))
-            part_ref[line, :] = jnp.dot(back, part.astype(bf16), preferred_element_type=f32).astype(bf16)
+            part = jnp.concatenate(
+                [
+                    part[first + size * s : first + size * (s + 1)]
+                    for s in range(8)
+                    for first, size in ((0, MAIN), (8 * MAIN, EXTRA))
+                ],
+                axis=0,
+            )
+            part_ref[line, :] = part.astype(bf16)
         rest = jnp.concatenate(terms, axis=0)
         stores[c][1].start()
         sums = jnp.zeros((8, CHUNK), f32)

time: 160 us -> 159 us (level)
  transfers between devices with their start and end apart: 10 -> 10, of which waited for: 5 -> 5; matrix products, arithmetic and copies ran while one was open for 7% -> 7% of each run, Pallas kernels for 5% -> 6%
where the time goes in v7:
time: 159 us; the launch traced here: 158 us
  starting transfers between devices  47.3 us (30%)
  waiting for transfers between devices  37.7 us (24%)
  blocking collectives  28 us (18%)
  Pallas kernels  19.1 us (12%)
  between operations  14.2 us (9%)
  matrix products  5.94 us (4%)
  local copies, waits for them, and re-layouts  4.49 us (3%)
    ppermute x6, starting transfers between devices, gather(): lax.ppermute(v, 'x', [(i, (i + k) % ROW) for i in range(ROW)])  17.8 us
    all_to_all x1, blocking collectives, body(): gate_grad = exchange(jnp.broadcast_to(gate_row, (EXP, FEAT)), both)  16.6 us
    all_to_all x1, waiting for transfers between devices, body(): recv = exchange(pack(ids, scores, grad_out), both)  15.8 us
    all_to_all x1, starting transfers between devices, body(): recv = exchange(pack(ids, scores, grad_out), both)  11.8 us
    ppermute x6, waiting for transfers between devices, gather(): lax.ppermute(v, 'x', [(i, (i + k) % ROW) for i in range(ROW)])  11.5 us
    all_to_all x1, blocking collectives, body(): exchange(gate(x, table, tables, back, tokens, others), ('y', 'node'))  11.4 us
    all_to_all x1, starting transfers between devices, body(): slot = exchange(slot, 'dp')  10.1 us
    all_to_all x1, starting transfers between devices, body(): back = exchange(spread(slot), both)  7.5 us
  transfers between devices with their start and end apart: 10, of which 5 were waited for; matrix products, arithmetic and copies ran while one was open for 7% of the time, Pallas kernels for 6%

profile of v7, /device:TPU:1, one launch (start us, length us, event | category | flops | bytes accessed | tf_op | source)
XLA Modules:
  0.0 158.0 jit_solution(14430840986907970968)
XLA Ops:
  7.2 2.9 %shard_map.85 = bf16[64,144,128]{2,1,0:T(8,128)(2,1)} custom-call(s32[8,128]{1,0:T(8,128)} %bitcast.40, f32[64,128]{1,0:T(8,128)} %bitcast.35, bf16[128,896]{1,0:T(8,128)(2,1)} %grad_any.1), custom_call_target="tpu_custom_call" | custom-call | flops 500000000 | bytes 2700000 | tf_op jit(solution)/shard_map/pallas_call | solution.py:99
  10.1 11.8 %all-to-all-start = ((bf16[64,144,128]{2,1,0:T(8,128)(2,1)}), bf16[64,144,128]{2,1,0:T(8,128)(2,1)}, u32[]{:S(2)}, u32[]{:S(2)}) async-start(bf16[64,144,128]{2,1,0:T(8,128)(2,1)} %shard_map.85), calls=%async_computation | async-start | bytes 4718592 | tf_op jit(solution)/shard_map/all_to_all | solution.py:323
  22.0 6.7 %shard_map.86.hidden_any = bf16[1280,1024]{1,0:T(8,128)(2,1)} custom-call(bf16[1280,1024]{1,0:T(8,128)(2,1)} %bitcast.30), custom_call_target="tpu_custom_call" | custom-call | flops 500000000 | bytes 5300000 | tf_op jit(solution)/shard_map/pallas_call | solution.py:132
  28.7 3.4 %collective-permute-start = (bf16[128,896]{1,0:T(8,128)(2,1)S(1)}, bf16[128,896]{1,0:T(8,128)(2,1)S(1)}, u32[]{:S(2)}, u32[]{:S(2)}) collective-permute-start(bf16[128,896]{1,0:T(8,128)(2,1)S(1)} %copy-done), channel_id=1, source_target_pairs={{0,128},{128,256},{256,384},{384,0},{1,129},{129,257},{257,385},{3... | collective-permute-start | bytes 688136 | tf_op jit(solution)/shard_map/ppermute | solution.py:320
  32.1 4.5 %collective-permute-start.1 = (bf16[128,896]{1,0:T(8,128)(2,1)S(1)}, bf16[128,896]{1,0:T(8,128)(2,1)S(1)}, u32[]{:S(2)}, u32[]{:S(2)}) collective-permute-start(bf16[128,896]{1,0:T(8,128)(2,1)S(1)} %copy-done), channel_id=1, source_target_pairs={{0,256},{128,384},{256,0},{384,128},{1,257},{129,385},{257,1},{385... | collective-permute-start | bytes 688136 | tf_op jit(solution)/shard_map/ppermute | solution.py:320
  36.6 3.0 %collective-permute-start.2 = (bf16[128,896]{1,0:T(8,128)(2,1)S(1)}, bf16[128,896]{1,0:T(8,128)(2,1)S(1)}, u32[]{:S(2)}, u32[]{:S(2)}) collective-permute-start(bf16[128,896]{1,0:T(8,128)(2,1)S(1)} %copy-done), channel_id=1, source_target_pairs={{0,384},{128,0},{256,128},{384,256},{1,385},{129,1},{257,129},{385... | collective-permute-start | bytes 688136 | tf_op jit(solution)/shard_map/ppermute | solution.py:320
  39.6 2.3 %collective-permute-start.3 = (f32[72,128]{1,0:T(8,128)S(1)}, f32[72,128]{1,0:T(8,128)S(1)}, u32[]{:S(2)}, u32[]{:S(2)}) collective-permute-start(f32[72,128]{1,0:T(8,128)S(1)} %pad_maximum_fusion.2.table_ref), channel_id=1, source_target_pairs={{0,128},{128,256},{256,384},{384,0},{1,129},{129,257},{257,385},{3... | collective-permute-start | bytes 110600 | tf_op jit(solution)/shard_map/ppermute | solution.py:320
  41.9 2.7 %collective-permute-start.4 = (f32[72,128]{1,0:T(8,128)S(1)}, f32[72,128]{1,0:T(8,128)S(1)}, u32[]{:S(2)}, u32[]{:S(2)}) collective-permute-start(f32[72,128]{1,0:T(8,128)S(1)} %pad_maximum_fusion.2.table_ref), channel_id=1, source_target_pairs={{0,256},{128,384},{256,0},{384,128},{1,257},{129,385},{257,1},{385... | collective-permute-start | bytes 110600 | tf_op jit(solution)/shard_map/ppermute | solution.py:320
  44.6 10.0 %collective-permute-done.3 = f32[72,128]{1,0:T(8,128)S(1)} collective-permute-done((f32[72,128]{1,0:T(8,128)S(1)}, f32[72,128]{1,0:T(8,128)S(1)}, u32[]{:S(2)}, u32[]{:S(2)}) %collective-permute-start.3) | collective-permute-done | bytes 36896 | tf_op jit(solution)/shard_map/ppermute | solution.py:320
  54.6 1.9 %collective-permute-start.5 = (f32[72,128]{1,0:T(8,128)S(1)}, f32[72,128]{1,0:T(8,128)S(1)}, u32[]{:S(2)}, u32[]{:S(2)}) collective-permute-start(f32[72,128]{1,0:T(8,128)S(1)} %pad_maximum_fusion.2.table_ref), channel_id=1, source_target_pairs={{0,384},{128,0},{256,128},{384,256},{1,385},{129,1},{257,129},{385... | collective-permute-start | bytes 110600 | tf_op jit(solution)/shard_map/ppermute | solution.py:320
  56.5 2.9 %copy.10 = bf16[1,1024,896]{1,2,0:T(8,128)(2,1)S(1)} copy(bf16[1,1024,896]{2,1,0:T(8,128)(2,1)} %param.11) | data formatting | bytes 3670016 | tf_op args[5]
  59.4 1.6 collective-permute-done.5
  61.7 1.0 pad_maximum_fusion.others_ref
  62.8 15.8 %all-to-all-done.recv_any = bf16[64,144,128]{2,1,0:T(8,128)(2,1)} async-done(((bf16[64,144,128]{2,1,0:T(8,128)(2,1)}), bf16[64,144,128]{2,1,0:T(8,128)(2,1)}, u32[]{:S(2)}, u32[]{:S(2)}) %all-to-all-start) | async-done | bytes 2359328 | tf_op jit(solution)/shard_map/all_to_all | solution.py:323
  78.5 7.5 %shard_map.87 = (bf16[1280,1024]{1,0:T(8,128)(2,1)}, f32[8,16,128]{2,1,0:T(8,128)}, bf16[1280,896]{1,0:T(8,128)(2,1)}) custom-call(bf16[64,144,128]{2,1,0:T(8,128)(2,1)} %all-to-all-done.recv_any, bf16[1280,1024]{1,0:T(8,128)(2,1)} %shard_map.86.hidden_any, bf16[896,1024]{1,0:T(8,128)(2,1)S(1)} %bitcast.27), custom_call_target="tpu_custom_call" | custom-call | flops 2400000000 | bytes 11000000 | tf_op jit(solution)/shard_map/pallas_call | solution.py:232
  86.1 10.1 %all-to-all-start.1 = ((f32[8,16,128]{2,1,0:T(8,128)}), f32[8,16,128]{2,1,0:T(8,128)S(1)}, u32[]{:S(2)}, u32[]{:S(2)}) async-start(f32[8,16,128]{2,1,0:T(8,128)} %get-tuple-element.18), calls=%async_computation.1 | async-start | bytes 131072 | tf_op jit(solution)/shard_map/all_to_all | solution.py:330
  96.2 7.2 %all-to-all-done.1.slot_ref = f32[8,16,128]{2,1,0:T(8,128)S(1)} async-done(((f32[8,16,128]{2,1,0:T(8,128)}), f32[8,16,128]{2,1,0:T(8,128)S(1)}, u32[]{:S(2)}, u32[]{:S(2)}) %all-to-all-start.1) | async-done | bytes 65568 | tf_op jit(solution)/shard_map/all_to_all | solution.py:330
  103.4 0.9 shard_map.88
  104.2 7.5 %all-to-all-start.2 = ((f32[64,1,128]{2,1,0:T(1,128)}), f32[64,1,128]{2,1,0:T(1,128)S(1)}, u32[]{:S(2)}, u32[]{:S(2)}) async-start(f32[64,1,128]{2,1,0:T(1,128)} %bitcast.12), calls=%async_computation.2 | async-start | bytes 65536 | tf_op jit(solution)/shard_map/all_to_all | solution.py:332
  111.7 5.9 %convert_bitcast_fusion = bf16[1,1024,896]{2,1,0:T(8,128)(2,1)} fusion(bf16[1280,1024]{1,0:T(8,128)(2,1)} %shard_map.86.hidden_any, bf16[1280,896]{1,0:T(8,128)(2,1)S(1)} %copy-done.4), kind=kOutput, calls=%fused_computation | convolution fusion | flops 2349727744 | bytes 6750208 | tf_op jit(solution)/shard_map/dot_general | solution.py:333
  117.7 3.3 %all-to-all-done.2 = f32[64,1,128]{2,1,0:T(1,128)S(1)} async-done(((f32[64,1,128]{2,1,0:T(1,128)}), f32[64,1,128]{2,1,0:T(1,128)S(1)}, u32[]{:S(2)}, u32[]{:S(2)}) %all-to-all-start.2) | async-done | bytes 32800 | tf_op jit(solution)/shard_map/all_to_all | solution.py:332
  120.9 1.2 shard_map.89
  122.2 11.4 %all_to_all.40 = f32[16,1,896]{2,1,0:T(1,128)S(1)} all-to-all(f32[16,1,896]{2,1,0:T(1,128)S(1)} %copy.12), channel_id=1, replica_groups=mesh['x'=4,'y'=8,'node'=2,'dp'=8] {'y','node'}, dimensions={0} | all-to-all | bytes 114688 | tf_op jit(solution)/shard_map/all_to_all | solution.py:337
  133.8 16.6 %all_to_all.41 = f32[64,1,896]{2,1,0:T(1,128)S(1)} all-to-all(f32[64,1,896]{2,1,0:T(1,128)S(1)} %broadcast_in_dim.14), channel_id=1, replica_groups=mesh['x'=4,'y'=8,'node'=2,'dp'=8] {'x','y','node'}, dimensions={0} | all-to-all | bytes 458752 | tf_op jit(solution)/shard_map/all_to_all | solution.py:339
  (24 shorter events, 1.7 us)
Async XLA Ops:
  10.1 68.4 %all-to-all-start = ((bf16[64,144,128]{2,1,0:T(8,128)(2,1)}), bf16[64,144,128]{2,1,0:T(8,128)(2,1)}, u32[]{:S(2)}, u32[]{:S(2)}) async-start(bf16[64,144,128]{2,1,0:T(8,128)(2,1)} %shard_map.85), calls=%async_computation | async-start | bytes 4718592 | tf_op jit(solution)/shard_map/all_to_all | solution.py:323
  21.9 129.2 %reduce-scatter.2.cloned.1.call-start = ((), (), s32[]{:S(2)}) async-start(), calls=%async_computation.6 | async-start | bytes 2949120 | tf_op jit(solution)/shard_map/reduce_scatter | solution.py:331
  21.9 6.7 %copy-start.3 = (s32[128,8]{0,1:T(8,128)S(1)}, s32[128,8]{0,1:T(8,128)}, u32[]{:S(2)}) copy-start(s32[128,8]{0,1:T(8,128)} %param.9) | copy-start | bytes 12292
  21.9 6.7 %copy-start.2 = (f32[128,64]{0,1:T(8,128)S(1)}, f32[128,64]{0,1:T(8,128)}, u32[]{:S(2)}) copy-start(f32[128,64]{0,1:T(8,128)} %param.8) | copy-start | bytes 98308
  22.0 6.7 %copy-start = (bf16[128,896]{1,0:T(8,128)(2,1)S(1)}, bf16[128,896]{1,0:T(8,128)(2,1)}, u32[]{:S(2)}) copy-start(bf16[128,896]{1,0:T(8,128)(2,1)} %tokens_ref.1) | copy-start | bytes 688132
  28.7 32.3 %collective-permute-start = (bf16[128,896]{1,0:T(8,128)(2,1)S(1)}, bf16[128,896]{1,0:T(8,128)(2,1)S(1)}, u32[]{:S(2)}, u32[]{:S(2)}) collective-permute-start(bf16[128,896]{1,0:T(8,128)(2,1)S(1)} %copy-done), channel_id=1, source_target_pairs={{0,128},{128,256},{256,384},{384,0},{1,129},{129,257},{257,385},{3... | collective-permute-start | bytes 688136 | tf_op jit(solution)/shard_map/ppermute | solution.py:320
  32.1 28.9 %collective-permute-start.1 = (bf16[128,896]{1,0:T(8,128)(2,1)S(1)}, bf16[128,896]{1,0:T(8,128)(2,1)S(1)}, u32[]{:S(2)}, u32[]{:S(2)}) collective-permute-start(bf16[128,896]{1,0:T(8,128)(2,1)S(1)} %copy-done), channel_id=1, source_target_pairs={{0,256},{128,384},{256,0},{384,128},{1,257},{129,385},{257,1},{385... | collective-permute-start | bytes 688136 | tf_op jit(solution)/shard_map/ppermute | solution.py:320
  36.6 24.4 %collective-permute-start.2 = (bf16[128,896]{1,0:T(8,128)(2,1)S(1)}, bf16[128,896]{1,0:T(8,128)(2,1)S(1)}, u32[]{:S(2)}, u32[]{:S(2)}) collective-permute-start(bf16[128,896]{1,0:T(8,128)(2,1)S(1)} %copy-done), channel_id=1, source_target_pairs={{0,384},{128,0},{256,128},{384,256},{1,385},{129,1},{257,129},{385... | collective-permute-start | bytes 688136 | tf_op jit(solution)/shard_map/ppermute | solution.py:320
  39.6 15.0 %collective-permute-start.3 = (f32[72,128]{1,0:T(8,128)S(1)}, f32[72,128]{1,0:T(8,128)S(1)}, u32[]{:S(2)}, u32[]{:S(2)}) collective-permute-start(f32[72,128]{1,0:T(8,128)S(1)} %pad_maximum_fusion.2.table_ref), channel_id=1, source_target_pairs={{0,128},{128,256},{256,384},{384,0},{1,129},{129,257},{257,385},{3... | collective-permute-start | bytes 110600 | tf_op jit(solution)/shard_map/ppermute | solution.py:320
  41.9 17.5 %collective-permute-start.4 = (f32[72,128]{1,0:T(8,128)S(1)}, f32[72,128]{1,0:T(8,128)S(1)}, u32[]{:S(2)}, u32[]{:S(2)}) collective-permute-start(f32[72,128]{1,0:T(8,128)S(1)} %pad_maximum_fusion.2.table_ref), channel_id=1, source_target_pairs={{0,256},{128,384},{256,0},{384,128},{1,257},{129,385},{257,1},{385... | collective-permute-start | bytes 110600 | tf_op jit(solution)/shard_map/ppermute | solution.py:320
  54.6 6.4 %collective-permute-start.5 = (f32[72,128]{1,0:T(8,128)S(1)}, f32[72,128]{1,0:T(8,128)S(1)}, u32[]{:S(2)}, u32[]{:S(2)}) collective-permute-start(f32[72,128]{1,0:T(8,128)S(1)} %pad_maximum_fusion.2.table_ref), channel_id=1, source_target_pairs={{0,384},{128,0},{256,128},{384,256},{1,385},{129,1},{257,129},{385... | collective-permute-start | bytes 110600 | tf_op jit(solution)/shard_map/ppermute | solution.py:320
  61.0 0.7 copy-start.1
  86.0 25.7 %copy-start.4 = (bf16[1280,896]{1,0:T(8,128)(2,1)S(1)}, bf16[1280,896]{1,0:T(8,128)(2,1)}, u32[]{:S(2)}) copy-start(bf16[1280,896]{1,0:T(8,128)(2,1)} %get-tuple-element.19) | copy-start | bytes 6881284
  86.1 17.3 %all-to-all-start.1 = ((f32[8,16,128]{2,1,0:T(8,128)}), f32[8,16,128]{2,1,0:T(8,128)S(1)}, u32[]{:S(2)}, u32[]{:S(2)}) async-start(f32[8,16,128]{2,1,0:T(8,128)} %get-tuple-element.18), calls=%async_computation.1 | async-start | bytes 131072 | tf_op jit(solution)/shard_map/all_to_all | solution.py:330
  104.2 16.7 %all-to-all-start.2 = ((f32[64,1,128]{2,1,0:T(1,128)}), f32[64,1,128]{2,1,0:T(1,128)S(1)}, u32[]{:S(2)}, u32[]{:S(2)}) async-start(f32[64,1,128]{2,1,0:T(1,128)} %bitcast.12), calls=%async_computation.2 | async-start | bytes 65536 | tf_op jit(solution)/shard_map/all_to_all | solution.py:332
Sparse Core Ops, SparseCore 0:
  86.2 43.3 reduce-scatter.1

commit v8 on v7

--- a/solution.py
+++ b/solution.py
@@ -139,6 +139,88 @@
     )(hidden)
 
 
+def extra_place(i):
+    return i % 32 // EXTRA * MAIN + i // 32 * EXTRA + i % EXTRA
+
+
+def output_kernel(hidden_ref, down_ref, out_ref):
+    y = jnp.dot(hidden_ref[...], down_ref[...], preferred_element_type=f32).astype(bf16)
+    j = lax.broadcasted_iota(jnp.int32, (LANES, LANES), 0)
+    i = lax.broadcasted_iota(jnp.int32, (LANES, LANES), 1)
+    move = jnp.where(extra_place(i) == j, 1.0, 0.0).astype(bf16)
+    for j in range(COLS):
+        out_ref[:, MAIN * j : MAIN * (j + 1), :] = y[: 8 * MAIN, LANES * j : LANES * (j + 1)].reshape(8, MAIN, LANES)
+    for part in range(2):
+        blocks = []
+        for q in range(4):
+            j = part * 4 + q
+            empty = jnp.zeros((32, LANES), bf16)
+            blocks.append(y[8 * MAIN :, LANES * j : LANES * (j + 1)] if j < COLS else empty)
+        x = jnp.dot(move, jnp.concatenate(blocks, axis=0), preferred_element_type=f32).astype(bf16)
+        start = COLS * MAIN + part * MAIN
+        out_ref[:, start : start + MAIN, :] = x.reshape(8, MAIN, LANES)
+
+
+def outputs(hidden, down):
+    return pl.pallas_call(
+        output_kernel,
+        grid=(GROUPS,),
+        in_specs=[pl.BlockSpec((BLOCK, HID), lambda i: (i, 0)), pl.BlockSpec((HID, FEAT), lambda i: (0, 0))],
+        out_specs=pl.BlockSpec((8, PIECE, LANES), lambda i: (i, 0, 0)),
+        out_shape=jax.ShapeDtypeStruct((EXP, PIECE, LANES), bf16),
+        compiler_params=pltpu.CompilerParams(vmem_limit_bytes=56 * MIB),
+        cost_estimate=pl.CostEstimate(flops=2_400_000_000, bytes_accessed=6_900_000, transcendentals=0),
+    )(hidden, down)
+
+
+def slot_kernel(recv_any, outs_any, slot_ref, recv_ref, outs_ref, sems):
+    copies = []
+    for c in range(PARTS):
+        at = slice(c * PAIR, (c + 1) * PAIR)
+        copies.append(
+            [
+                pltpu.make_async_copy(recv_any.at[at], recv_ref.at[at], sems.at[0, c]),
+                pltpu.make_async_copy(outs_any.at[at], outs_ref.at[at], sems.at[1, c]),
+            ]
+        )
+        for copy in copies[c]:
+            copy.start()
+    ones = jnp.ones((8, LANES), bf16)
+    for c in range(PARTS):
+        at = slice(c * PAIR, (c + 1) * PAIR)
+        for copy in copies[c]:
+            copy.wait()
+        tiles = []
+        for j in range(PIECE // MAIN):
+            rows = slice(MAIN * j, MAIN * (j + 1))
+            tiles.append(recv_ref[at, rows, :].astype(f32) * outs_ref[at, rows, :].astype(f32))
+        for kind, some in enumerate((tiles[:COLS], tiles[COLS:])):
+            rest = sum(some).reshape(PAIR * MAIN, LANES)
+            sums = jnp.zeros((8, PAIR * MAIN), f32)
+            for _ in range(3):
+                term = rest.astype(bf16)
+                rest = rest - term.astype(f32)
+                sums = sums + lax.dot_general(ones, term, (((1,), (1,)), ((), ())), preferred_element_type=f32)
+            for h in range(PAIR // 8):
+                slot_ref[:, kind * GROUPS + PAIR // 8 * c + h, :] = sums[:, LANES * h : LANES * (h + 1)]
+
+
+def slots(recv, outs):
+    any_space = pl.BlockSpec(memory_space=pl.ANY)
+    return pl.pallas_call(
+        slot_kernel,
+        in_specs=[any_space] * 2,
+        out_shape=jax.ShapeDtypeStruct((GROUPS, SLOT_ROWS, LANES), f32),
+        scratch_shapes=[
+            pltpu.VMEM((EXP, PIECE, LANES), bf16),
+            pltpu.VMEM((EXP, PIECE, LANES), bf16),
+            pltpu.SemaphoreType.DMA((2, PARTS)),
+        ],
+        compiler_params=pltpu.CompilerParams(vmem_limit_bytes=52 * MIB),
+        cost_estimate=pl.CostEstimate(flops=10_000_000, bytes_accessed=4_800_000, transcendentals=0),
+    )(recv, outs)
+
+
 PARTS = 2
 CHUNK = SLOTS // PARTS
 PAIR = EXP // PARTS
@@ -146,15 +228,13 @@
 
 
 def expert_kernel(
-    recv_any, hidden_any, down_ref, part_any, slot_ref, rows_any,
-    recv_ref, hidden_ref, part_ref, rows_ref, in_sems, out_sems,
+    recv_any, down_ref, part_any, rows_any, recv_ref, part_ref, rows_ref, in_sems, out_sems,
 ):
-    come, saved, stores = [], [], []
+    come, stores = [], []
     for c in range(PARTS):
         at = slice(c * PAIR, (c + 1) * PAIR)
-        come.append(pltpu.make_async_copy(recv_any.at[at], recv_ref.at[at], in_sems.at[0, c]))
+        come.append(pltpu.make_async_copy(recv_any.at[at], recv_ref.at[at], in_sems.at[c]))
         at = slice(c * CHUNK, (c + 1) * CHUNK)
-        saved.append(pltpu.make_async_copy(hidden_any.at[at], hidden_ref.at[at], in_sems.at[1, c]))
         stores.append(
             [
                 pltpu.make_async_copy(rows_ref.at[at], rows_any.at[at], out_sems.at[0, c]),
@@ -163,14 +243,10 @@
         )
     for c in range(PARTS):
         come[c].start()
-        saved[c].start()
 
     i = lax.broadcasted_iota(jnp.int32, (LANES, LANES), 0)
     j = lax.broadcasted_iota(jnp.int32, (LANES, LANES), 1)
-    q, source, r = i // 32, i % 32 // EXTRA, i % EXTRA
-    move = jnp.where(source * MAIN + q * EXTRA + r == j, 1.0, 0.0).astype(bf16)
-    ones = jnp.ones((8, LANES), bf16)
-    slot_ref[...] = jnp.zeros_like(slot_ref)
+    move = jnp.where(extra_place(i) == j, 1.0, 0.0).astype(bf16)
     for c in range(PARTS):
         at = slice(c * CHUNK, (c + 1) * CHUNK)
         come[c].wait()
@@ -191,14 +267,10 @@
                             32 * q : 32 * (q + 1)
                         ]
         stores[c][0].start()
-        saved[c].wait()
-        terms = []
         whole = jnp.dot(rows_ref[at, :], down_ref[...], preferred_element_type=f32)
         for g in range(CHUNK // BLOCK * c, CHUNK // BLOCK * (c + 1)):
             line = slice(BLOCK * g, BLOCK * (g + 1))
             part = whole[BLOCK * g - c * CHUNK : BLOCK * (g + 1) - c * CHUNK]
-            both = part * hidden_ref[line, :].astype(f32)
-            terms.append(sum(both[:, LANES * q : LANES * (q + 1)] for q in range(HID // LANES)))
             part = jnp.concatenate(
                 [
                     part[first + size * s : first + size * (s + 1)]
@@ -208,17 +280,7 @@
                 axis=0,
             )
             part_ref[line, :] = part.astype(bf16)
-        rest = jnp.concatenate(terms, axis=0)
         stores[c][1].start()
-        sums = jnp.zeros((8, CHUNK), f32)
-        for _ in range(3):
-            term = rest.astype(bf16)
-            rest = rest - term.astype(f32)
-            sums = sums + lax.dot_general(ones, term, (((1,), (1,)), ((), ())), preferred_element_type=f32)
-        for h in range(CHUNK // BLOCK):
-            g = CHUNK // BLOCK * c + h
-            slot_ref[:, g, :] = sums[:, BLOCK * h : BLOCK * h + LANES]
-            slot_ref[:, GROUPS + g, : BLOCK - LANES] = sums[:, BLOCK * h + LANES : BLOCK * (h + 1)]
     for pair in stores:
         for store in pair:
             store.wait()
@@ -227,39 +289,38 @@
 EXPERT_LIMIT = 52
 
 
-def expert(recv, hidden, down_t):
+def expert(recv, down_t):
     any_space = pl.BlockSpec(memory_space=pl.ANY)
     return pl.pallas_call(
         expert_kernel,
-        in_specs=[any_space, any_space, pl.BlockSpec(memory_space=pltpu.VMEM)],
-        out_specs=[any_space, pl.BlockSpec(memory_space=pltpu.VMEM), any_space],
+        in_specs=[any_space, pl.BlockSpec(memory_space=pltpu.VMEM)],
+        out_specs=[any_space, any_space],
         out_shape=[
             jax.ShapeDtypeStruct((SLOTS, HID), bf16),
-            jax.ShapeDtypeStruct((GROUPS, SLOT_ROWS, LANES), f32),
             jax.ShapeDtypeStruct((SLOTS, FEAT), bf16),
         ],
         scratch_shapes=[
             pltpu.VMEM((EXP, PIECE, LANES), bf16),
             pltpu.VMEM((SLOTS, HID), bf16),
-            pltpu.VMEM((SLOTS, HID), bf16),
             pltpu.VMEM((SLOTS, FEAT), bf16),
-            pltpu.SemaphoreType.DMA((2, PARTS)),
+            pltpu.SemaphoreType.DMA((PARTS,)),
             pltpu.SemaphoreType.DMA((2, PARTS)),
         ],
         compiler_params=pltpu.CompilerParams(vmem_limit_bytes=EXPERT_LIMIT * MIB),
         cost_estimate=pl.CostEstimate(flops=2_400_000_000, bytes_accessed=11_000_000, transcendentals=0),
-    )(recv, hidden, down_t)
+    )(recv, down_t)
 
 
 def spread_kernel(slot_ref, out_ref):
     summed = jnp.sum(slot_ref[...], axis=0)
     main = summed[:GROUPS]
-    extra = pltpu.roll(summed[GROUPS:], MAIN, 1)
+    extra = summed[GROUPS:]
+    extra = sum(pltpu.roll(extra, (MAIN - EXTRA * q) % LANES, 1) for q in range(4))
     lane = lax.broadcasted_iota(jnp.int32, (GROUPS, LANES), 1)
     span = lane[:1] // 32
     for place in range(8):
         a = pltpu.roll(main, -MAIN * place % LANES, 1) if place else main
-        b = pltpu.roll(extra, -EXTRA * place % LANES, 1) if place else extra
+        b = pltpu.roll(extra, -MAIN * place % LANES, 1) if place else extra
         value = jnp.where(lane < MAIN, a, b)
         moved = [pltpu.roll(value, 32 * k, 1) if k else value for k in range(ROW)]
         for x in range(ROW):
@@ -325,9 +386,12 @@
     table = jnp.concatenate([scores, ids.astype(f32)], axis=0)
     hidden, far_tokens, far_table = lax.optimization_barrier((hidden, tokens, table))
     others, tables = gather(far_tokens), gather(far_table)
-    recv, others, tables = lax.optimization_barrier((recv, others, tables))
-    part, slot, rows = expert(recv, hidden, down_weight[0].T)
+    outs = outputs(hidden, down_weight[0])
+    recv, others, tables, outs = lax.optimization_barrier((recv, others, tables, outs))
+    slot = slots(recv, outs)
+    part, rows = expert(recv, down_weight[0].T)
     slot = exchange(slot, "dp")
+    part, slot = lax.optimization_barrier((part, slot))
     summed = lax.psum_scatter(part, "dp", scatter_dimension=0, tiled=True)
     back = exchange(spread(slot), both)
     weight_grad = lax.dot_general(hidden, rows, (((0,), (0,)), ((), ())), preferred_element_type=f32)

time: 159 us -> 156 us (0.981)
  waiting for transfers between devices: 37.7 us -> 20.5 us
  Pallas kernels: 19.1 us -> 29.8 us
    pallas_call x1 -> x3, Pallas kernels: 7.5 us -> 18.1 us  [the longest x1 9 us: outputs(): pl.pallas_call(output_kernel, grid=(GROUPS,), in_specs=[pl.BlockSpec((BLO...]
    ppermute x6, waiting for transfers between devices: 11.5 us -> 3.14 us  [gather(): lax.ppermute(v, 'x', [(i, (i + k) % ROW) for i in range(ROW)])]
    all_to_all x1, waiting for transfers between devices: 7.15 us -> 1.39 us  [body(): slot = exchange(slot, 'dp')]
    all_to_all x1, waiting for transfers between devices: 15.8 us -> 13.6 us  [body(): recv = exchange(pack(ids, scores, grad_out), both)]
    ppermute x6, starting transfers between devices: 17.8 us -> 19.4 us  [gather(): lax.ppermute(v, 'x', [(i, (i + k) % ROW) for i in range(ROW)])]
    unnamed x12 -> x10, local copies, waits for them, and re-layouts: 4.3 us -> 4.3 us
  transfers between devices with their start and end apart: 10 -> 10, of which waited for: 5 -> 5; matrix products, arithmetic and copies ran while one was open for 7% -> 8% of each run, Pallas kernels for 6% -> 15%
where the time goes in v8:
time: 156 us; the launch traced here: 155 us
  starting transfers between devices  48.8 us (31%)
  Pallas kernels  29.8 us (19%)
  blocking collectives  28.9 us (19%)
  waiting for transfers between devices  20.5 us (13%)
  between operations  14.2 us (9%)
  matrix products  6.83 us (4%)
  local copies, waits for them, and re-layouts  4.49 us (3%)
    ppermute x6, starting transfers between devices, gather(): lax.ppermute(v, 'x', [(i, (i + k) % ROW) for i in range(ROW)])  19.4 us
    all_to_all x1, blocking collectives, body(): gate_grad = exchange(jnp.broadcast_to(gate_row, (EXP, FEAT)), both)  16.6 us
    all_to_all x1, waiting for transfers between devices, body(): recv = exchange(pack(ids, scores, grad_out), both)  13.6 us
    all_to_all x1, blocking collectives, body(): exchange(gate(x, table, tables, back, tokens, others), ('y', 'node'))  12.3 us
    all_to_all x1, starting transfers between devices, body(): recv = exchange(pack(ids, scores, grad_out), both)  11.8 us
    all_to_all x1, starting transfers between devices, body(): slot = exchange(slot, 'dp')  10 us
    pallas_call x1, Pallas kernels, outputs(): pl.pallas_call(output_kernel, grid=(GROUPS,), in_specs=[pl.BlockSpec((BLO...  9 us
    all_to_all x1, starting transfers between devices, body(): back = exchange(spread(slot), both)  7.49 us
  transfers between devices with their start and end apart: 10, of which 5 were waited for; matrix products, arithmetic and copies ran while one was open for 8% of the time, Pallas kernels for 15%

profile of v8, /device:TPU:1, one launch (start us, length us, event | category | flops | bytes accessed | tf_op | source)
XLA Modules:
  0.0 154.6 jit_solution(5701853628719405041)
XLA Ops:
  7.2 2.9 %shard_map.85 = bf16[64,144,128]{2,1,0:T(8,128)(2,1)} custom-call(s32[8,128]{1,0:T(8,128)} %bitcast.42, f32[64,128]{1,0:T(8,128)} %bitcast.37, bf16[128,896]{1,0:T(8,128)(2,1)} %grad_any.1), custom_call_target="tpu_custom_call" | custom-call | flops 500000000 | bytes 2700000 | tf_op jit(solution)/shard_map/pallas_call | solution.py:99
  10.1 11.8 %all-to-all-start = ((bf16[64,144,128]{2,1,0:T(8,128)(2,1)}), bf16[64,144,128]{2,1,0:T(8,128)(2,1)}, u32[]{:S(2)}, u32[]{:S(2)}) async-start(bf16[64,144,128]{2,1,0:T(8,128)(2,1)} %shard_map.85), calls=%async_computation | async-start | bytes 4718592 | tf_op jit(solution)/shard_map/all_to_all | solution.py:384
  21.9 6.7 %shard_map.86.hidden_ref = bf16[1280,1024]{1,0:T(8,128)(2,1)} custom-call(bf16[1280,1024]{1,0:T(8,128)(2,1)} %bitcast.31), custom_call_target="tpu_custom_call" | custom-call | flops 500000000 | bytes 5300000 | tf_op jit(solution)/shard_map/pallas_call | solution.py:132
  28.6 3.4 %collective-permute-start.3 = (f32[72,128]{1,0:T(8,128)S(1)}, f32[72,128]{1,0:T(8,128)S(1)}, u32[]{:S(2)}, u32[]{:S(2)}) collective-permute-start(f32[72,128]{1,0:T(8,128)S(1)} %pad_maximum_fusion.2.table_ref), channel_id=1, source_target_pairs={{0,128},{128,256},{256,384},{384,0},{1,129},{129,257},{257,385},{3... | collective-permute-start | bytes 110600 | tf_op jit(solution)/shard_map/ppermute | solution.py:381
  32.0 4.5 %collective-permute-start.4 = (f32[72,128]{1,0:T(8,128)S(1)}, f32[72,128]{1,0:T(8,128)S(1)}, u32[]{:S(2)}, u32[]{:S(2)}) collective-permute-start(f32[72,128]{1,0:T(8,128)S(1)} %pad_maximum_fusion.2.table_ref), channel_id=1, source_target_pairs={{0,256},{128,384},{256,0},{384,128},{1,257},{129,385},{257,1},{385... | collective-permute-start | bytes 110600 | tf_op jit(solution)/shard_map/ppermute | solution.py:381
  36.6 3.0 %collective-permute-start.5 = (f32[72,128]{1,0:T(8,128)S(1)}, f32[72,128]{1,0:T(8,128)S(1)}, u32[]{:S(2)}, u32[]{:S(2)}) collective-permute-start(f32[72,128]{1,0:T(8,128)S(1)} %pad_maximum_fusion.2.table_ref), channel_id=1, source_target_pairs={{0,384},{128,0},{256,128},{384,256},{1,385},{129,1},{257,129},{385... | collective-permute-start | bytes 110600 | tf_op jit(solution)/shard_map/ppermute | solution.py:381
  39.6 2.3 %collective-permute-start = (bf16[128,896]{1,0:T(8,128)(2,1)S(1)}, bf16[128,896]{1,0:T(8,128)(2,1)S(1)}, u32[]{:S(2)}, u32[]{:S(2)}) collective-permute-start(bf16[128,896]{1,0:T(8,128)(2,1)S(1)} %copy-done), channel_id=1, source_target_pairs={{0,128},{128,256},{256,384},{384,0},{1,129},{129,257},{257,385},{3... | collective-permute-start | bytes 688136 | tf_op jit(solution)/shard_map/ppermute | solution.py:381
  41.9 2.7 %collective-permute-start.1 = (bf16[128,896]{1,0:T(8,128)(2,1)S(1)}, bf16[128,896]{1,0:T(8,128)(2,1)S(1)}, u32[]{:S(2)}, u32[]{:S(2)}) collective-permute-start(bf16[128,896]{1,0:T(8,128)(2,1)S(1)} %copy-done), channel_id=1, source_target_pairs={{0,256},{128,384},{256,0},{384,128},{1,257},{129,385},{257,1},{385... | collective-permute-start | bytes 688136 | tf_op jit(solution)/shard_map/ppermute | solution.py:381
  44.6 3.5 %collective-permute-start.2 = (bf16[128,896]{1,0:T(8,128)(2,1)S(1)}, bf16[128,896]{1,0:T(8,128)(2,1)S(1)}, u32[]{:S(2)}, u32[]{:S(2)}) collective-permute-start(bf16[128,896]{1,0:T(8,128)(2,1)S(1)} %copy-done), channel_id=1, source_target_pairs={{0,384},{128,0},{256,128},{384,256},{1,385},{129,1},{257,129},{385... | collective-permute-start | bytes 688136 | tf_op jit(solution)/shard_map/ppermute | solution.py:381
  48.1 9.0 %shard_map.87.outs_any = bf16[64,144,128]{2,1,0:T(8,128)(2,1)} custom-call(bf16[1280,1024]{1,0:T(8,128)(2,1)} %shard_map.86.hidden_ref, bf16[1024,896]{1,0:T(8,128)(2,1)} %bitcast.32), custom_call_target="tpu_custom_call" | custom-call | flops 2400000000 | bytes 6900000 | tf_op jit(solution)/shard_map/pallas_call | solution.py:165
  57.1 2.9 %copy.11 = bf16[1,1024,896]{1,2,0:T(8,128)(2,1)S(1)} copy(bf16[1,1024,896]{2,1,0:T(8,128)(2,1)} %param.11) | data formatting | bytes 3670016 | tf_op args[5]
  60.7 2.5 %collective-permute-done.2 = bf16[128,896]{1,0:T(8,128)(2,1)S(1)} collective-permute-done((bf16[128,896]{1,0:T(8,128)(2,1)S(1)}, bf16[128,896]{1,0:T(8,128)(2,1)S(1)}, u32[]{:S(2)}, u32[]{:S(2)}) %collective-permute-start.2) | collective-permute-done | bytes 229408 | tf_op jit(solution)/shard_map/ppermute | solution.py:381
  63.9 1.0 pad_maximum_fusion.others_ref
  64.9 13.6 %all-to-all-done.recv_any = bf16[64,144,128]{2,1,0:T(8,128)(2,1)} async-done(((bf16[64,144,128]{2,1,0:T(8,128)(2,1)}), bf16[64,144,128]{2,1,0:T(8,128)(2,1)}, u32[]{:S(2)}, u32[]{:S(2)}) %all-to-all-start) | async-done | bytes 2359328 | tf_op jit(solution)/shard_map/all_to_all | solution.py:384
  78.5 3.4 %shard_map.89 = f32[8,16,128]{2,1,0:T(8,128)} custom-call(bf16[64,144,128]{2,1,0:T(8,128)(2,1)} %all-to-all-done.recv_any, bf16[64,144,128]{2,1,0:T(8,128)(2,1)} %shard_map.87.outs_any), custom_call_target="tpu_custom_call" | custom-call | flops 10000000 | bytes 4800000 | tf_op jit(solution)/shard_map/pallas_call | solution.py:210
  81.9 10.0 %all-to-all-start.1 = ((f32[8,16,128]{2,1,0:T(8,128)}), f32[8,16,128]{2,1,0:T(8,128)S(1)}, u32[]{:S(2)}, u32[]{:S(2)}) async-start(f32[8,16,128]{2,1,0:T(8,128)} %shard_map.89), calls=%async_computation.1 | async-start | bytes 131072 | tf_op jit(solution)/shard_map/all_to_all | solution.py:393
  92.0 5.7 %shard_map.88 = (bf16[1280,1024]{1,0:T(8,128)(2,1)}, bf16[1280,896]{1,0:T(8,128)(2,1)}) custom-call(bf16[64,144,128]{2,1,0:T(8,128)(2,1)} %all-to-all-done.recv_any, bf16[896,1024]{1,0:T(8,128)(2,1)S(1)} %bitcast.28), custom_call_target="tpu_custom_call" | custom-call | flops 2400000000 | bytes 11000000 | tf_op jit(solution)/shard_map/pallas_call | solution.py:294
  97.7 1.4 all-to-all-done.1.slot_ref
  100.0 7.5 %all-to-all-start.2 = ((f32[64,1,128]{2,1,0:T(1,128)}), f32[64,1,128]{2,1,0:T(1,128)S(1)}, u32[]{:S(2)}, u32[]{:S(2)}) async-start(f32[64,1,128]{2,1,0:T(1,128)} %bitcast.13), calls=%async_computation.2 | async-start | bytes 65536 | tf_op jit(solution)/shard_map/all_to_all | solution.py:396
  107.5 6.8 %convert_bitcast_fusion = bf16[1,1024,896]{2,1,0:T(8,128)(2,1)} fusion(bf16[1280,1024]{1,0:T(8,128)(2,1)} %shard_map.86.hidden_ref, bf16[1280,896]{1,0:T(8,128)(2,1)} %get-tuple-element.23), kind=kOutput, calls=%fused_computation | convolution fusion | flops 2349727744 | bytes 6750208 | tf_op jit(solution)/shard_map/dot_general | solution.py:397
  114.3 2.4 %all-to-all-done.2 = f32[64,1,128]{2,1,0:T(1,128)S(1)} async-done(((f32[64,1,128]{2,1,0:T(1,128)}), f32[64,1,128]{2,1,0:T(1,128)S(1)}, u32[]{:S(2)}, u32[]{:S(2)}) %all-to-all-start.2) | async-done | bytes 32800 | tf_op jit(solution)/shard_map/all_to_all | solution.py:396
  116.7 1.2 shard_map.91
  118.0 12.3 %all_to_all.40 = f32[16,1,896]{2,1,0:T(1,128)S(1)} all-to-all(f32[16,1,896]{2,1,0:T(1,128)S(1)} %copy.14), channel_id=1, replica_groups=mesh['x'=4,'y'=8,'node'=2,'dp'=8] {'y','node'}, dimensions={0} | all-to-all | bytes 114688 | tf_op jit(solution)/shard_map/all_to_all | solution.py:401
  130.4 16.6 %all_to_all.41 = f32[64,1,896]{2,1,0:T(1,128)S(1)} all-to-all(f32[64,1,896]{2,1,0:T(1,128)S(1)} %broadcast_in_dim.14), channel_id=1, replica_groups=mesh['x'=4,'y'=8,'node'=2,'dp'=8] {'x','y','node'}, dimensions={0} | all-to-all | bytes 458752 | tf_op jit(solution)/shard_map/all_to_all | solution.py:403
  (24 shorter events, 3.2 us)
Async XLA Ops:
  10.1 68.4 %all-to-all-start = ((bf16[64,144,128]{2,1,0:T(8,128)(2,1)}), bf16[64,144,128]{2,1,0:T(8,128)(2,1)}, u32[]{:S(2)}, u32[]{:S(2)}) async-start(bf16[64,144,128]{2,1,0:T(8,128)(2,1)} %shard_map.85), calls=%async_computation | async-start | bytes 4718592 | tf_op jit(solution)/shard_map/all_to_all | solution.py:384
  21.9 6.7 %copy-start.3 = (s32[128,8]{0,1:T(8,128)S(1)}, s32[128,8]{0,1:T(8,128)}, u32[]{:S(2)}) copy-start(s32[128,8]{0,1:T(8,128)} %param.9) | copy-start | bytes 12292
  21.9 6.7 %copy-start.2 = (f32[128,64]{0,1:T(8,128)S(1)}, f32[128,64]{0,1:T(8,128)}, u32[]{:S(2)}) copy-start(f32[128,64]{0,1:T(8,128)} %param.8) | copy-start | bytes 98308
  21.9 17.6 %copy-start = (bf16[128,896]{1,0:T(8,128)(2,1)S(1)}, bf16[128,896]{1,0:T(8,128)(2,1)}, u32[]{:S(2)}) copy-start(bf16[128,896]{1,0:T(8,128)(2,1)} %tokens_ref.1) | copy-start | bytes 688132
  28.6 16.0 %collective-permute-start.3 = (f32[72,128]{1,0:T(8,128)S(1)}, f32[72,128]{1,0:T(8,128)S(1)}, u32[]{:S(2)}, u32[]{:S(2)}) collective-permute-start(f32[72,128]{1,0:T(8,128)S(1)} %pad_maximum_fusion.2.table_ref), channel_id=1, source_target_pairs={{0,128},{128,256},{256,384},{384,0},{1,129},{129,257},{257,385},{3... | collective-permute-start | bytes 110600 | tf_op jit(solution)/shard_map/ppermute | solution.py:381
  32.0 28.0 %collective-permute-start.4 = (f32[72,128]{1,0:T(8,128)S(1)}, f32[72,128]{1,0:T(8,128)S(1)}, u32[]{:S(2)}, u32[]{:S(2)}) collective-permute-start(f32[72,128]{1,0:T(8,128)S(1)} %pad_maximum_fusion.2.table_ref), channel_id=1, source_target_pairs={{0,256},{128,384},{256,0},{384,128},{1,257},{129,385},{257,1},{385... | collective-permute-start | bytes 110600 | tf_op jit(solution)/shard_map/ppermute | solution.py:381
  36.6 23.5 %collective-permute-start.5 = (f32[72,128]{1,0:T(8,128)S(1)}, f32[72,128]{1,0:T(8,128)S(1)}, u32[]{:S(2)}, u32[]{:S(2)}) collective-permute-start(f32[72,128]{1,0:T(8,128)S(1)} %pad_maximum_fusion.2.table_ref), channel_id=1, source_target_pairs={{0,384},{128,0},{256,128},{384,256},{1,385},{129,1},{257,129},{385... | collective-permute-start | bytes 110600 | tf_op jit(solution)/shard_map/ppermute | solution.py:381
  39.6 20.5 %collective-permute-start = (bf16[128,896]{1,0:T(8,128)(2,1)S(1)}, bf16[128,896]{1,0:T(8,128)(2,1)S(1)}, u32[]{:S(2)}, u32[]{:S(2)}) collective-permute-start(bf16[128,896]{1,0:T(8,128)(2,1)S(1)} %copy-done), channel_id=1, source_target_pairs={{0,128},{128,256},{256,384},{384,0},{1,129},{129,257},{257,385},{3... | collective-permute-start | bytes 688136 | tf_op jit(solution)/shard_map/ppermute | solution.py:381
  41.9 18.8 %collective-permute-start.1 = (bf16[128,896]{1,0:T(8,128)(2,1)S(1)}, bf16[128,896]{1,0:T(8,128)(2,1)S(1)}, u32[]{:S(2)}, u32[]{:S(2)}) collective-permute-start(bf16[128,896]{1,0:T(8,128)(2,1)S(1)} %copy-done), channel_id=1, source_target_pairs={{0,256},{128,384},{256,0},{384,128},{1,257},{129,385},{257,1},{385... | collective-permute-start | bytes 688136 | tf_op jit(solution)/shard_map/ppermute | solution.py:381
  44.6 18.6 %collective-permute-start.2 = (bf16[128,896]{1,0:T(8,128)(2,1)S(1)}, bf16[128,896]{1,0:T(8,128)(2,1)S(1)}, u32[]{:S(2)}, u32[]{:S(2)}) collective-permute-start(bf16[128,896]{1,0:T(8,128)(2,1)S(1)} %copy-done), channel_id=1, source_target_pairs={{0,384},{128,0},{256,128},{384,256},{1,385},{129,1},{257,129},{385... | collective-permute-start | bytes 688136 | tf_op jit(solution)/shard_map/ppermute | solution.py:381
  63.2 0.7 copy-start.1
  81.9 17.1 %all-to-all-start.1 = ((f32[8,16,128]{2,1,0:T(8,128)}), f32[8,16,128]{2,1,0:T(8,128)S(1)}, u32[]{:S(2)}, u32[]{:S(2)}) async-start(f32[8,16,128]{2,1,0:T(8,128)} %shard_map.89), calls=%async_computation.1 | async-start | bytes 131072 | tf_op jit(solution)/shard_map/all_to_all | solution.py:393
  91.9 55.8 %reduce-scatter.2.cloned.1.call-start = ((), (), s32[]{:S(2)}) async-start(), calls=%async_computation.6 | async-start | bytes 2949120 | tf_op jit(solution)/shard_map/reduce_scatter | solution.py:395
  100.0 16.7 %all-to-all-start.2 = ((f32[64,1,128]{2,1,0:T(1,128)}), f32[64,1,128]{2,1,0:T(1,128)S(1)}, u32[]{:S(2)}, u32[]{:S(2)}) async-start(f32[64,1,128]{2,1,0:T(1,128)} %bitcast.13), calls=%async_computation.2 | async-start | bytes 65536 | tf_op jit(solution)/shard_map/all_to_all | solution.py:396
Sparse Core Ops, SparseCore 0:
  99.2 39.1 reduce-scatter.1

commit v9 on v8

--- a/solution.py
+++ b/solution.py
@@ -173,10 +173,14 @@
     )(hidden, down)
 
 
+SLOT_PARTS = 4
+SOURCES = EXP // SLOT_PARTS
+
+
 def slot_kernel(recv_any, outs_any, slot_ref, recv_ref, outs_ref, sems):
     copies = []
-    for c in range(PARTS):
-        at = slice(c * PAIR, (c + 1) * PAIR)
+    for c in range(SLOT_PARTS):
+        at = slice(c * SOURCES, (c + 1) * SOURCES)
         copies.append(
             [
                 pltpu.make_async_copy(recv_any.at[at], recv_ref.at[at], sems.at[0, c]),
@@ -186,8 +190,8 @@
         for copy in copies[c]:
             copy.start()
     ones = jnp.ones((8, LANES), bf16)
-    for c in range(PARTS):
-        at = slice(c * PAIR, (c + 1) * PAIR)
+    for c in range(SLOT_PARTS):
+        at = slice(c * SOURCES, (c + 1) * SOURCES)
         for copy in copies[c]:
             copy.wait()
         tiles = []
@@ -195,14 +199,14 @@
             rows = slice(MAIN * j, MAIN * (j + 1))
             tiles.append(recv_ref[at, rows, :].astype(f32) * outs_ref[at, rows, :].astype(f32))
         for kind, some in enumerate((tiles[:COLS], tiles[COLS:])):
-            rest = sum(some).reshape(PAIR * MAIN, LANES)
-            sums = jnp.zeros((8, PAIR * MAIN), f32)
+            rest = sum(some).reshape(SOURCES * MAIN, LANES)
+            sums = jnp.zeros((8, SOURCES * MAIN), f32)
             for _ in range(3):
                 term = rest.astype(bf16)
                 rest = rest - term.astype(f32)
                 sums = sums + lax.dot_general(ones, term, (((1,), (1,)), ((), ())), preferred_element_type=f32)
-            for h in range(PAIR // 8):
-                slot_ref[:, kind * GROUPS + PAIR // 8 * c + h, :] = sums[:, LANES * h : LANES * (h + 1)]
+            for h in range(SOURCES // 8):
+                slot_ref[:, kind * GROUPS + SOURCES // 8 * c + h, :] = sums[:, LANES * h : LANES * (h + 1)]
 
 
 def slots(recv, outs):
@@ -214,7 +218,7 @@
         scratch_shapes=[
             pltpu.VMEM((EXP, PIECE, LANES), bf16),
             pltpu.VMEM((EXP, PIECE, LANES), bf16),
-            pltpu.SemaphoreType.DMA((2, PARTS)),
+            pltpu.SemaphoreType.DMA((2, SLOT_PARTS)),
         ],
         compiler_params=pltpu.CompilerParams(vmem_limit_bytes=52 * MIB),
         cost_estimate=pl.CostEstimate(flops=10_000_000, bytes_accessed=4_800_000, transcendentals=0),

time: 156 us -> 156 us (level)
  no operation moved by 1% of the time
where the time goes in v9:
time: 156 us; the launch traced here: 154 us
  starting transfers between devices  48.8 us (31%)
  Pallas kernels  29.7 us (19%)
  blocking collectives  28.9 us (19%)
  waiting for transfers between devices  20.5 us (13%)
  between operations  14.2 us (9%)
  matrix products  6.83 us (4%)
  local copies, waits for them, and re-layouts  4.49 us (3%)
    ppermute x6, starting transfers between devices, gather(): lax.ppermute(v, 'x', [(i, (i + k) % ROW) for i in range(ROW)])  19.4 us
    all_to_all x1, blocking collectives, body(): gate_grad = exchange(jnp.broadcast_to(gate_row, (EXP, FEAT)), both)  16.6 us
    all_to_all x1, waiting for transfers between devices, body(): recv = exchange(pack(ids, scores, grad_out), both)  13.6 us
    all_to_all x1, blocking collectives, body(): exchange(gate(x, table, tables, back, tokens, others), ('y', 'node'))  12.3 us
    all_to_all x1, starting transfers between devices, body(): recv = exchange(pack(ids, scores, grad_out), both)  11.8 us
    all_to_all x1, starting transfers between devices, body(): slot = exchange(slot, 'dp')  10 us
    pallas_call x1, Pallas kernels, outputs(): pl.pallas_call(output_kernel, grid=(GROUPS,), in_specs=[pl.BlockSpec((BLO...  9 us
    all_to_all x1, starting transfers between devices, body(): back = exchange(spread(slot), both)  7.5 us
  transfers between devices with their start and end apart: 10, of which 5 were waited for; matrix products, arithmetic and copies ran while one was open for 8% of the time, Pallas kernels for 15%

profile of v9, /device:TPU:1, one launch (start us, length us, event | category | flops | bytes accessed | tf_op | source)
XLA Modules:
  0.0 154.5 jit_solution(7601518109195366815)
XLA Ops:
  7.2 2.9 %shard_map.85 = bf16[64,144,128]{2,1,0:T(8,128)(2,1)} custom-call(s32[8,128]{1,0:T(8,128)} %bitcast.42, f32[64,128]{1,0:T(8,128)} %bitcast.37, bf16[128,896]{1,0:T(8,128)(2,1)} %grad_any.1), custom_call_target="tpu_custom_call" | custom-call | flops 500000000 | bytes 2700000 | tf_op jit(solution)/shard_map/pallas_call | solution.py:99
  10.1 11.8 %all-to-all-start = ((bf16[64,144,128]{2,1,0:T(8,128)(2,1)}), bf16[64,144,128]{2,1,0:T(8,128)(2,1)}, u32[]{:S(2)}, u32[]{:S(2)}) async-start(bf16[64,144,128]{2,1,0:T(8,128)(2,1)} %shard_map.85), calls=%async_computation | async-start | bytes 4718592 | tf_op jit(solution)/shard_map/all_to_all | solution.py:388
  21.9 6.7 %shard_map.86.hidden_ref = bf16[1280,1024]{1,0:T(8,128)(2,1)} custom-call(bf16[1280,1024]{1,0:T(8,128)(2,1)} %bitcast.31), custom_call_target="tpu_custom_call" | custom-call | flops 500000000 | bytes 5300000 | tf_op jit(solution)/shard_map/pallas_call | solution.py:132
  28.6 3.4 %collective-permute-start.3 = (f32[72,128]{1,0:T(8,128)S(1)}, f32[72,128]{1,0:T(8,128)S(1)}, u32[]{:S(2)}, u32[]{:S(2)}) collective-permute-start(f32[72,128]{1,0:T(8,128)S(1)} %pad_maximum_fusion.2.table_ref), channel_id=1, source_target_pairs={{0,128},{128,256},{256,384},{384,0},{1,129},{129,257},{257,385},{3... | collective-permute-start | bytes 110600 | tf_op jit(solution)/shard_map/ppermute | solution.py:385
  32.0 4.5 %collective-permute-start.4 = (f32[72,128]{1,0:T(8,128)S(1)}, f32[72,128]{1,0:T(8,128)S(1)}, u32[]{:S(2)}, u32[]{:S(2)}) collective-permute-start(f32[72,128]{1,0:T(8,128)S(1)} %pad_maximum_fusion.2.table_ref), channel_id=1, source_target_pairs={{0,256},{128,384},{256,0},{384,128},{1,257},{129,385},{257,1},{385... | collective-permute-start | bytes 110600 | tf_op jit(solution)/shard_map/ppermute | solution.py:385
  36.6 3.0 %collective-permute-start.5 = (f32[72,128]{1,0:T(8,128)S(1)}, f32[72,128]{1,0:T(8,128)S(1)}, u32[]{:S(2)}, u32[]{:S(2)}) collective-permute-start(f32[72,128]{1,0:T(8,128)S(1)} %pad_maximum_fusion.2.table_ref), channel_id=1, source_target_pairs={{0,384},{128,0},{256,128},{384,256},{1,385},{129,1},{257,129},{385... | collective-permute-start | bytes 110600 | tf_op jit(solution)/shard_map/ppermute | solution.py:385
  39.6 2.3 %collective-permute-start = (bf16[128,896]{1,0:T(8,128)(2,1)S(1)}, bf16[128,896]{1,0:T(8,128)(2,1)S(1)}, u32[]{:S(2)}, u32[]{:S(2)}) collective-permute-start(bf16[128,896]{1,0:T(8,128)(2,1)S(1)} %copy-done), channel_id=1, source_target_pairs={{0,128},{128,256},{256,384},{384,0},{1,129},{129,257},{257,385},{3... | collective-permute-start | bytes 688136 | tf_op jit(solution)/shard_map/ppermute | solution.py:385
  41.9 2.7 %collective-permute-start.1 = (bf16[128,896]{1,0:T(8,128)(2,1)S(1)}, bf16[128,896]{1,0:T(8,128)(2,1)S(1)}, u32[]{:S(2)}, u32[]{:S(2)}) collective-permute-start(bf16[128,896]{1,0:T(8,128)(2,1)S(1)} %copy-done), channel_id=1, source_target_pairs={{0,256},{128,384},{256,0},{384,128},{1,257},{129,385},{257,1},{385... | collective-permute-start | bytes 688136 | tf_op jit(solution)/shard_map/ppermute | solution.py:385
  44.6 3.5 %collective-permute-start.2 = (bf16[128,896]{1,0:T(8,128)(2,1)S(1)}, bf16[128,896]{1,0:T(8,128)(2,1)S(1)}, u32[]{:S(2)}, u32[]{:S(2)}) collective-permute-start(bf16[128,896]{1,0:T(8,128)(2,1)S(1)} %copy-done), channel_id=1, source_target_pairs={{0,384},{128,0},{256,128},{384,256},{1,385},{129,1},{257,129},{385... | collective-permute-start | bytes 688136 | tf_op jit(solution)/shard_map/ppermute | solution.py:385
  48.1 9.0 %shard_map.87.outs_any = bf16[64,144,128]{2,1,0:T(8,128)(2,1)} custom-call(bf16[1280,1024]{1,0:T(8,128)(2,1)} %shard_map.86.hidden_ref, bf16[1024,896]{1,0:T(8,128)(2,1)} %bitcast.32), custom_call_target="tpu_custom_call" | custom-call | flops 2400000000 | bytes 6900000 | tf_op jit(solution)/shard_map/pallas_call | solution.py:165
  57.1 2.9 %copy.11 = bf16[1,1024,896]{1,2,0:T(8,128)(2,1)S(1)} copy(bf16[1,1024,896]{2,1,0:T(8,128)(2,1)} %param.11) | data formatting | bytes 3670016 | tf_op args[5]
  60.7 2.5 %collective-permute-done.2 = bf16[128,896]{1,0:T(8,128)(2,1)S(1)} collective-permute-done((bf16[128,896]{1,0:T(8,128)(2,1)S(1)}, bf16[128,896]{1,0:T(8,128)(2,1)S(1)}, u32[]{:S(2)}, u32[]{:S(2)}) %collective-permute-start.2) | collective-permute-done | bytes 229408 | tf_op jit(solution)/shard_map/ppermute | solution.py:385
  63.9 1.0 pad_maximum_fusion.others_ref
  64.9 13.6 %all-to-all-done.recv_any = bf16[64,144,128]{2,1,0:T(8,128)(2,1)} async-done(((bf16[64,144,128]{2,1,0:T(8,128)(2,1)}), bf16[64,144,128]{2,1,0:T(8,128)(2,1)}, u32[]{:S(2)}, u32[]{:S(2)}) %all-to-all-start) | async-done | bytes 2359328 | tf_op jit(solution)/shard_map/all_to_all | solution.py:388
  78.5 3.3 %shard_map.89 = f32[8,16,128]{2,1,0:T(8,128)} custom-call(bf16[64,144,128]{2,1,0:T(8,128)(2,1)} %all-to-all-done.recv_any, bf16[64,144,128]{2,1,0:T(8,128)(2,1)} %shard_map.87.outs_any), custom_call_target="tpu_custom_call" | custom-call | flops 10000000 | bytes 4800000 | tf_op jit(solution)/shard_map/pallas_call | solution.py:214
  81.8 10.0 %all-to-all-start.1 = ((f32[8,16,128]{2,1,0:T(8,128)}), f32[8,16,128]{2,1,0:T(8,128)S(1)}, u32[]{:S(2)}, u32[]{:S(2)}) async-start(f32[8,16,128]{2,1,0:T(8,128)} %shard_map.89), calls=%async_computation.1 | async-start | bytes 131072 | tf_op jit(solution)/shard_map/all_to_all | solution.py:397
  91.9 5.7 %shard_map.88 = (bf16[1280,1024]{1,0:T(8,128)(2,1)}, bf16[1280,896]{1,0:T(8,128)(2,1)}) custom-call(bf16[64,144,128]{2,1,0:T(8,128)(2,1)} %all-to-all-done.recv_any, bf16[896,1024]{1,0:T(8,128)(2,1)S(1)} %bitcast.28), custom_call_target="tpu_custom_call" | custom-call | flops 2400000000 | bytes 11000000 | tf_op jit(solution)/shard_map/pallas_call | solution.py:298
  97.6 1.4 all-to-all-done.1.slot_ref
  99.9 7.5 %all-to-all-start.2 = ((f32[64,1,128]{2,1,0:T(1,128)}), f32[64,1,128]{2,1,0:T(1,128)S(1)}, u32[]{:S(2)}, u32[]{:S(2)}) async-start(f32[64,1,128]{2,1,0:T(1,128)} %bitcast.13), calls=%async_computation.2 | async-start | bytes 65536 | tf_op jit(solution)/shard_map/all_to_all | solution.py:400
  107.4 6.8 %convert_bitcast_fusion = bf16[1,1024,896]{2,1,0:T(8,128)(2,1)} fusion(bf16[1280,1024]{1,0:T(8,128)(2,1)} %shard_map.86.hidden_ref, bf16[1280,896]{1,0:T(8,128)(2,1)} %get-tuple-element.23), kind=kOutput, calls=%fused_computation | convolution fusion | flops 2349727744 | bytes 6750208 | tf_op jit(solution)/shard_map/dot_general | solution.py:401
  114.2 2.4 %all-to-all-done.2 = f32[64,1,128]{2,1,0:T(1,128)S(1)} async-done(((f32[64,1,128]{2,1,0:T(1,128)}), f32[64,1,128]{2,1,0:T(1,128)S(1)}, u32[]{:S(2)}, u32[]{:S(2)}) %all-to-all-start.2) | async-done | bytes 32800 | tf_op jit(solution)/shard_map/all_to_all | solution.py:400
  116.6 1.2 shard_map.91
  117.9 12.3 %all_to_all.40 = f32[16,1,896]{2,1,0:T(1,128)S(1)} all-to-all(f32[16,1,896]{2,1,0:T(1,128)S(1)} %copy.14), channel_id=1, replica_groups=mesh['x'=4,'y'=8,'node'=2,'dp'=8] {'y','node'}, dimensions={0} | all-to-all | bytes 114688 | tf_op jit(solution)/shard_map/all_to_all | solution.py:405
  130.3 16.6 %all_to_all.41 = f32[64,1,896]{2,1,0:T(1,128)S(1)} all-to-all(f32[64,1,896]{2,1,0:T(1,128)S(1)} %broadcast_in_dim.14), channel_id=1, replica_groups=mesh['x'=4,'y'=8,'node'=2,'dp'=8] {'x','y','node'}, dimensions={0} | all-to-all | bytes 458752 | tf_op jit(solution)/shard_map/all_to_all | solution.py:407
  (24 shorter events, 3.2 us)
Async XLA Ops:
  10.1 68.4 %all-to-all-start = ((bf16[64,144,128]{2,1,0:T(8,128)(2,1)}), bf16[64,144,128]{2,1,0:T(8,128)(2,1)}, u32[]{:S(2)}, u32[]{:S(2)}) async-start(bf16[64,144,128]{2,1,0:T(8,128)(2,1)} %shard_map.85), calls=%async_computation | async-start | bytes 4718592 | tf_op jit(solution)/shard_map/all_to_all | solution.py:388
  21.9 6.7 %copy-start.3 = (s32[128,8]{0,1:T(8,128)S(1)}, s32[128,8]{0,1:T(8,128)}, u32[]{:S(2)}) copy-start(s32[128,8]{0,1:T(8,128)} %param.9) | copy-start | bytes 12292
  21.9 6.7 %copy-start.2 = (f32[128,64]{0,1:T(8,128)S(1)}, f32[128,64]{0,1:T(8,128)}, u32[]{:S(2)}) copy-start(f32[128,64]{0,1:T(8,128)} %param.8) | copy-start | bytes 98308
  21.9 17.6 %copy-start = (bf16[128,896]{1,0:T(8,128)(2,1)S(1)}, bf16[128,896]{1,0:T(8,128)(2,1)}, u32[]{:S(2)}) copy-start(bf16[128,896]{1,0:T(8,128)(2,1)} %tokens_ref.1) | copy-start | bytes 688132
  28.6 16.0 %collective-permute-start.3 = (f32[72,128]{1,0:T(8,128)S(1)}, f32[72,128]{1,0:T(8,128)S(1)}, u32[]{:S(2)}, u32[]{:S(2)}) collective-permute-start(f32[72,128]{1,0:T(8,128)S(1)} %pad_maximum_fusion.2.table_ref), channel_id=1, source_target_pairs={{0,128},{128,256},{256,384},{384,0},{1,129},{129,257},{257,385},{3... | collective-permute-start | bytes 110600 | tf_op jit(solution)/shard_map/ppermute | solution.py:385
  32.0 28.0 %collective-permute-start.4 = (f32[72,128]{1,0:T(8,128)S(1)}, f32[72,128]{1,0:T(8,128)S(1)}, u32[]{:S(2)}, u32[]{:S(2)}) collective-permute-start(f32[72,128]{1,0:T(8,128)S(1)} %pad_maximum_fusion.2.table_ref), channel_id=1, source_target_pairs={{0,256},{128,384},{256,0},{384,128},{1,257},{129,385},{257,1},{385... | collective-permute-start | bytes 110600 | tf_op jit(solution)/shard_map/ppermute | solution.py:385
  36.6 23.5 %collective-permute-start.5 = (f32[72,128]{1,0:T(8,128)S(1)}, f32[72,128]{1,0:T(8,128)S(1)}, u32[]{:S(2)}, u32[]{:S(2)}) collective-permute-start(f32[72,128]{1,0:T(8,128)S(1)} %pad_maximum_fusion.2.table_ref), channel_id=1, source_target_pairs={{0,384},{128,0},{256,128},{384,256},{1,385},{129,1},{257,129},{385... | collective-permute-start | bytes 110600 | tf_op jit(solution)/shard_map/ppermute | solution.py:385
  39.6 20.5 %collective-permute-start = (bf16[128,896]{1,0:T(8,128)(2,1)S(1)}, bf16[128,896]{1,0:T(8,128)(2,1)S(1)}, u32[]{:S(2)}, u32[]{:S(2)}) collective-permute-start(bf16[128,896]{1,0:T(8,128)(2,1)S(1)} %copy-done), channel_id=1, source_target_pairs={{0,128},{128,256},{256,384},{384,0},{1,129},{129,257},{257,385},{3... | collective-permute-start | bytes 688136 | tf_op jit(solution)/shard_map/ppermute | solution.py:385
  41.9 18.8 %collective-permute-start.1 = (bf16[128,896]{1,0:T(8,128)(2,1)S(1)}, bf16[128,896]{1,0:T(8,128)(2,1)S(1)}, u32[]{:S(2)}, u32[]{:S(2)}) collective-permute-start(bf16[128,896]{1,0:T(8,128)(2,1)S(1)} %copy-done), channel_id=1, source_target_pairs={{0,256},{128,384},{256,0},{384,128},{1,257},{129,385},{257,1},{385... | collective-permute-start | bytes 688136 | tf_op jit(solution)/shard_map/ppermute | solution.py:385
  44.6 18.6 %collective-permute-start.2 = (bf16[128,896]{1,0:T(8,128)(2,1)S(1)}, bf16[128,896]{1,0:T(8,128)(2,1)S(1)}, u32[]{:S(2)}, u32[]{:S(2)}) collective-permute-start(bf16[128,896]{1,0:T(8,128)(2,1)S(1)} %copy-done), channel_id=1, source_target_pairs={{0,384},{128,0},{256,128},{384,256},{1,385},{129,1},{257,129},{385... | collective-permute-start | bytes 688136 | tf_op jit(solution)/shard_map/ppermute | solution.py:385
  63.2 0.7 copy-start.1
  81.8 17.1 %all-to-all-start.1 = ((f32[8,16,128]{2,1,0:T(8,128)}), f32[8,16,128]{2,1,0:T(8,128)S(1)}, u32[]{:S(2)}, u32[]{:S(2)}) async-start(f32[8,16,128]{2,1,0:T(8,128)} %shard_map.89), calls=%async_computation.1 | async-start | bytes 131072 | tf_op jit(solution)/shard_map/all_to_all | solution.py:397
  91.8 55.8 %reduce-scatter.2.cloned.1.call-start = ((), (), s32[]{:S(2)}) async-start(), calls=%async_computation.6 | async-start | bytes 2949120 | tf_op jit(solution)/shard_map/reduce_scatter | solution.py:399
  99.9 16.7 %all-to-all-start.2 = ((f32[64,1,128]{2,1,0:T(1,128)}), f32[64,1,128]{2,1,0:T(1,128)S(1)}, u32[]{:S(2)}, u32[]{:S(2)}) async-start(f32[64,1,128]{2,1,0:T(1,128)} %bitcast.13), calls=%async_computation.2 | async-start | bytes 65536 | tf_op jit(solution)/shard_map/all_to_all | solution.py:400
Sparse Core Ops, SparseCore 0:
  99.1 39.0 reduce-scatter.1
